TPU v7x, 512 devices: a whole 4x4x16 slice. The times are simulated.
512 devices in a mesh: dp: 32 (over y_lo, z), ctx: 16 (over x, y_hi, core).
Axes of the slice: x: 4, y: 4 (y_hi: 2, y_lo: 2; y = y_hi * 2 + y_lo), z: 16, core: 2. Of those that a mesh axis runs over, the one named last changes fastest.
Arguments:
- hidden_in: bfloat16 [32, 2048, 8192], P('dp', 'ctx'), may hold values from -6 to 6
- query: bfloat16 [32, 2048, 1024], P('dp', 'ctx'), may hold values from -88 to 88
- key_value: bfloat16 [32, 2048, 256], P('dp', 'ctx'), may hold values from -4 to 4
- grad_out: bfloat16 [32, 2048, 1024], P('dp', 'ctx'), may hold values from -6 to 6
- lengths: int32 [32, 8], P('dp'), may hold values from 1 to 1792, 2048 in all within a row
- owner: int32 [64, 1], replicated, may hold values from 0 to 31; in each aligned block of 64 rows (0 to 63, 64 to 127, ...) at most 4 rows name the same one
Outputs:
- grad_query: bfloat16 [32, 2048, 1024], P('dp', 'ctx')
- grad_kv: bfloat16 [32, 2048, 256], P('dp', 'ctx')
- factors: float32 [32, 4, 2, 128, 128], P('dp')
Inputs may be any that keep to these rules, and one draw needn't show every extreme that they name: `lengths`: each row sums to 2048; its longest document has exactly 1792 positions. No owner holds more than 4 tiles, one holds exactly 4, and every owner holds one or more.
All inputs are finite; a program needn't handle non-finite values.
Results may differ from a plain program's by a relative error of at most 0.017.
Values may be sent and summed in bfloat16 or wider, within the bound.
No kernel may reach another device: no remote copies, remote signals or barrier semaphores. Data moves between devices by JAX's collectives and lax.ppermute only.
A program may use at most 64 MiB of HBM per device.

v0:
```python
import math

import jax
import jax.numpy as jnp
from jax import lax
from jax.sharding import PartitionSpec as P

TILE = 128


masked_value = -1e30


def doc_of(positions, doc_ends):
    return jnp.sum((positions[:, None] >= doc_ends[None, :]).astype(jnp.int32), axis=1)


def owner_slots(owner_col, owner_count, slot_count):
    tile_count = owner_col.shape[0]
    tile_order = jnp.arange(tile_count, dtype=jnp.int32)
    same_owner = owner_col[:, None] == owner_col[None, :]
    owner_rank = jnp.sum(
        (same_owner & (tile_order[None, :] < tile_order[:, None])).astype(jnp.int32), axis=1
    )
    owner_ids = jnp.arange(owner_count, dtype=jnp.int32)
    slot_ids = jnp.arange(slot_count, dtype=jnp.int32)
    slot_table = (owner_col[None, None, :] == owner_ids[:, None, None]) & (
        owner_rank[None, None, :] == slot_ids[None, :, None]
    )
    return slot_table.astype(jnp.float32)


def as_tiles(matrix, tile_rows, tile_cols):
    return (
        matrix.reshape(tile_rows, TILE, tile_cols, TILE)
        .transpose(0, 2, 1, 3)
        .reshape(tile_rows * tile_cols, TILE, TILE)
    )


def body(hidden_in, query, key_value, grad_out, lengths, owner):
    tok_rows = query.shape[1]
    head_dim = key_value.shape[2] // 2
    head_count = query.shape[2] // head_dim
    model_width = hidden_in.shape[2]
    ctx_count = lax.axis_size("ctx")
    dp_count = lax.axis_size("dp")
    seq_len = tok_rows * ctx_count
    key_block = min(512, seq_len)
    blocks = seq_len // key_block
    score_scale = 1.0 / math.sqrt(head_dim)
    doc_ends = jnp.cumsum(lengths[0])
    first_pos = lax.axis_index("ctx") * tok_rows
    query_pos = first_pos + jnp.arange(tok_rows, dtype=jnp.int32)
    query_doc = doc_of(query_pos, doc_ends)
    queries = query[0].reshape(tok_rows, head_count, head_dim)
    out_grads = grad_out[0].reshape(tok_rows, head_count, head_dim)
    gathered = lax.all_gather(key_value[0], "ctx", axis=0, tiled=True)
    block_rows = gathered.reshape(blocks, key_block, 2 * head_dim)
    block_ids = jnp.arange(blocks, dtype=jnp.int32)

    def scores_of(block_index):
        rows_here = lax.dynamic_index_in_dim(block_rows, block_index, 0, keepdims=False)
        key_rows = rows_here[:, :head_dim]
        value_rows = rows_here[:, head_dim:]
        key_pos = block_index * key_block + jnp.arange(key_block, dtype=jnp.int32)
        visible = (query_doc[:, None] == doc_of(key_pos, doc_ends)[None, :]) & (
            key_pos[None, :] <= query_pos[:, None]
        )
        visible = visible[:, None, :]
        raw_scores = (
            jnp.einsum("thd,kd->thk", queries, key_rows, preferred_element_type=jnp.float32)
            * score_scale
        )
        return (jnp.where(visible, raw_scores, masked_value), visible, key_rows, value_rows)

    def stat_step(carried, block_index):
        row_top, row_total = carried
        masked, visible, key_rows, value_rows = scores_of(block_index)
        new_top = jnp.maximum(row_top, jnp.max(masked, axis=2))
        weights = jnp.where(visible, jnp.exp(masked - new_top[..., None]), 0.0)
        return ((new_top, row_total * jnp.exp(row_top - new_top) + jnp.sum(weights, axis=2)), None)

    start_stats = (
        jnp.full((tok_rows, head_count), masked_value, jnp.float32),
        jnp.zeros((tok_rows, head_count), jnp.float32),
    )
    (row_top, row_total), _ = lax.scan(stat_step, start_stats, block_ids)

    def probs_of(masked, visible):
        return jnp.where(visible, jnp.exp(masked - row_top[..., None]), 0.0) / row_total[..., None]

    def out_step(output_sum, block_index):
        masked, visible, key_rows, value_rows = scores_of(block_index)
        low_weights = probs_of(masked, visible).astype(jnp.bfloat16)
        return (
            output_sum
            + jnp.einsum(
                "thk,kd->thd", low_weights, value_rows, preferred_element_type=jnp.float32
            ),
            None,
        )

    output_sum, _ = lax.scan(
        out_step, jnp.zeros((tok_rows, head_count, head_dim), jnp.float32), block_ids
    )
    row_delta = jnp.sum(out_grads.astype(jnp.float32) * output_sum, axis=2)

    def back_step(query_grad, block_index):
        back_query_grad = query_grad
        masked, visible, key_rows, value_rows = scores_of(block_index)
        weights = probs_of(masked, visible)
        low_weights = weights.astype(jnp.bfloat16)
        prob_grad = jnp.einsum(
            "thd,kd->thk", out_grads, value_rows, preferred_element_type=jnp.float32
        )
        score_grad = (weights * (prob_grad - row_delta[..., None])).astype(jnp.bfloat16)
        back_query_grad = back_query_grad + jnp.einsum(
            "thk,kd->thd", score_grad, key_rows, preferred_element_type=jnp.float32
        )
        key_grad = (
            jnp.einsum("thk,thd->kd", score_grad, queries, preferred_element_type=jnp.float32)
            * score_scale
        )
        value_grad = jnp.einsum(
            "thk,thd->kd", low_weights, out_grads, preferred_element_type=jnp.float32
        )
        return (back_query_grad, jnp.concatenate([key_grad, value_grad], axis=1))

    query_grad, partial_blocks = lax.scan(
        back_step, jnp.zeros((tok_rows, head_count, head_dim), jnp.float32), block_ids
    )
    partial_value = partial_blocks.reshape(seq_len, 2 * head_dim)
    kv_total = lax.psum_scatter(partial_value, "ctx", scatter_dimension=0, tiled=True)
    kv_low = kv_total.astype(jnp.bfloat16)
    grad_query = (
        (query_grad * score_scale).astype(jnp.bfloat16).reshape(1, tok_rows, head_count * head_dim)
    )
    weight_grad = lax.dot_general(
        hidden_in[0],
        kv_low[:, :head_dim],
        (((0,), (0,)), ((), ())),
        preferred_element_type=jnp.float32,
    )
    tile_rows = model_width // TILE
    tile_cols = head_dim // TILE
    tile_count = tile_rows * tile_cols
    slot_count = max(2, 2 * tile_count // dp_count)
    slot_table = owner_slots(owner[:, 0], dp_count, slot_count)
    pieces = as_tiles(weight_grad, tile_rows, tile_cols)
    outgoing = jnp.einsum("ost,tab->osab", slot_table, pieces, precision=lax.Precision.HIGHEST)
    incoming = lax.all_to_all(outgoing, "dp", split_axis=0, concat_axis=0, tiled=True)
    owned = lax.psum(jnp.sum(incoming, axis=0), "ctx")
    gradient = owned * (1.0 / math.sqrt(dp_count * seq_len))
    left_factor = (
        jnp.einsum("sab,scb->sac", gradient, gradient, precision=lax.Precision.HIGHEST) / TILE
    )
    right_factor = (
        jnp.einsum("sab,sac->sbc", gradient, gradient, precision=lax.Precision.HIGHEST) / TILE
    )
    factors = jnp.stack([left_factor, right_factor], axis=1)[None]
    return (grad_query, kv_low[None], factors)


def solution(mesh):
    return jax.shard_map(
        body,
        mesh=mesh,
        in_specs=(
            P("dp", "ctx", None),
            P("dp", "ctx", None),
            P("dp", "ctx", None),
            P("dp", "ctx", None),
            P("dp", None),
            P(),
        ),
        out_specs=(P("dp", "ctx", None), P("dp", "ctx", None), P("dp", None, None, None, None)),
        check_vma=False,
    )
```

profile of v0, /device:TPU:1, one launch (start us, length us, event | category | flops | bytes accessed | tf_op | source)
XLA Modules:
  0.0 820.8 jit_solution(11045027284102490409)
XLA Ops:
  8.8 1.8 copy.46
  13.0 64.4 %all-gather.3.cloned.1.call-done = bf16[1,2048,256]{2,1,0:T(8,128)(2,1)} async-done(((bf16[1,128,256]{2,1,0:T(8,128)(2,1)}), bf16[1,2048,256]{2,1,0:T(8,128)(2,1)}) %all-gather.3.cloned.1.call-update) | async-done | bytes 1048592 | tf_op jit(solution)/shard_map/all_gather | solution.py:58
  77.4 20.9 %while.37 = (s32[]{:T(128)}, f32[128,8]{0,1:T(8,128)S(1)}, f32[128,8]{0,1:T(8,128)S(1)}, s32[128]{0:T(128)S(1)}, s32[4]{0:T(128)S(1)}, /*index=5*/s32[8]{0:T(128...) while((s32[]{:T(128)}, f32[128,8]{0,1:T(8,128)S(1)}, ...), condition=%wide.region_6.7_spmd.clone, body=%wide.region_2.6_spmd.clone.sunk | while | flops 138626176 | bytes 5373686 | solution.py:88
  98.4 23.6 %while.38 = (s32[]{:T(128)}, f32[128,8,128]{2,0,1:T(8,128)S(1)}, s32[128]{0:T(128)S(1)}, s32[4]{0:T(128)S(1)}, s32[8]{0:T(128)S(1)}, /*index=5*/bf16[4,512,256]{...) while((s32[]{:T(128)}, f32[128,8,128]{2,0,1:T(8,128)S(1)}, ...), condition=%wide.region_9.10_spmd.clone, body=%wide.region_7.9_spmd.clone.sunk | while | flops 272052352 | bytes 2248445 | solution.py:104
  122.3 46.1 %while.39 = (s32[]{:T(128)}, f32[128,8,128]{2,0,1:T(8,128)}, f32[4,512,256]{2,1,0:T(8,128)}, s32[128]{0:T(128)S(1)}, s32[4]{0:T(128)S(1)}, /*index=5*/s32[8]{0:T...) while((s32[]{:T(128)}, f32[128,8,128]{2,0,1:T(8,128)}, ...), condition=%wide.region_13.14_spmd.clone, body=%wide.region_11.13_spmd.clone.sunk | while | flops 676475008 | bytes 16277273 | solution.py:130
  126.7 1.6 fusion.84
  137.4 1.6 fusion.84
  140.0 2.3 convolution_add_fusion.2
  142.3 1.4 fusion.86
  149.2 1.6 fusion.84
  151.8 2.3 convolution_add_fusion.2
  154.1 1.4 fusion.86
  161.0 1.6 fusion.84
  163.5 2.3 convolution_add_fusion.2
  169.3 89.9 %reduce-scatter.2.cloned.1.call-done = f32[128,256]{1,0:T(8,128)} async-done(((f32[2048,256]{1,0:T(8,128)}), f32[128,256]{1,0:T(8,128)}) %reduce-scatter.2.cloned.1.call-update) | async-done | bytes 131088 | tf_op jit(solution)/shard_map/reduce_scatter | solution.py:134
  260.9 2.7 copy.69
  263.5 5.5 copy.53
  269.0 5.3 fusion.32
  274.3 4.9 copy.54
  279.2 376.3 %all_to_all.5 = f32[32,4,128,128]{3,2,1,0:T(8,128)} all-to-all(f32[32,4,128,128]{3,2,1,0:T(8,128)S(1)} %copy.54), channel_id=1, replica_groups=mesh['dp'=32,'ctx'=16] {'dp'}, dimensions={0} | all-to-all | bytes 16777216 | tf_op jit(solution)/shard_map/all_to_all | solution.py:152
  655.5 4.5 reduce_sum.75
  662.8 147.2 %all-reduce.2.cloned.1.call-done = f32[4,128,128]{2,1,0:T(8,128)} async-done(((f32[4,128,128]{2,1,0:T(8,128)}), f32[4,128,128]{2,1,0:T(8,128)}) %all-reduce.2.cloned.1.call-update) | async-done | bytes 262160 | tf_op jit(solution)/shard_map/psum | solution.py:153
  810.0 1.6 fusion.35
  811.7 1.7 fusion.36
  (157 shorter events, 53.6 us)
Async XLA Ops:
  7.2 253.0 %copy-start = (bf16[1,128,8192]{2,1,0:T(8,128)(2,1)S(1)}, bf16[1,128,8192]{2,1,0:T(8,128)(2,1)}, u32[]{:S(2)}) copy-start(bf16[1,128,8192]{2,1,0:T(8,128)(2,1)} %param.12) | copy-start | bytes 6291460
  7.2 70.2 %all-gather.3.cloned.1.call-start = ((), (), s32[]{:S(2)}) async-start(), calls=%async_computation.4 | async-start | bytes 1114112 | tf_op jit(solution)/shard_map/all_gather | solution.py:58
  7.9 251.3 %reduce-scatter.2.cloned.1.call-start = ((), (), s32[]{:S(2)}) async-start(), calls=%async_computation.2 | async-start | bytes 2228224 | tf_op jit(solution)/shard_map/reduce_scatter | solution.py:134
  168.4 0.7 copy-start.2
  168.4 641.6 %all-reduce.2.cloned.1.call-start = ((), (), s32[]{:S(2)}) async-start(), calls=%async_computation.3 | async-start | bytes 524288 | tf_op jit(solution)/shard_map/psum | solution.py:153
  660.0 2.2 copy-start.1
Sparse Core Ops, SparseCore 0:
  11.3 66.0 all-gather.2
  168.5 90.6 reduce-scatter.1
  660.1 149.8 all-reduce.1
where the time goes:
time: 822 us; the launch traced here: 821 us
  blocking collectives  376 us (46%)
  waiting for transfers between devices  302 us (37%)
  local copies, waits for them, and re-layouts  42.7 us (5%)
  matrix products  39.9 us (5%)
  loops' own time  31 us (4%)
  other arithmetic  14.3 us (2%)
  between operations  13.9 us (2%)
    all_to_all x1, blocking collectives, body(): lax.all_to_all(outgoing, 'dp', split_axis=0, concat_axis=0, tiled=True)  376 us
    psum x1, waiting for transfers between devices, body(): owned = lax.psum(jnp.sum(incoming, axis=0), 'ctx')  147 us
    reduce_scatter x1, waiting for transfers between devices, body(): lax.psum_scatter(partial_value, 'ctx', scatter_dimension=0, tiled=True)  89.9 us
    all_gather x1, waiting for transfers between devices, body(): gathered = lax.all_gather(key_value[0], 'ctx', axis=0, tiled=True)  64.4 us
  transfers between devices with their start and end apart: 3, of which 3 were waited for; matrix products, arithmetic and copies ran while one was open for 1% of the time, Pallas kernels for 0%

commit v1 on v0

v1 whole, which is shorter than its diff:
```python
import math

import jax
import jax.numpy as jnp
from jax import lax
from jax.experimental import pallas as pl
from jax.experimental.pallas import tpu as pltpu
from jax.sharding import Mesh
from jax.sharding import PartitionSpec as P

HEADS = 8
HD = 128
TILE = 128
ROWS = 128
CHIPS = 8
SEQ = 2048
TILES = 64
CAP = 4
N_DP = 32
MODEL = 8192
PAIR = 2 * ROWS
HIDDEN_NEG = -1e30
SCALE = 1.0 / math.sqrt(HD)
EXP2_SCALE = SCALE * math.log2(math.e)
F32 = jnp.float32
BF16 = jnp.bfloat16


def attention_kernel(
    lengths_ref, q_ref, go_ref, mine_ref, other_ref,
    dq_ref, dmine_ref, dother_ref,
    q_t, go_t, q_rows, go_rows, scores, prob_grads, ds_buf, w_buf, top, total, delta, dq_t,
):
    chip = lax.axis_index("chip")
    core = lax.axis_index("core")
    first = (2 * chip + core) * ROWS
    for h in range(HEADS):
        cols = pl.ds(h * HD, HD)
        qh = q_ref[:, cols]
        gh = go_ref[:, cols]
        q_t[:, cols] = qh.T
        go_t[:, cols] = gh.T
        q_rows[cols, :] = qh
        go_rows[cols, :] = gh
    row_pos = first + lax.broadcasted_iota(jnp.int32, (1, ROWS), 1)
    row_low = jnp.zeros((1, ROWS), jnp.int32)
    first_low = jnp.int32(0)
    end = jnp.int32(0)
    for d in range(lengths_ref.shape[1]):
        end = end + lengths_ref[0, d]
        row_low = jnp.maximum(row_low, jnp.where(row_pos >= end, end, 0))
        first_low = jnp.maximum(first_low, jnp.where(first >= end, end, 0))
    low_block = first_low // PAIR
    high_block = chip + 1
    top[...] = jnp.full(top.shape, HIDDEN_NEG, F32)
    total[...] = jnp.zeros(total.shape, F32)
    delta[...] = jnp.zeros(delta.shape, F32)
    dq_t[...] = jnp.zeros(dq_t.shape, F32)
    dmine_ref[...] = jnp.zeros(dmine_ref.shape, dmine_ref.dtype)
    dother_ref[...] = jnp.zeros(dother_ref.shape, dother_ref.dtype)

    def rows_of(j):
        return pl.ds(pl.multiple_of(j * PAIR, PAIR), PAIR)

    def sides(j):
        return ((mine_ref, core, 0), (other_ref, 1 - core, ROWS))

    def score_step(j, carry):
        base = pl.multiple_of(j * PAIR, PAIR)
        for ref, side, offset in sides(j):
            pos = (2 * j + side) * ROWS + lax.broadcasted_iota(jnp.int32, (ROWS, ROWS), 0)
            seen = (pos >= row_low) & (pos <= row_pos)
            keys = ref[j, :, :HD]
            for h in range(HEADS):
                cols = pl.ds(h * HD, HD)
                s = jnp.dot(keys, q_t[:, cols], preferred_element_type=F32)
                s = jnp.where(seen, s, HIDDEN_NEG)
                scores[pl.ds(base + offset, ROWS), cols] = s
                best = jnp.max(s.reshape(ROWS // 8, 8, ROWS), axis=0)
                top[:, cols] = jnp.maximum(top[:, cols], best)
        return carry

    lax.fori_loop(low_block, high_block, score_step, 0)
    top[0:1, :] = jnp.max(top[...], axis=0, keepdims=True)

    def weight_step(j, carry):
        base = pl.multiple_of(j * PAIR, PAIR)
        for ref, side, offset in sides(j):
            values = ref[j, :, HD:]
            for h in range(HEADS):
                cols = pl.ds(h * HD, HD)
                rows = pl.ds(base + offset, ROWS)
                p = jnp.exp2((scores[rows, cols] - top[0:1, cols]) * EXP2_SCALE)
                pg = jnp.dot(values, go_t[:, cols], preferred_element_type=F32)
                scores[rows, cols] = p
                prob_grads[rows, cols] = pg
                total[:, cols] += jnp.sum(p.reshape(ROWS // 8, 8, ROWS), axis=0)
                delta[:, cols] += jnp.sum((p * pg).reshape(ROWS // 8, 8, ROWS), axis=0)
        return carry

    lax.fori_loop(low_block, high_block, weight_step, 0)
    inverse = 1.0 / jnp.sum(total[...], axis=0, keepdims=True)
    total[0:1, :] = inverse
    delta[0:1, :] = jnp.sum(delta[...], axis=0, keepdims=True) * inverse

    def back_step(j, carry):
        base = pl.multiple_of(j * PAIR, PAIR)
        for h in range(HEADS):
            cols = pl.ds(h * HD, HD)
            rows = pl.ds(base, PAIR)
            w = scores[rows, cols] * total[0:1, cols]
            w_buf[:, cols] = w.astype(BF16)
            ds_buf[:, cols] = (w * (prob_grads[rows, cols] - delta[0:1, cols])).astype(BF16)
        ds = ds_buf[...]
        dk = jnp.dot(ds, q_rows[...], preferred_element_type=F32) * SCALE
        dv = jnp.dot(w_buf[...], go_rows[...], preferred_element_type=F32)
        dmine_ref[j, :, :HD] = dk[:ROWS]
        dmine_ref[j, :, HD:] = dv[:ROWS]
        dother_ref[j, :, :HD] = dk[ROWS:].astype(BF16)
        dother_ref[j, :, HD:] = dv[ROWS:].astype(BF16)
        keys = jnp.concatenate([mine_ref[j, :, :HD], other_ref[j, :, :HD]], axis=0)
        dq_t[...] += lax.dot_general(
            keys, ds, (((0,), (0,)), ((), ())), preferred_element_type=F32
        )
        return carry

    lax.fori_loop(low_block, high_block, back_step, 0)
    for h in range(HEADS):
        cols = pl.ds(h * HD, HD)
        dq_ref[:, cols] = (dq_t[:, cols].T * SCALE).astype(BF16)


def attention(lengths, query, grad_out, mine, other):
    vmem = pl.BlockSpec(memory_space=pltpu.VMEM)
    wide = HEADS * HD
    return pl.pallas_call(
        attention_kernel,
        out_shape=(
            jax.ShapeDtypeStruct((ROWS, wide), BF16),
            jax.ShapeDtypeStruct((CHIPS, ROWS, 2 * HD), F32),
            jax.ShapeDtypeStruct((CHIPS, ROWS, 2 * HD), BF16),
        ),
        in_specs=[pl.BlockSpec(memory_space=pltpu.SMEM), vmem, vmem, vmem, vmem],
        out_specs=(vmem, vmem, vmem),
        scratch_shapes=[
            pltpu.VMEM((HD, wide), BF16),
            pltpu.VMEM((HD, wide), BF16),
            pltpu.VMEM((wide, HD), BF16),
            pltpu.VMEM((wide, HD), BF16),
            pltpu.VMEM((SEQ, wide), F32),
            pltpu.VMEM((SEQ, wide), F32),
            pltpu.VMEM((PAIR, wide), BF16),
            pltpu.VMEM((PAIR, wide), BF16),
            pltpu.VMEM((8, wide), F32),
            pltpu.VMEM((8, wide), F32),
            pltpu.VMEM((8, wide), F32),
            pltpu.VMEM((HD, wide), F32),
        ],
        compiler_params=pltpu.CompilerParams(vmem_limit_bytes=44 * 1024 * 1024),
        name="attention_backward",
    )(lengths, query, grad_out, mine, other)


STEP_TILES = 8


def weight_kernel(parts_ref, hidden_ref, kv_ref, mine_ref, other_ref, k_t):
    core = lax.axis_index("core")

    @pl.when(pl.program_id(0) == 0)
    def _():
        low = jnp.sum(parts_ref[...].astype(F32), axis=0).astype(BF16)
        kv_ref[...] = low
        k_t[...] = low[:, :HD].T

    grad_t = jnp.dot(k_t[...], hidden_ref[...], preferred_element_type=F32)
    for pair in range(STEP_TILES // 2):
        even = grad_t[:, (2 * pair) * TILE : (2 * pair + 1) * TILE].reshape(CHIPS, 2, 8, TILE)
        odd = grad_t[:, (2 * pair + 1) * TILE : (2 * pair + 2) * TILE].reshape(CHIPS, 2, 8, TILE)
        both = [jnp.concatenate([even[:, c], odd[:, c]], axis=1) for c in range(2)]
        rows = pl.ds(pair * 16, 16)
        here = jnp.where(core == 0, both[0], both[1])
        there = jnp.where(core == 0, both[1], both[0])
        mine_ref[:, rows, :] = here
        other_ref[:, rows, :] = there.astype(BF16)


def weight_terms(parts, hidden):
    steps = TILES // STEP_TILES
    rows = STEP_TILES * 8
    return pl.pallas_call(
        weight_kernel,
        grid=(steps,),
        out_shape=(
            jax.ShapeDtypeStruct((ROWS, 2 * HD), BF16),
            jax.ShapeDtypeStruct((CHIPS, TILES * 8, TILE), F32),
            jax.ShapeDtypeStruct((CHIPS, TILES * 8, TILE), BF16),
        ),
        in_specs=[
            pl.BlockSpec((CHIPS, ROWS, 2 * HD), lambda i: (0, 0, 0)),
            pl.BlockSpec((ROWS, STEP_TILES * TILE), lambda i: (0, i)),
        ],
        out_specs=(
            pl.BlockSpec((ROWS, 2 * HD), lambda i: (0, 0)),
            pl.BlockSpec((CHIPS, rows, TILE), lambda i: (0, i, 0)),
            pl.BlockSpec((CHIPS, rows, TILE), lambda i: (0, i, 0)),
        ),
        scratch_shapes=[pltpu.VMEM((HD, ROWS), BF16)],
        compiler_params=pltpu.CompilerParams(vmem_limit_bytes=32 * 1024 * 1024),
        name="weight_gradient",
    )(parts, hidden)


def owner_kernel(owner_ref, parts_ref, out_ref, sums, placed, held):
    sums[...] = jnp.sum(parts_ref[...].astype(F32), axis=0)
    placed[...] = jnp.zeros(placed.shape, F32)
    for o in range(N_DP):
        held[o] = 0

    def place(t, carry):
        o = owner_ref[t, 0]
        slot = held[o]
        held[o] = slot + 1
        to = pl.multiple_of((o * CAP + slot) * 8, 8)
        placed[pl.ds(to, 8), :] = sums[pl.ds(pl.multiple_of(t * 8, 8), 8), :]
        return carry

    lax.fori_loop(0, TILES, place, 0)
    out_ref[...] = placed[...].astype(BF16).reshape(out_ref.shape)


def to_owners(owner, parts):
    vmem = pl.BlockSpec(memory_space=pltpu.VMEM)
    return pl.pallas_call(
        owner_kernel,
        out_shape=jax.ShapeDtypeStruct((N_DP, CAP * 8, TILE), BF16),
        in_specs=[pl.BlockSpec(memory_space=pltpu.SMEM), vmem],
        out_specs=vmem,
        scratch_shapes=[
            pltpu.VMEM((TILES * 8, TILE), F32),
            pltpu.VMEM((N_DP * CAP * 8, TILE), F32),
            pltpu.SMEM((N_DP,), jnp.int32),
        ],
        compiler_params=pltpu.CompilerParams(vmem_limit_bytes=32 * 1024 * 1024),
        name="owner_slots",
    )(owner, parts)


def sum_kernel(parts_ref, out_ref):
    gradient = jnp.sum(parts_ref[...].astype(F32), axis=0) * (1.0 / math.sqrt(N_DP * SEQ))
    out_ref[...] = jnp.broadcast_to(gradient.astype(BF16)[None], out_ref.shape)


def owned_sum(parts):
    vmem = pl.BlockSpec(memory_space=pltpu.VMEM)
    return pl.pallas_call(
        sum_kernel,
        out_shape=jax.ShapeDtypeStruct((2 * CHIPS, CAP * 8, TILE), BF16),
        in_specs=[vmem],
        out_specs=vmem,
        name="owned_sum",
    )(parts)


def factor_kernel(pieces_ref, out_ref):
    pieces = pieces_ref[...].astype(F32)
    for s in range(CAP):
        grad_t = pieces[:, s * 8 : (s + 1) * 8, :].reshape(TILE, TILE)
        low = grad_t.astype(BF16)
        low_t = grad_t.T.astype(BF16)
        out_ref[s, 0] = jnp.dot(low_t, low, preferred_element_type=F32) * (1.0 / TILE)
        out_ref[s, 1] = jnp.dot(low, low_t, preferred_element_type=F32) * (1.0 / TILE)


def factors_of(pieces):
    vmem = pl.BlockSpec(memory_space=pltpu.VMEM)
    return pl.pallas_call(
        factor_kernel,
        out_shape=jax.ShapeDtypeStruct((CAP, 2, TILE, TILE), F32),
        in_specs=[vmem],
        out_specs=vmem,
        name="factors",
    )(pieces)


SWAP = ((0, 1), (1, 0))


def body(hidden_in, query, key_value, grad_out, lengths, owner):
    mine = lax.all_to_all(
        jnp.broadcast_to(key_value, (CHIPS, ROWS, 2 * HD)), "chip", 0, 0, tiled=True
    )
    other = lax.ppermute(mine, "core", SWAP)
    grad_query, dkv_mine, dkv_other = attention(lengths, query[0], grad_out[0], mine, other)
    dkv = (dkv_mine + lax.ppermute(dkv_other, "core", SWAP).astype(F32)).astype(BF16)
    dkv = lax.all_to_all(dkv, "chip", 0, 0, tiled=True)
    grad_kv, wg_mine, wg_other = weight_terms(dkv, hidden_in[0])
    wg = (wg_mine + lax.ppermute(wg_other, "core", SWAP).astype(F32)).astype(BF16)
    wg = lax.all_to_all(wg, "chip", 0, 0, tiled=True)
    outgoing = to_owners(owner, wg)
    incoming = lax.all_to_all(outgoing, "dp", 0, 0, tiled=True)
    pieces = lax.all_to_all(owned_sum(incoming), ("chip", "core"), 0, 0, tiled=True)
    return grad_query[None], grad_kv[None], factors_of(pieces)[None]


def solution(mesh):
    fine = Mesh(mesh.devices.reshape(N_DP, CHIPS, 2), ("dp", "chip", "core"))
    ctx = ("chip", "core")
    return jax.shard_map(
        body,
        mesh=fine,
        in_specs=(
            P("dp", ctx, None),
            P("dp", ctx, None),
            P("dp", ctx, None),
            P("dp", ctx, None),
            P("dp", None),
            P(),
        ),
        out_specs=(P("dp", ctx, None), P("dp", ctx, None), P("dp", None, None, None, None)),
        check_vma=False,
    )
```

time: 822 us -> 142 us (0.17)
  blocking collectives: 376 us -> 87.8 us
  waiting for transfers between devices: 302 us -> 21.5 us
  matrix products: 39.9 us -> 0 us
  local copies, waits for them, and re-layouts: 42.7 us -> 3.53 us
  loops' own time: 31 us -> 0 us
  starting transfers between devices: 0.3 us -> 15.3 us
  between operations: 13.9 us -> 0.7 us
  other arithmetic: 14.3 us -> 1.36 us
  Pallas kernels: 0 us -> 11.3 us
    all_to_all x1 -> x4, blocking collectives: 376 us -> 87.8 us  [the longest x1 34.4 us: body(): incoming = lax.all_to_all(outgoing, 'dp', 0, 0, tiled=True)]
    psum x1 -> x0, waiting for transfers between devices: 147 us -> none  [body(): owned = lax.psum(jnp.sum(incoming, axis=0), 'ctx')]
    reduce_scatter x1 -> x0, waiting for transfers between devices: 89.9 us -> none  [body(): lax.psum_scatter(partial_value, 'ctx', scatter_dimension=0, tiled=True)]
    all_gather x1 -> x0, waiting for transfers between devices: 64.4 us -> none  [body(): gathered = lax.all_gather(key_value[0], 'ctx', axis=0, tiled=True)]
    dot_general x32 -> x0, matrix products: 39.9 us -> none  [the longest x8 8.41 us: scores_of(): jnp.einsum('thd,kd->thk', queries, key_rows, preferred_element_type=jnp.f...]
    another operation x3 -> x0, loops' own time: 31 us -> none  [the longest x1 11.3 us: body(): lax.scan(out_step, jnp.zeros((tok_rows, head_count, head_dim), jnp.float3...]
    all_to_all x0 -> x1, waiting for transfers between devices: none -> 16.2 us  [body(): wg = lax.all_to_all(wg, 'chip', 0, 0, tiled=True)]
    squeeze x12 -> x0, local copies, waits for them, and re-layouts: 11.7 us -> none  [scores_of(): lax.dynamic_index_in_dim(block_rows, block_index, 0, keepdims=False)]
  transfers between devices with their start and end apart: 3 -> 4, of which waited for: 3 -> 4; matrix products, arithmetic and copies ran while one was open for 1% -> 0% of each run, Pallas kernels for 0% -> 0%
where the time goes in v1:
time: 142 us
  blocking collectives  87.8 us (62%)
  waiting for transfers between devices  21.5 us (15%)
  starting transfers between devices  15.3 us (11%)
  Pallas kernels  11.3 us (8%)
  local copies, waits for them, and re-layouts  3.53 us (2%)
    all_to_all x1, blocking collectives, body(): incoming = lax.all_to_all(outgoing, 'dp', 0, 0, tiled=True)  34.4 us
    all_to_all x1, blocking collectives, body(): dkv = lax.all_to_all(dkv, 'chip', 0, 0, tiled=True)  21.3 us
    all_to_all x1, waiting for transfers between devices, body(): wg = lax.all_to_all(wg, 'chip', 0, 0, tiled=True)  16.2 us
    all_to_all x1, blocking collectives, body(): lax.all_to_all(jnp.broadcast_to(key_value, (CHIPS, ROWS, 2 * HD)), 'chip'...  16.1 us
    all_to_all x1, blocking collectives, body(): lax.all_to_all(owned_sum(incoming), ('chip', 'core'), 0, 0, tiled=True)  15.9 us
    ppermute x1, starting transfers between devices, body(): other = lax.ppermute(mine, 'core', SWAP)  5.25 us
    ppermute x1, starting transfers between devices, body(): lax.ppermute(wg_other, 'core', SWAP).astype(F32)  4.13 us
    all_to_all x1, starting transfers between devices, body(): wg = lax.all_to_all(wg, 'chip', 0, 0, tiled=True)  3.69 us
  transfers between devices with their start and end apart: 4, of which 4 were waited for; matrix products, arithmetic and copies ran while one was open for 0% of the time, Pallas kernels for 0%

profile of v1, /device:TPU:1, one launch (start us, length us, event | category | flops | bytes accessed | tf_op | source)
XLA Modules:
  0.0 141.5 jit_solution(4733569327573513752)
XLA Ops:
  0.6 0.9 broadcast_in_dim.17
  1.5 16.1 %all_to_all.25.mine_ref = bf16[8,128,256]{2,1,0:T(8,128)(2,1)S(1)} all-to-all(bf16[8,128,256]{2,1,0:T(8,128)(2,1)S(1)} %broadcast_in_dim.17), channel_id=1, replica_groups=mesh['dp'=32,'chip'=8,'core'=2] {'chip'}, dimensions={0} | all-to-all | bytes 1048576 | tf_op jit(solution)/shard_map/all_to_all | solution.py:290
  17.6 5.3 %collective-permute-start = (bf16[8,128,256]{2,1,0:T(8,128)(2,1)S(1)}, bf16[8,128,256]{2,1,0:T(8,128)(2,1)S(1)}, u32[]{:S(2)}, u32[]{:S(2)}) collective-permute-start(bf16[8,128,256]{2,1,0:T(8,128)(2,1)S(1)} %all_to_all.25.mine_ref), channel_id=1, source_target_pairs={{0,1},{1,0},{2,3},{3,2},{4,5},{5,4},{6,7},{7,6},{8,9},{9,8},{10,11... | collective-permute-start | bytes 1572872 | tf_op jit(solution)/shard_map/ppermute | solution.py:293
  22.9 1.5 %collective-permute-done.other_ref = bf16[8,128,256]{2,1,0:T(8,128)(2,1)S(1)} collective-permute-done((bf16[8,128,256]{2,1,0:T(8,128)(2,1)S(1)}, bf16[8,128,256]{2,1,0:T(8,128)(2,1)S(1)}, u32[]{:S(2)}, u32[]{:S(2)}) %collective-permute-start) | collective-permute-done | bytes 524320 | tf_op jit(solution)/shard_map/ppermute | solution.py:293
  24.4 0.9 copy-done.1
  25.4 0.9 copy-done.2
  26.3 0.7 copy-done.3
  27.0 3.1 %attention_backward.1 = (bf16[128,1024]{1,0:T(8,128)(2,1)}, f32[8,128,256]{2,1,0:T(8,128)S(1)}, bf16[8,128,256]{2,1,0:T(8,128)(2,1)S(1)}) custom-call(s32[1,8]{1,0:T(1,128)S(1)} %copy-done.3, bf16[128,1024]{1,0:T(8,128)(2,1)S(1)} %bitcast.8, bf16[128,1024]{1,0:T(8,128)(2,1)S(1)} %bitcast.9, bf16[8,128,256]{2,1,0:T(8,128)(2,1)S(1)} %all_to_all.25.mine_ref, ...), custom_call_target="tpu_custom_call" | custom-call | tf_op jit(solution)/shard_map/attention_backward/pallas_call | solution.py:136
  30.1 2.3 %collective-permute-start.1 = (bf16[8,128,256]{2,1,0:T(8,128)(2,1)S(1)}, bf16[8,128,256]{2,1,0:T(8,128)(2,1)S(1)}, u32[]{:S(2)}, u32[]{:S(2)}) collective-permute-start(bf16[8,128,256]{2,1,0:T(8,128)(2,1)S(1)} %get-tuple-element.11), channel_id=1, source_target_pairs={{0,1},{1,0},{2,3},{3,2},{4,5},{5,4},{6,7},{7,6},{8,9},{9,8},{10,11... | collective-permute-start | bytes 1572872 | tf_op jit(solution)/shard_map/ppermute | solution.py:295
  32.4 1.5 %collective-permute-done.1 = bf16[8,128,256]{2,1,0:T(8,128)(2,1)S(1)} collective-permute-done((bf16[8,128,256]{2,1,0:T(8,128)(2,1)S(1)}, bf16[8,128,256]{2,1,0:T(8,128)(2,1)S(1)}, u32[]{:S(2)}, u32[]{:S(2)}) %collective-permute-start.1) | collective-permute-done | bytes 524320 | tf_op jit(solution)/shard_map/ppermute | solution.py:295
  33.9 0.1 add_convert_fusion.1
  34.0 21.3 %all_to_all.26.parts_ref = bf16[8,128,256]{2,1,0:T(8,128)(2,1)S(1)} all-to-all(bf16[8,128,256]{2,1,0:T(8,128)(2,1)S(1)} %add_convert_fusion.1), channel_id=1, replica_groups=mesh['dp'=32,'chip'=8,'core'=2] {'chip'}, dimensions={0} | all-to-all | bytes 1048576 | tf_op jit(solution)/shard_map/all_to_all | solution.py:296
  55.4 2.7 %weight_gradient.1 = (bf16[128,256]{1,0:T(8,128)(2,1)}, f32[8,512,128]{2,1,0:T(8,128)S(1)}, bf16[8,512,128]{2,1,0:T(8,128)(2,1)S(1)}) custom-call(bf16[8,128,256]{2,1,0:T(8,128)(2,1)S(1)} %all_to_all.26.parts_ref, bf16[128,8192]{1,0:T(8,128)(2,1)S(1)} %bitcast.7), custom_call_target="tpu_custom_call" | custom-call | tf_op jit(solution)/shard_map/weight_gradient/pallas_call | solution.py:191
  58.0 4.1 %collective-permute-start.2 = (bf16[8,512,128]{2,1,0:T(8,128)(2,1)S(1)}, bf16[8,512,128]{2,1,0:T(8,128)(2,1)S(1)}, u32[]{:S(2)}, u32[]{:S(2)}) collective-permute-start(bf16[8,512,128]{2,1,0:T(8,128)(2,1)S(1)} %get-tuple-element.14), channel_id=1, source_target_pairs={{0,1},{1,0},{2,3},{3,2},{4,5},{5,4},{6,7},{7,6},{8,9},{9,8},{10,11... | collective-permute-start | bytes 3145736 | tf_op jit(solution)/shard_map/ppermute | solution.py:298
  62.2 2.3 %collective-permute-done.2 = bf16[8,512,128]{2,1,0:T(8,128)(2,1)S(1)} collective-permute-done((bf16[8,512,128]{2,1,0:T(8,128)(2,1)S(1)}, bf16[8,512,128]{2,1,0:T(8,128)(2,1)S(1)}, u32[]{:S(2)}, u32[]{:S(2)}) %collective-permute-start.2) | collective-permute-done | bytes 1048608 | tf_op jit(solution)/shard_map/ppermute | solution.py:298
  64.4 1.2 add_convert_fusion
  65.7 3.7 %all-to-all-start.2 = ((bf16[8,512,128]{2,1,0:T(8,128)(2,1)}), bf16[8,512,128]{2,1,0:T(8,128)(2,1)S(1)}, u32[]{:S(2)}, u32[]{:S(2)}) async-start(bf16[8,512,128]{2,1,0:T(8,128)(2,1)} %add_convert_fusion), calls=%async_computation.2 | async-start | bytes 2097152 | tf_op jit(solution)/shard_map/all_to_all | solution.py:299
  69.4 0.1 copy.9.owner_ref
  69.5 16.2 %all-to-all-done.2.parts_ref = bf16[8,512,128]{2,1,0:T(8,128)(2,1)S(1)} async-done(((bf16[8,512,128]{2,1,0:T(8,128)(2,1)}), bf16[8,512,128]{2,1,0:T(8,128)(2,1)S(1)}, u32[]{:S(2)}, u32[]{:S(2)}) %all-to-all-start.2) | async-done | bytes 1048608 | tf_op jit(solution)/shard_map/all_to_all | solution.py:299
  85.7 1.8 %owner_slots.1 = bf16[32,32,128]{2,1,0:T(8,128)(2,1)S(1)} custom-call(s32[64,1]{1,0:T(8,128)S(1)} %copy.9.owner_ref, bf16[8,512,128]{2,1,0:T(8,128)(2,1)S(1)} %all-to-all-done.2.parts_ref), custom_call_target="tpu_custom_call" | custom-call | tf_op jit(solution)/shard_map/owner_slots/pallas_call | solution.py:234
  87.5 34.4 %all_to_all.27.parts_ref = bf16[32,32,128]{2,1,0:T(8,128)(2,1)} all-to-all(bf16[32,32,128]{2,1,0:T(8,128)(2,1)S(1)} %owner_slots.1), channel_id=1, replica_groups=mesh['dp'=32,'chip'=8,'core'=2] {'dp'}, dimensions={0} | all-to-all | bytes 524288 | tf_op jit(solution)/shard_map/all_to_all | solution.py:301
  122.0 1.7 %owned_sum.1 = bf16[16,32,128]{2,1,0:T(8,128)(2,1)} custom-call(bf16[32,32,128]{2,1,0:T(8,128)(2,1)} %all_to_all.27.parts_ref), custom_call_target="tpu_custom_call" | custom-call | tf_op jit(solution)/shard_map/owned_sum/pallas_call | solution.py:256
  123.6 15.9 %all_to_all.28.pieces_ref = bf16[16,32,128]{2,1,0:T(8,128)(2,1)} all-to-all(bf16[16,32,128]{2,1,0:T(8,128)(2,1)} %owned_sum.1), channel_id=1, replica_groups=mesh['dp'=32,'chip'=8,'core'=2] {'chip','core'}, dimensions={0} | all-to-all | bytes 262144 | tf_op jit(solution)/shard_map/all_to_all | solution.py:302
  139.6 2.0 %factors.1 = f32[4,2,128,128]{3,2,1,0:T(8,128)} custom-call(bf16[16,32,128]{2,1,0:T(8,128)(2,1)} %all_to_all.28.pieces_ref), custom_call_target="tpu_custom_call" | custom-call | tf_op jit(solution)/shard_map/factors/pallas_call | solution.py:277
  (7 shorter events, 0.0 us)
Async XLA Ops:
  17.6 6.8 %collective-permute-start = (bf16[8,128,256]{2,1,0:T(8,128)(2,1)S(1)}, bf16[8,128,256]{2,1,0:T(8,128)(2,1)S(1)}, u32[]{:S(2)}, u32[]{:S(2)}) collective-permute-start(bf16[8,128,256]{2,1,0:T(8,128)(2,1)S(1)} %all_to_all.25.mine_ref), channel_id=1, source_target_pairs={{0,1},{1,0},{2,3},{3,2},{4,5},{5,4},{6,7},{7,6},{8,9},{9,8},{10,11... | collective-permute-start | bytes 1572872 | tf_op jit(solution)/shard_map/ppermute | solution.py:293
  24.4 0.9 copy-start.1
  25.4 0.9 copy-start.2
  26.3 0.7 copy-start.3
  27.0 28.4 %copy-start = (bf16[1,128,8192]{2,1,0:T(8,128)(2,1)S(1)}, bf16[1,128,8192]{2,1,0:T(8,128)(2,1)}, u32[]{:S(2)}) copy-start(bf16[1,128,8192]{2,1,0:T(8,128)(2,1)} %param.6) | copy-start | bytes 6291460
  30.1 3.8 %collective-permute-start.1 = (bf16[8,128,256]{2,1,0:T(8,128)(2,1)S(1)}, bf16[8,128,256]{2,1,0:T(8,128)(2,1)S(1)}, u32[]{:S(2)}, u32[]{:S(2)}) collective-permute-start(bf16[8,128,256]{2,1,0:T(8,128)(2,1)S(1)} %get-tuple-element.11), channel_id=1, source_target_pairs={{0,1},{1,0},{2,3},{3,2},{4,5},{5,4},{6,7},{7,6},{8,9},{9,8},{10,11... | collective-permute-start | bytes 1572872 | tf_op jit(solution)/shard_map/ppermute | solution.py:295
  58.0 6.4 %collective-permute-start.2 = (bf16[8,512,128]{2,1,0:T(8,128)(2,1)S(1)}, bf16[8,512,128]{2,1,0:T(8,128)(2,1)S(1)}, u32[]{:S(2)}, u32[]{:S(2)}) collective-permute-start(bf16[8,512,128]{2,1,0:T(8,128)(2,1)S(1)} %get-tuple-element.14), channel_id=1, source_target_pairs={{0,1},{1,0},{2,3},{3,2},{4,5},{5,4},{6,7},{7,6},{8,9},{9,8},{10,11... | collective-permute-start | bytes 3145736 | tf_op jit(solution)/shard_map/ppermute | solution.py:298
  65.7 3.7 %copy-start.4 = (s32[64,1]{0,1:T(1,128)S(1)}, s32[64,1]{0,1:T(1,128)}, u32[]{:S(2)}) copy-start(s32[64,1]{0,1:T(1,128)} %param.11) | copy-start | bytes 772
  65.7 20.0 %all-to-all-start.2 = ((bf16[8,512,128]{2,1,0:T(8,128)(2,1)}), bf16[8,512,128]{2,1,0:T(8,128)(2,1)S(1)}, u32[]{:S(2)}, u32[]{:S(2)}) async-start(bf16[8,512,128]{2,1,0:T(8,128)(2,1)} %add_convert_fusion), calls=%async_computation.2 | async-start | bytes 2097152 | tf_op jit(solution)/shard_map/all_to_all | solution.py:299

commit v2 on v1

v2 whole, which is shorter than its diff:
```python
import math

import jax
import jax.numpy as jnp
from jax import lax
from jax.experimental import pallas as pl
from jax.experimental.pallas import tpu as pltpu
from jax.sharding import Mesh
from jax.sharding import PartitionSpec as P

HEADS = 8
HD = 128
TILE = 128
ROWS = 128
CHIPS = 8
SEQ = 2048
TILES = 64
CAP = 4
N_DP = 32
MODEL = 8192
N_YL = 2
N_Z = 16
PLANE = N_YL * CHIPS
OWNED = N_YL * CAP * 4
BLOCK = 1024
GROUP = 2
HIDDEN_NEG = -1e30
SCALE = 1.0 / math.sqrt(HD)
EXP2_SCALE = SCALE * math.log2(math.e)
F32 = jnp.float32
BF16 = jnp.bfloat16


def attention_kernel(
    lengths_hbm, q_hbm, go_hbm, mine_ref, other_ref,
    dq_ref, dmine_ref, dother_ref,
    lengths_ref, q_ref, go_ref, q_rows, go_rows, k_all, v_all,
    scores, prob_grads, ds_buf, w_buf, top, total, delta, dq_t, sems,
):
    copies = [
        pltpu.make_async_copy(q_hbm, q_ref, sems.at[0]),
        pltpu.make_async_copy(go_hbm, go_ref, sems.at[1]),
        pltpu.make_async_copy(lengths_hbm, lengths_ref, sems.at[2]),
    ]
    for copy in copies:
        copy.start()
    chip = lax.axis_index("chip")
    core = lax.axis_index("core")
    first = (2 * chip + core) * ROWS
    for ref, side in ((mine_ref, core), (other_ref, 1 - core)):
        for j in range(CHIPS):
            rows = pl.ds(pl.multiple_of((2 * j + side) * ROWS, ROWS), ROWS)
            k_all[rows, :] = ref[j, :, :HD]
            v_all[rows, :] = ref[j, :, HD:]
    top[...] = jnp.full(top.shape, HIDDEN_NEG, F32)
    total[...] = jnp.zeros(total.shape, F32)
    delta[...] = jnp.zeros(delta.shape, F32)
    dq_t[...] = jnp.zeros(dq_t.shape, F32)
    dmine_ref[...] = jnp.zeros(dmine_ref.shape, dmine_ref.dtype)
    dother_ref[...] = jnp.zeros(dother_ref.shape, dother_ref.dtype)
    for copy in copies:
        copy.wait()
    for h in range(HEADS):
        cols = pl.ds(h * HD, HD)
        q_rows[cols, :] = q_ref[:, cols]
        go_rows[cols, :] = go_ref[:, cols]
    row_pos = first + lax.broadcasted_iota(jnp.int32, (1, ROWS), 1)
    row_low = jnp.zeros((1, ROWS), jnp.int32)
    first_low = jnp.int32(0)
    end = jnp.int32(0)
    for d in range(lengths_ref.shape[1]):
        end = end + lengths_ref[0, d]
        row_low = jnp.maximum(row_low, jnp.where(row_pos >= end, end, 0))
        first_low = jnp.maximum(first_low, jnp.where(first >= end, end, 0))
    low_block = first_low // BLOCK
    high_block = (first + ROWS - 1) // BLOCK + 1

    def fold(values, op):
        return op(values.reshape(values.shape[0] // 8, 8, values.shape[1]), axis=0)

    def against(rows, ref, cols):
        return lax.dot_general(
            rows, ref[cols, :], (((1,), (1,)), ((), ())), preferred_element_type=F32
        )

    def score_step(j, carry):
        rows = pl.ds(pl.multiple_of(j * BLOCK, BLOCK), BLOCK)
        pos = j * BLOCK + lax.broadcasted_iota(jnp.int32, (BLOCK, ROWS), 0)
        seen = (pos >= row_low) & (pos <= row_pos)
        seen = jnp.concatenate([seen] * GROUP, axis=1)
        keys = k_all[rows, :]
        for g in range(HEADS // GROUP):
            cols = pl.ds(g * GROUP * HD, GROUP * HD)
            s = jnp.where(seen, against(keys, q_rows, cols), HIDDEN_NEG)
            scores[rows, cols] = s
            top[:, cols] = jnp.maximum(top[:, cols], fold(s, jnp.max))
        return carry

    lax.fori_loop(low_block, high_block, score_step, 0)
    top[0:1, :] = jnp.max(top[...], axis=0, keepdims=True)

    def weight_step(j, carry):
        rows = pl.ds(pl.multiple_of(j * BLOCK, BLOCK), BLOCK)
        values = v_all[rows, :]
        for g in range(HEADS // GROUP):
            cols = pl.ds(g * GROUP * HD, GROUP * HD)
            pg = against(values, go_rows, cols)
            p = jnp.exp2((scores[rows, cols] - top[0:1, cols]) * EXP2_SCALE)
            scores[rows, cols] = p
            prob_grads[rows, cols] = pg
            total[:, cols] += fold(p, jnp.sum)
            delta[:, cols] += fold(p * pg, jnp.sum)
        return carry

    lax.fori_loop(low_block, high_block, weight_step, 0)
    inverse = 1.0 / jnp.sum(total[...], axis=0, keepdims=True)
    total[0:1, :] = inverse
    delta[0:1, :] = jnp.sum(delta[...], axis=0, keepdims=True) * inverse

    def back_step(j, carry):
        rows = pl.ds(pl.multiple_of(j * BLOCK, BLOCK), BLOCK)
        for g in range(HEADS // GROUP):
            cols = pl.ds(g * GROUP * HD, GROUP * HD)
            w = scores[rows, cols] * total[0:1, cols]
            w_buf[:, cols] = w.astype(BF16)
            ds_buf[:, cols] = (w * (prob_grads[rows, cols] - delta[0:1, cols])).astype(BF16)
        ds = ds_buf[...]
        dk = jnp.dot(ds, q_rows[...], preferred_element_type=F32) * SCALE
        dv = jnp.dot(w_buf[...], go_rows[...], preferred_element_type=F32)
        dq_t[...] += lax.dot_general(
            k_all[rows, :], ds, (((0,), (0,)), ((), ())), preferred_element_type=F32
        )
        for i in range(BLOCK // ROWS):
            here = slice(i * ROWS, (i + 1) * ROWS)
            pair = j * (BLOCK // (2 * ROWS)) + i // 2

            @pl.when(core == i % 2)
            def _():
                dmine_ref[pair, :, :HD] = dk[here]
                dmine_ref[pair, :, HD:] = dv[here]

            @pl.when(core != i % 2)
            def _():
                dother_ref[pair, :, :HD] = dk[here].astype(BF16)
                dother_ref[pair, :, HD:] = dv[here].astype(BF16)

        return carry

    lax.fori_loop(low_block, high_block, back_step, 0)
    for h in range(HEADS):
        cols = pl.ds(h * HD, HD)
        dq_ref[:, cols] = (dq_t[:, cols].T * SCALE).astype(BF16)


VMEM = pl.BlockSpec(memory_space=pltpu.VMEM)


def in_hbm(x):
    return pltpu.with_memory_space_constraint(x, pltpu.HBM)


def limit(mib):
    return pltpu.CompilerParams(vmem_limit_bytes=mib * 1024 * 1024)


def attention(lengths, query, grad_out, mine, other):
    hbm = pl.BlockSpec(memory_space=pltpu.HBM)
    wide = HEADS * HD
    return pl.pallas_call(
        attention_kernel,
        out_shape=(
            jax.ShapeDtypeStruct((ROWS, wide), BF16),
            jax.ShapeDtypeStruct((CHIPS, ROWS, 2 * HD), F32),
            jax.ShapeDtypeStruct((CHIPS, ROWS, 2 * HD), BF16),
        ),
        in_specs=[hbm, hbm, hbm, VMEM, VMEM],
        out_specs=(VMEM, VMEM, VMEM),
        scratch_shapes=[
            pltpu.SMEM((1, 8), jnp.int32),
            pltpu.VMEM((ROWS, wide), BF16),
            pltpu.VMEM((ROWS, wide), BF16),
            pltpu.VMEM((wide, HD), BF16),
            pltpu.VMEM((wide, HD), BF16),
            pltpu.VMEM((SEQ, HD), BF16),
            pltpu.VMEM((SEQ, HD), BF16),
            pltpu.VMEM((SEQ, wide), F32),
            pltpu.VMEM((SEQ, wide), F32),
            pltpu.VMEM((BLOCK, wide), BF16),
            pltpu.VMEM((BLOCK, wide), BF16),
            pltpu.VMEM((8, wide), F32),
            pltpu.VMEM((8, wide), F32),
            pltpu.VMEM((8, wide), F32),
            pltpu.VMEM((HD, wide), F32),
            pltpu.SemaphoreType.DMA((3,)),
        ],
        compiler_params=limit(44),
        name="attention_backward",
    )(in_hbm(lengths), in_hbm(query), in_hbm(grad_out), mine, other)


STEP_TILES = 8


def low_half(shape, axis):
    return lax.broadcasted_iota(jnp.int32, shape, axis) < 4


def weight_kernel(parts_ref, hidden_ref, kv_ref, mine_ref, other_ref, k_t):
    core = lax.axis_index("core")
    shape = (PLANE, 8, TILE)

    @pl.when(pl.program_id(0) == 0)
    def _():
        low = jnp.sum(parts_ref[...].astype(F32), axis=0).astype(BF16)
        kv_ref[...] = low
        key_t = low[:, :HD].astype(F32).T.reshape(shape)
        key_t = jnp.where(core == 0, key_t, pltpu.roll(key_t, 4, axis=1))
        k_t[...] = key_t.reshape(HD, ROWS).astype(BF16)

    grad_t = jnp.dot(k_t[...], hidden_ref[...], preferred_element_type=F32)
    low = low_half(shape, 1)

    def pieces(pair):
        even = grad_t[:, (2 * pair) * TILE : (2 * pair + 1) * TILE].reshape(shape)
        odd = grad_t[:, (2 * pair + 1) * TILE : (2 * pair + 2) * TILE].reshape(shape)
        here = jnp.where(low, even, pltpu.roll(odd, 4, axis=1))
        there = jnp.where(low, pltpu.roll(even, 4, axis=1), odd)
        return here, there

    for quad in range(STEP_TILES // 4):
        first, second = pieces(2 * quad), pieces(2 * quad + 1)
        rows = pl.ds(quad * 16, 16)
        mine_ref[:, rows, :] = jnp.concatenate([first[0], second[0]], axis=1)
        other_ref[:, rows, :] = jnp.concatenate([first[1], second[1]], axis=1).astype(BF16)


def weight_terms(parts, hidden):
    steps = TILES // STEP_TILES
    rows = STEP_TILES * 4
    return pl.pallas_call(
        weight_kernel,
        grid=(steps,),
        out_shape=(
            jax.ShapeDtypeStruct((ROWS, 2 * HD), BF16),
            jax.ShapeDtypeStruct((PLANE, TILES * 4, TILE), F32),
            jax.ShapeDtypeStruct((PLANE, TILES * 4, TILE), BF16),
        ),
        in_specs=[
            pl.BlockSpec((CHIPS, ROWS, 2 * HD), lambda i: (0, 0, 0)),
            pl.BlockSpec((ROWS, STEP_TILES * TILE), lambda i: (0, i)),
        ],
        out_specs=(
            pl.BlockSpec((ROWS, 2 * HD), lambda i: (0, 0)),
            pl.BlockSpec((PLANE, rows, TILE), lambda i: (0, i, 0)),
            pl.BlockSpec((PLANE, rows, TILE), lambda i: (0, i, 0)),
        ),
        scratch_shapes=[pltpu.VMEM((HD, ROWS), BF16)],
        compiler_params=limit(16),
        name="weight_gradient",
    )(parts, hidden)


def owner_kernel(owner_ref, parts_ref, out_ref, sums, placed, held):
    rows = TILES * 4
    own = jnp.sum(parts_ref[...].astype(F32), axis=0)
    sums[:rows, :] = own
    sums[rows:, :] = pltpu.roll(own.reshape(rows // 8, 8, TILE), 4, axis=1).reshape(rows, TILE)
    placed[...] = jnp.zeros(placed.shape, F32)
    for o in range(N_DP):
        held[o] = 0
    low = low_half((8, TILE), 0)
    for t in range(TILES):
        o = owner_ref[0, t]
        slot = held[o]
        held[o] = slot + 1
        half = slot & 1
        block = ((o & (N_Z - 1)) * N_YL + o // N_Z) * (CAP // 2) + slot // 2
        at = pl.ds(pl.multiple_of(block * 8, 8), 8)
        source = pl.multiple_of((half ^ (t & 1)) * rows + (t // 2) * 8, 8)
        placed[at, :] = jnp.where(low == (half == 0), sums[pl.ds(source, 8), :], placed[at, :])
    out_ref[...] = placed[...].astype(BF16).reshape(out_ref.shape)


def to_owners(owner, parts):
    return pl.pallas_call(
        owner_kernel,
        out_shape=jax.ShapeDtypeStruct((N_Z, OWNED, TILE), BF16),
        in_specs=[pl.BlockSpec(memory_space=pltpu.SMEM), VMEM],
        out_specs=VMEM,
        scratch_shapes=[
            pltpu.VMEM((2 * TILES * 4, TILE), F32),
            pltpu.VMEM((N_Z * OWNED, TILE), F32),
            pltpu.SMEM((N_DP,), jnp.int32),
        ],
        compiler_params=limit(12),
        name="owner_slots",
    )(owner, parts)


def sum_kernel(parts_ref, out_ref):
    gradient = jnp.sum(parts_ref[...].astype(F32), axis=0) * (1.0 / math.sqrt(N_DP * SEQ))
    gradient = gradient.astype(BF16)
    rows = OWNED // N_YL
    for yl in range(N_YL):
        piece = gradient[yl * rows : (yl + 1) * rows]
        out_ref[yl * PLANE : (yl + 1) * PLANE] = jnp.broadcast_to(piece[None], (PLANE, rows, TILE))


def owned_sum(parts):
    return pl.pallas_call(
        sum_kernel,
        out_shape=jax.ShapeDtypeStruct((2 * PLANE, OWNED // N_YL, TILE), BF16),
        in_specs=[VMEM],
        out_specs=VMEM,
        compiler_params=limit(8),
        name="owned_sum",
    )(parts)


def factor_kernel(pieces_ref, out_ref):
    pieces = pieces_ref[...].astype(F32)
    low = low_half((PLANE, 8, TILE), 1)
    for two in range(CAP // 2):
        pair = pieces[:, two * 8 : (two + 1) * 8, :].reshape(PLANE, 2, 8, TILE)
        even, odd = pair[:, 0], pair[:, 1]
        both = (
            jnp.where(low, even, pltpu.roll(odd, 4, axis=1)),
            jnp.where(low, pltpu.roll(even, 4, axis=1), odd),
        )
        for i in range(2):
            grad_t = both[i].reshape(TILE, TILE)
            flat = grad_t.astype(BF16)
            flat_t = grad_t.T.astype(BF16)
            s = 2 * two + i
            out_ref[s, 0] = jnp.dot(flat_t, flat, preferred_element_type=F32) * (1.0 / TILE)
            out_ref[s, 1] = jnp.dot(flat, flat_t, preferred_element_type=F32) * (1.0 / TILE)


def factors_of(pieces):
    return pl.pallas_call(
        factor_kernel,
        out_shape=jax.ShapeDtypeStruct((CAP, 2, TILE, TILE), F32),
        in_specs=[VMEM],
        out_specs=VMEM,
        compiler_params=limit(8),
        name="factors",
    )(pieces)


SWAP = ((0, 1), (1, 0))


def body(hidden_in, query, key_value, grad_out, lengths, owner):
    mine = lax.all_to_all(
        jnp.broadcast_to(key_value, (CHIPS, ROWS, 2 * HD)), "chip", 0, 0, tiled=True
    )
    other = lax.ppermute(mine, "core", SWAP)
    grad_query, dkv_mine, dkv_other = attention(lengths, query[0], grad_out[0], mine, other)
    dkv = (dkv_mine + lax.ppermute(dkv_other, "core", SWAP).astype(F32)).astype(BF16)
    dkv = lax.all_to_all(dkv, "chip", 0, 0, tiled=True)
    grad_kv, wg_mine, wg_other = weight_terms(dkv, hidden_in[0])
    wg = (wg_mine + lax.ppermute(wg_other, "core", SWAP).astype(F32)).astype(BF16)
    wg = lax.all_to_all(wg, ("yl", "chip"), 0, 0, tiled=True)
    outgoing = to_owners(owner.reshape(1, TILES), wg)
    incoming = lax.all_to_all(outgoing, "z", 0, 0, tiled=True)
    pieces = lax.all_to_all(owned_sum(incoming), ("yl", "chip", "core"), 0, 0, tiled=True)
    return grad_query[None], grad_kv[None], factors_of(pieces)[None]


def solution(mesh):
    fine = Mesh(mesh.devices.reshape(N_YL, N_Z, CHIPS, 2), ("yl", "z", "chip", "core"))
    dp, ctx = ("yl", "z"), ("chip", "core")
    split = P(dp, ctx, None)
    return jax.shard_map(
        body,
        mesh=fine,
        in_specs=(split, split, split, split, P(dp, None), P()),
        out_specs=(split, split, P(dp, None, None, None, None)),
        check_vma=False,
    )
```

time: 142 us -> 123 us (0.87)
  waiting for transfers between devices: 21.5 us -> 5.29 us
  blocking collectives: 87.8 us -> 92.8 us
  starting transfers between devices: 15.3 us -> 11.7 us
  local copies, waits for them, and re-layouts: 3.53 us -> 0.88 us
    all_to_all x1 -> x0, waiting for transfers between devices: 16.2 us -> none  [body(): wg = lax.all_to_all(wg, 'chip', 0, 0, tiled=True)]
    all_to_all x2 -> x3, blocking collectives: 50.4 us -> 60.8 us  [the longest x1 26.7 us: body(): incoming = lax.all_to_all(outgoing, 'z', 0, 0, tiled=True)]
    all_to_all x1, blocking collectives: 21.3 us -> 15.9 us  [body(): dkv = lax.all_to_all(dkv, 'chip', 0, 0, tiled=True)]
    all_to_all x1 -> x0, starting transfers between devices: 3.69 us -> none  [body(): wg = lax.all_to_all(wg, 'chip', 0, 0, tiled=True)]
    pallas_call x1, Pallas kernels: 3.13 us -> 5.79 us  [attention(): pl.pallas_call(attention_kernel, out_shape=(jax.ShapeDtypeStruct((ROWS, w...]
    unnamed x11 -> x4, local copies, waits for them, and re-layouts: 2.66 us -> 0.01 us
    pallas_call x2, Pallas kernels: 3.48 us -> 1.59 us  [the longest x1 1.56 us: to_owners(): pl.pallas_call(owner_kernel, out_shape=jax.ShapeDtypeStruct((N_Z, OWNED,...]
  transfers between devices with their start and end apart: 4 -> 3, of which waited for: 4 -> 3; matrix products, arithmetic and copies ran while one was open for 0% -> 0% of each run, Pallas kernels for 0% -> 0%
where the time goes in v2:
time: 123 us
  blocking collectives  92.8 us (75%)
  starting transfers between devices  11.7 us (10%)
  Pallas kernels  11.2 us (9%)
  waiting for transfers between devices  5.29 us (4%)
    all_to_all x1, blocking collectives, body(): incoming = lax.all_to_all(outgoing, 'z', 0, 0, tiled=True)  26.7 us
    all_to_all x1, blocking collectives, body(): wg = lax.all_to_all(wg, ('yl', 'chip'), 0, 0, tiled=True)  18.6 us
    all_to_all x1, blocking collectives, body(): lax.all_to_all(jnp.broadcast_to(key_value, (CHIPS, ROWS, 2 * HD)), 'chip'...  16.1 us
    all_to_all x1, blocking collectives, body(): dkv = lax.all_to_all(dkv, 'chip', 0, 0, tiled=True)  15.9 us
    all_to_all x1, blocking collectives, body(): lax.all_to_all(owned_sum(incoming), ('yl', 'chip', 'core'), 0, 0, tiled=T...  15.5 us
    pallas_call x1, Pallas kernels, attention(): pl.pallas_call(attention_kernel, out_shape=(jax.ShapeDtypeStruct((ROWS, w...  5.79 us
    ppermute x1, starting transfers between devices, body(): other = lax.ppermute(mine, 'core', SWAP)  5.25 us
    ppermute x1, starting transfers between devices, body(): lax.ppermute(wg_other, 'core', SWAP).astype(F32)  4.13 us
  transfers between devices with their start and end apart: 3, of which 3 were waited for; matrix products, arithmetic and copies ran while one was open for 0% of the time, Pallas kernels for 0%

profile of v2, /device:TPU:1, one launch (start us, length us, event | category | flops | bytes accessed | tf_op | source)
XLA Modules:
  0.0 122.9 jit_solution(9570674989165104850)
XLA Ops:
  0.6 0.9 broadcast_in_dim.17
  1.5 16.1 %all_to_all.25.mine_ref = bf16[8,128,256]{2,1,0:T(8,128)(2,1)S(1)} all-to-all(bf16[8,128,256]{2,1,0:T(8,128)(2,1)S(1)} %broadcast_in_dim.17), channel_id=1, replica_groups=mesh['yl'=2,'z'=16,'chip'=8,'core'=2] {'chip'}, dimensions={0} | all-to-all | bytes 1048576 | tf_op jit(solution)/shard_map/all_to_all | solution.py:354
  17.6 5.3 %collective-permute-start = (bf16[8,128,256]{2,1,0:T(8,128)(2,1)S(1)}, bf16[8,128,256]{2,1,0:T(8,128)(2,1)S(1)}, u32[]{:S(2)}, u32[]{:S(2)}) collective-permute-start(bf16[8,128,256]{2,1,0:T(8,128)(2,1)S(1)} %all_to_all.25.mine_ref), channel_id=1, source_target_pairs={{0,1},{1,0},{2,3},{3,2},{4,5},{5,4},{6,7},{7,6},{8,9},{9,8},{10,11... | collective-permute-start | bytes 1572872 | tf_op jit(solution)/shard_map/ppermute | solution.py:357
  22.9 1.5 %collective-permute-done.other_ref = bf16[8,128,256]{2,1,0:T(8,128)(2,1)S(1)} collective-permute-done((bf16[8,128,256]{2,1,0:T(8,128)(2,1)S(1)}, bf16[8,128,256]{2,1,0:T(8,128)(2,1)S(1)}, u32[]{:S(2)}, u32[]{:S(2)}) %collective-permute-start) | collective-permute-done | bytes 524320 | tf_op jit(solution)/shard_map/ppermute | solution.py:357
  24.4 0.0 copy-start
  24.4 5.8 %attention_backward.1 = (bf16[128,1024]{1,0:T(8,128)(2,1)}, f32[8,128,256]{2,1,0:T(8,128)S(1)}, bf16[8,128,256]{2,1,0:T(8,128)(2,1)S(1)}) custom-call(s32[1,8]{1,0:T(1,128)} %lengths_hbm.1, bf16[128,1024]{1,0:T(8,128)(2,1)} %bitcast.11, bf16[128,1024]{1,0:T(8,128)(2,1)} %bitcast.12, bf16[8,128,256]{2,1,0:T(8,128)(2,1)S(1)} %all_to_all.25.mine_ref, ...), custom_call_target="tpu_custom_call" | custom-call | tf_op jit(solution)/shard_map/attention_backward/pallas_call | solution.py:169
  30.2 2.3 %collective-permute-start.1 = (bf16[8,128,256]{2,1,0:T(8,128)(2,1)S(1)}, bf16[8,128,256]{2,1,0:T(8,128)(2,1)S(1)}, u32[]{:S(2)}, u32[]{:S(2)}) collective-permute-start(bf16[8,128,256]{2,1,0:T(8,128)(2,1)S(1)} %get-tuple-element.11), channel_id=1, source_target_pairs={{0,1},{1,0},{2,3},{3,2},{4,5},{5,4},{6,7},{7,6},{8,9},{9,8},{10,11... | collective-permute-start | bytes 1572872 | tf_op jit(solution)/shard_map/ppermute | solution.py:359
  32.5 1.5 %collective-permute-done.1 = bf16[8,128,256]{2,1,0:T(8,128)(2,1)S(1)} collective-permute-done((bf16[8,128,256]{2,1,0:T(8,128)(2,1)S(1)}, bf16[8,128,256]{2,1,0:T(8,128)(2,1)S(1)}, u32[]{:S(2)}, u32[]{:S(2)}) %collective-permute-start.1) | collective-permute-done | bytes 524320 | tf_op jit(solution)/shard_map/ppermute | solution.py:359
  34.0 0.1 add_convert_fusion.1
  34.1 15.9 %all_to_all.26.parts_ref = bf16[8,128,256]{2,1,0:T(8,128)(2,1)S(1)} all-to-all(bf16[8,128,256]{2,1,0:T(8,128)(2,1)S(1)} %add_convert_fusion.1), channel_id=1, replica_groups=mesh['yl'=2,'z'=16,'chip'=8,'core'=2] {'chip'}, dimensions={0} | all-to-all | bytes 1048576 | tf_op jit(solution)/shard_map/all_to_all | solution.py:360
  50.0 0.0 copy-done
  50.0 2.7 %weight_gradient.1 = (bf16[128,256]{1,0:T(8,128)(2,1)}, f32[16,256,128]{2,1,0:T(8,128)S(1)}, bf16[16,256,128]{2,1,0:T(8,128)(2,1)S(1)}) custom-call(bf16[8,128,256]{2,1,0:T(8,128)(2,1)S(1)} %all_to_all.26.parts_ref, bf16[128,8192]{1,0:T(8,128)(2,1)S(1)} %bitcast.8), custom_call_target="tpu_custom_call" | custom-call | tf_op jit(solution)/shard_map/weight_gradient/pallas_call | solution.py:240
  52.8 4.1 %collective-permute-start.2 = (bf16[16,256,128]{2,1,0:T(8,128)(2,1)S(1)}, bf16[16,256,128]{2,1,0:T(8,128)(2,1)S(1)}, u32[]{:S(2)}, u32[]{:S(2)}) collective-permute-start(bf16[16,256,128]{2,1,0:T(8,128)(2,1)S(1)} %get-tuple-element.14), channel_id=1, source_target_pairs={{0,1},{1,0},{2,3},{3,2},{4,5},{5,4},{6,7},{7,6},{8,9},{9,8},{10,11... | collective-permute-start | bytes 3145736 | tf_op jit(solution)/shard_map/ppermute | solution.py:362
  56.9 2.3 %collective-permute-done.2 = bf16[16,256,128]{2,1,0:T(8,128)(2,1)S(1)} collective-permute-done((bf16[16,256,128]{2,1,0:T(8,128)(2,1)S(1)}, bf16[16,256,128]{2,1,0:T(8,128)(2,1)S(1)}, u32[]{:S(2)}, u32[]{:S(2)}) %collective-permute-start.2) | collective-permute-done | bytes 1048608 | tf_op jit(solution)/shard_map/ppermute | solution.py:362
  59.2 0.3 add_convert_fusion
  59.4 0.0 copy-start.1
  59.4 18.6 %all_to_all.27.parts_ref = bf16[16,256,128]{2,1,0:T(8,128)(2,1)S(1)} all-to-all(bf16[16,256,128]{2,1,0:T(8,128)(2,1)S(1)} %add_convert_fusion), channel_id=1, replica_groups=mesh['yl'=2,'z'=16,'chip'=8,'core'=2] {'yl','chip'}, dimensions={0} | all-to-all | bytes 2097152 | tf_op jit(solution)/shard_map/all_to_all | solution.py:363
  78.0 0.0 copy-done.1
  78.0 1.6 %owner_slots.1 = bf16[16,32,128]{2,1,0:T(8,128)(2,1)S(1)} custom-call(s32[1,64]{1,0:T(1,128)S(1)} %bitcast.9, bf16[16,256,128]{2,1,0:T(8,128)(2,1)S(1)} %all_to_all.27.parts_ref), custom_call_target="tpu_custom_call" | custom-call | tf_op jit(solution)/shard_map/owner_slots/pallas_call | solution.py:285
  79.6 26.7 %all_to_all.28.parts_ref = bf16[16,32,128]{2,1,0:T(8,128)(2,1)S(1)} all-to-all(bf16[16,32,128]{2,1,0:T(8,128)(2,1)S(1)} %owner_slots.1), channel_id=1, replica_groups=mesh['yl'=2,'z'=16,'chip'=8,'core'=2] {'z'}, dimensions={0} | all-to-all | bytes 262144 | tf_op jit(solution)/shard_map/all_to_all | solution.py:365
  106.4 15.5 %all_to_all.29.pieces_ref = bf16[32,16,128]{2,1,0:T(8,128)(2,1)S(1)} all-to-all(bf16[32,16,128]{2,1,0:T(8,128)(2,1)S(1)} %owned_sum.1), channel_id=1, replica_groups=mesh['yl'=2,'z'=16,'chip'=8,'core'=2] {'yl','chip','core'}, dimensions={0} | all-to-all | bytes 262144 | tf_op jit(solution)/shard_map/all_to_all | solution.py:366
  121.8 1.1 factors.1
  (1 shorter events, 0.0 us)
Async XLA Ops:
  17.6 6.8 %collective-permute-start = (bf16[8,128,256]{2,1,0:T(8,128)(2,1)S(1)}, bf16[8,128,256]{2,1,0:T(8,128)(2,1)S(1)}, u32[]{:S(2)}, u32[]{:S(2)}) collective-permute-start(bf16[8,128,256]{2,1,0:T(8,128)(2,1)S(1)} %all_to_all.25.mine_ref), channel_id=1, source_target_pairs={{0,1},{1,0},{2,3},{3,2},{4,5},{5,4},{6,7},{7,6},{8,9},{9,8},{10,11... | collective-permute-start | bytes 1572872 | tf_op jit(solution)/shard_map/ppermute | solution.py:357
  24.4 25.6 %copy-start = (bf16[1,128,8192]{2,1,0:T(8,128)(2,1)S(1)}, bf16[1,128,8192]{2,1,0:T(8,128)(2,1)}, u32[]{:S(2)}) copy-start(bf16[1,128,8192]{2,1,0:T(8,128)(2,1)} %param.6) | copy-start | bytes 6291460
  30.2 3.8 %collective-permute-start.1 = (bf16[8,128,256]{2,1,0:T(8,128)(2,1)S(1)}, bf16[8,128,256]{2,1,0:T(8,128)(2,1)S(1)}, u32[]{:S(2)}, u32[]{:S(2)}) collective-permute-start(bf16[8,128,256]{2,1,0:T(8,128)(2,1)S(1)} %get-tuple-element.11), channel_id=1, source_target_pairs={{0,1},{1,0},{2,3},{3,2},{4,5},{5,4},{6,7},{7,6},{8,9},{9,8},{10,11... | collective-permute-start | bytes 1572872 | tf_op jit(solution)/shard_map/ppermute | solution.py:359
  52.8 6.4 %collective-permute-start.2 = (bf16[16,256,128]{2,1,0:T(8,128)(2,1)S(1)}, bf16[16,256,128]{2,1,0:T(8,128)(2,1)S(1)}, u32[]{:S(2)}, u32[]{:S(2)}) collective-permute-start(bf16[16,256,128]{2,1,0:T(8,128)(2,1)S(1)} %get-tuple-element.14), channel_id=1, source_target_pairs={{0,1},{1,0},{2,3},{3,2},{4,5},{5,4},{6,7},{7,6},{8,9},{9,8},{10,11... | collective-permute-start | bytes 3145736 | tf_op jit(solution)/shard_map/ppermute | solution.py:362
  59.4 18.6 %copy-start.1 = (s32[64,1]{0,1:T(1,128)S(1)}, s32[64,1]{0,1:T(1,128)}, u32[]{:S(2)}) copy-start(s32[64,1]{0,1:T(1,128)} %param.11) | copy-start | bytes 772

commit v3 on v2

--- a/solution.py
+++ b/solution.py
@@ -33,7 +33,7 @@
 
 def attention_kernel(
     lengths_hbm, q_hbm, go_hbm, mine_ref, other_ref,
-    dq_ref, dmine_ref, dother_ref,
+    dq_ref, keep_ref, send_ref,
     lengths_ref, q_ref, go_ref, q_rows, go_rows, k_all, v_all,
     scores, prob_grads, ds_buf, w_buf, top, total, delta, dq_t, sems,
 ):
@@ -56,8 +56,8 @@
     total[...] = jnp.zeros(total.shape, F32)
     delta[...] = jnp.zeros(delta.shape, F32)
     dq_t[...] = jnp.zeros(dq_t.shape, F32)
-    dmine_ref[...] = jnp.zeros(dmine_ref.shape, dmine_ref.dtype)
-    dother_ref[...] = jnp.zeros(dother_ref.shape, dother_ref.dtype)
+    keep_ref[...] = jnp.zeros(keep_ref.shape, keep_ref.dtype)
+    send_ref[...] = jnp.zeros(send_ref.shape, send_ref.dtype)
     for copy in copies:
         copy.wait()
     for h in range(HEADS):
@@ -133,16 +133,17 @@
         for i in range(BLOCK // ROWS):
             here = slice(i * ROWS, (i + 1) * ROWS)
             pair = j * (BLOCK // (2 * ROWS)) + i // 2
+            at = pl.ds((i % 2) * ROWS, ROWS)
+            keep_ref[pair, at, :] = dk[here]
+            send_ref[pair, at, :] = dk[here].astype(BF16)
 
             @pl.when(core == i % 2)
             def _():
-                dmine_ref[pair, :, :HD] = dk[here]
-                dmine_ref[pair, :, HD:] = dv[here]
+                keep_ref[pair, 2 * ROWS :, :] = dv[here]
 
             @pl.when(core != i % 2)
             def _():
-                dother_ref[pair, :, :HD] = dk[here].astype(BF16)
-                dother_ref[pair, :, HD:] = dv[here].astype(BF16)
+                send_ref[pair, 2 * ROWS :, :] = dv[here].astype(BF16)
 
         return carry
 
@@ -170,8 +171,8 @@
         attention_kernel,
         out_shape=(
             jax.ShapeDtypeStruct((ROWS, wide), BF16),
-            jax.ShapeDtypeStruct((CHIPS, ROWS, 2 * HD), F32),
-            jax.ShapeDtypeStruct((CHIPS, ROWS, 2 * HD), BF16),
+            jax.ShapeDtypeStruct((CHIPS, 3 * ROWS, HD), F32),
+            jax.ShapeDtypeStruct((CHIPS, 3 * ROWS, HD), BF16),
         ),
         in_specs=[hbm, hbm, hbm, VMEM, VMEM],
         out_specs=(VMEM, VMEM, VMEM),
@@ -198,66 +199,57 @@
     )(in_hbm(lengths), in_hbm(query), in_hbm(grad_out), mine, other)
 
 
-STEP_TILES = 8
-
-
 def low_half(shape, axis):
     return lax.broadcasted_iota(jnp.int32, shape, axis) < 4
 
 
-def weight_kernel(parts_ref, hidden_ref, kv_ref, mine_ref, other_ref, k_t):
+def weight_kernel(parts_ref, own_ref, other_ref, kv_ref, out_ref, k_t):
     core = lax.axis_index("core")
-    shape = (PLANE, 8, TILE)
-
-    @pl.when(pl.program_id(0) == 0)
-    def _():
-        low = jnp.sum(parts_ref[...].astype(F32), axis=0).astype(BF16)
-        kv_ref[...] = low
-        key_t = low[:, :HD].astype(F32).T.reshape(shape)
-        key_t = jnp.where(core == 0, key_t, pltpu.roll(key_t, 4, axis=1))
-        k_t[...] = key_t.reshape(HD, ROWS).astype(BF16)
-
-    grad_t = jnp.dot(k_t[...], hidden_ref[...], preferred_element_type=F32)
-    low = low_half(shape, 1)
-
-    def pieces(pair):
-        even = grad_t[:, (2 * pair) * TILE : (2 * pair + 1) * TILE].reshape(shape)
-        odd = grad_t[:, (2 * pair + 1) * TILE : (2 * pair + 2) * TILE].reshape(shape)
+    sums = jnp.sum(parts_ref[...].astype(F32), axis=0).astype(BF16)
+    keys = sums[: 2 * ROWS].astype(F32)
+    first, second = keys[:ROWS], keys[ROWS:]
+    own_keys = jnp.where(core == 0, first, second)
+    other_keys = jnp.where(core == 0, second, first)
+    kv_ref[:, :HD] = own_keys.astype(BF16)
+    kv_ref[:, HD:] = sums[2 * ROWS :]
+    for i, side in enumerate((own_keys, other_keys)):
+        rows = side.T.reshape(PLANE // 2, 2, 8, ROWS)
+        even, odd = rows[:, 0], rows[:, 1]
+        low = low_half(even.shape, 1)
         here = jnp.where(low, even, pltpu.roll(odd, 4, axis=1))
         there = jnp.where(low, pltpu.roll(even, 4, axis=1), odd)
-        return here, there
-
-    for quad in range(STEP_TILES // 4):
-        first, second = pieces(2 * quad), pieces(2 * quad + 1)
+        mine = jnp.where(core == 0, here, there).reshape(HD // 2, ROWS)
+        k_t[:, i * ROWS : (i + 1) * ROWS] = mine.astype(BF16)
+    shape = (PLANE // 2, 8, TILE)
+    low = low_half(shape, 1)
+    for quad in range(TILES // 4):
+        cols = pl.ds(quad * 4 * TILE, 4 * TILE)
+        hidden = jnp.concatenate([own_ref[:, cols], other_ref[:, cols]], axis=0)
+        grad_t = jnp.dot(k_t[...], hidden, preferred_element_type=F32)
+        tiles = [grad_t[:, i * TILE : (i + 1) * TILE].reshape(shape) for i in range(4)]
+        evens, odds = [], []
+        for even, odd in (tiles[:2], tiles[2:]):
+            evens.append(jnp.where(low, even, pltpu.roll(odd, 4, axis=1)))
+            odds.append(jnp.where(low, pltpu.roll(even, 4, axis=1), odd))
         rows = pl.ds(quad * 16, 16)
-        mine_ref[:, rows, :] = jnp.concatenate([first[0], second[0]], axis=1)
-        other_ref[:, rows, :] = jnp.concatenate([first[1], second[1]], axis=1).astype(BF16)
-
-
-def weight_terms(parts, hidden):
-    steps = TILES // STEP_TILES
-    rows = STEP_TILES * 4
-    return pl.pallas_call(
+        out_ref[:, 0, rows, :] = jnp.concatenate(evens, axis=1).astype(BF16)
+        out_ref[:, 1, rows, :] = jnp.concatenate(odds, axis=1).astype(BF16)
+
+
+def weight_terms(parts, own, other):
+    grad_kv, terms = pl.pallas_call(
         weight_kernel,
-        grid=(steps,),
         out_shape=(
             jax.ShapeDtypeStruct((ROWS, 2 * HD), BF16),
-            jax.ShapeDtypeStruct((PLANE, TILES * 4, TILE), F32),
-            jax.ShapeDtypeStruct((PLANE, TILES * 4, TILE), BF16),
+            jax.ShapeDtypeStruct((PLANE // 2, 2, TILES * 4, TILE), BF16),
         ),
-        in_specs=[
-            pl.BlockSpec((CHIPS, ROWS, 2 * HD), lambda i: (0, 0, 0)),
-            pl.BlockSpec((ROWS, STEP_TILES * TILE), lambda i: (0, i)),
-        ],
-        out_specs=(
-            pl.BlockSpec((ROWS, 2 * HD), lambda i: (0, 0)),
-            pl.BlockSpec((PLANE, rows, TILE), lambda i: (0, i, 0)),
-            pl.BlockSpec((PLANE, rows, TILE), lambda i: (0, i, 0)),
-        ),
-        scratch_shapes=[pltpu.VMEM((HD, ROWS), BF16)],
+        in_specs=[VMEM, VMEM, VMEM],
+        out_specs=(VMEM, VMEM),
+        scratch_shapes=[pltpu.VMEM((HD // 2, 2 * ROWS), BF16)],
         compiler_params=limit(16),
         name="weight_gradient",
-    )(parts, hidden)
+    )(parts, own, other)
+    return grad_kv, terms.reshape(PLANE, TILES * 4, TILE)
 
 
 def owner_kernel(owner_ref, parts_ref, out_ref, sums, placed, held):
@@ -351,15 +343,16 @@
 
 
 def body(hidden_in, query, key_value, grad_out, lengths, owner):
+    hidden = hidden_in[0]
+    hidden_other = lax.ppermute(hidden, "core", SWAP)
     mine = lax.all_to_all(
         jnp.broadcast_to(key_value, (CHIPS, ROWS, 2 * HD)), "chip", 0, 0, tiled=True
     )
     other = lax.ppermute(mine, "core", SWAP)
-    grad_query, dkv_mine, dkv_other = attention(lengths, query[0], grad_out[0], mine, other)
-    dkv = (dkv_mine + lax.ppermute(dkv_other, "core", SWAP).astype(F32)).astype(BF16)
+    grad_query, keep, send = attention(lengths, query[0], grad_out[0], mine, other)
+    dkv = (keep + lax.ppermute(send, "core", SWAP).astype(F32)).astype(BF16)
     dkv = lax.all_to_all(dkv, "chip", 0, 0, tiled=True)
-    grad_kv, wg_mine, wg_other = weight_terms(dkv, hidden_in[0])
-    wg = (wg_mine + lax.ppermute(wg_other, "core", SWAP).astype(F32)).astype(BF16)
+    grad_kv, wg = weight_terms(dkv, hidden, hidden_other)
     wg = lax.all_to_all(wg, ("yl", "chip"), 0, 0, tiled=True)
     outgoing = to_owners(owner.reshape(1, TILES), wg)
     incoming = lax.all_to_all(outgoing, "z", 0, 0, tiled=True)

time: 123 us -> 123 us (level)
  blocking collectives: 92.8 us -> 77.8 us
  waiting for transfers between devices: 5.29 us -> 14.8 us
  starting transfers between devices: 11.7 us -> 15.7 us
    all_to_all x1 -> x0, blocking collectives: 15.9 us -> none  [body(): dkv = lax.all_to_all(dkv, 'chip', 0, 0, tiled=True)]
    all_to_all x0 -> x1, waiting for transfers between devices: none -> 13 us  [body(): dkv = lax.all_to_all(dkv, 'chip', 0, 0, tiled=True)]
    all_to_all x0 -> x1, starting transfers between devices: none -> 6.09 us  [body(): dkv = lax.all_to_all(dkv, 'chip', 0, 0, tiled=True)]
    ppermute x2, starting transfers between devices: 6.41 us -> 4.33 us  [the longest x1 2.4 us: body(): dkv = (keep + lax.ppermute(send, 'core', SWAP).astype(F32)).astype(BF16)]
    ppermute x2, waiting for transfers between devices: 3.78 us -> 1.89 us  [the longest x1 1.89 us: body(): dkv = (keep + lax.ppermute(send, 'core', SWAP).astype(F32)).astype(BF16)]
    ppermute x1, waiting for transfers between devices: 1.51 us -> 0.01 us  [body(): other = lax.ppermute(mine, 'core', SWAP)]
  transfers between devices with their start and end apart: 3 -> 4, of which waited for: 3 -> 2; matrix products, arithmetic and copies ran while one was open for 0% -> 1% of each run, Pallas kernels for 0% -> 5%
where the time goes in v3:
time: 123 us
  blocking collectives  77.8 us (63%)
  starting transfers between devices  15.7 us (13%)
  waiting for transfers between devices  14.8 us (12%)
  Pallas kernels  11.5 us (9%)
    all_to_all x1, blocking collectives, body(): incoming = lax.all_to_all(outgoing, 'z', 0, 0, tiled=True)  26.7 us
    all_to_all x1, blocking collectives, body(): wg = lax.all_to_all(wg, ('yl', 'chip'), 0, 0, tiled=True)  19.4 us
    all_to_all x1, blocking collectives, body(): lax.all_to_all(jnp.broadcast_to(key_value, (CHIPS, ROWS, 2 * HD)), 'chip'...  16.1 us
    all_to_all x1, blocking collectives, body(): lax.all_to_all(owned_sum(incoming), ('yl', 'chip', 'core'), 0, 0, tiled=T...  15.6 us
    all_to_all x1, waiting for transfers between devices, body(): dkv = lax.all_to_all(dkv, 'chip', 0, 0, tiled=True)  13 us
    all_to_all x1, starting transfers between devices, body(): dkv = lax.all_to_all(dkv, 'chip', 0, 0, tiled=True)  6.09 us
    pallas_call x1, Pallas kernels, attention(): pl.pallas_call(attention_kernel, out_shape=(jax.ShapeDtypeStruct((ROWS, w...  5.7 us
    ppermute x1, starting transfers between devices, body(): other = lax.ppermute(mine, 'core', SWAP)  5.25 us
  transfers between devices with their start and end apart: 4, of which 2 were waited for; matrix products, arithmetic and copies ran while one was open for 1% of the time, Pallas kernels for 5%

profile of v3, /device:TPU:1, one launch (start us, length us, event | category | flops | bytes accessed | tf_op | source)
XLA Modules:
  0.0 122.5 jit_solution(6247349443823636554)
XLA Ops:
  0.6 0.9 broadcast_in_dim.17
  1.5 16.1 %all_to_all.25.mine_ref = bf16[8,128,256]{2,1,0:T(8,128)(2,1)S(1)} all-to-all(bf16[8,128,256]{2,1,0:T(8,128)(2,1)S(1)} %broadcast_in_dim.17), channel_id=1, replica_groups=mesh['yl'=2,'z'=16,'chip'=8,'core'=2] {'chip'}, dimensions={0} | all-to-all | bytes 1048576 | tf_op jit(solution)/shard_map/all_to_all | solution.py:348
  17.6 5.3 %collective-permute-start = (bf16[8,128,256]{2,1,0:T(8,128)(2,1)S(1)}, bf16[8,128,256]{2,1,0:T(8,128)(2,1)S(1)}, u32[]{:S(2)}, u32[]{:S(2)}) collective-permute-start(bf16[8,128,256]{2,1,0:T(8,128)(2,1)S(1)} %all_to_all.25.mine_ref), channel_id=1, source_target_pairs={{0,1},{1,0},{2,3},{3,2},{4,5},{5,4},{6,7},{7,6},{8,9},{9,8},{10,11... | collective-permute-start | bytes 1572872 | tf_op jit(solution)/shard_map/ppermute | solution.py:351
  22.9 1.9 %collective-permute-start.2 = (bf16[128,8192]{1,0:T(8,128)(2,1)}, bf16[128,8192]{1,0:T(8,128)(2,1)}, u32[]{:S(2)}, u32[]{:S(2)}) collective-permute-start(bf16[128,8192]{1,0:T(8,128)(2,1)} %bitcast.9), channel_id=1, source_target_pairs={{0,1},{1,0},{2,3},{3,2},{4,5},{5,4},{6,7},{7,6},{8,9},{9,8},{10,11... | collective-permute-start | bytes 6291464 | tf_op jit(solution)/shard_map/ppermute | solution.py:347
  24.8 0.0 collective-permute-done.other_ref
  24.8 5.7 %attention_backward.1 = (bf16[128,1024]{1,0:T(8,128)(2,1)}, f32[8,384,128]{2,1,0:T(8,128)S(1)}, bf16[8,384,128]{2,1,0:T(8,128)(2,1)S(1)}) custom-call(s32[1,8]{1,0:T(1,128)} %lengths_hbm.1, bf16[128,1024]{1,0:T(8,128)(2,1)} %bitcast.14, bf16[128,1024]{1,0:T(8,128)(2,1)} %bitcast.15, bf16[8,128,256]{2,1,0:T(8,128)(2,1)S(1)} %all_to_all.25.mine_ref, ...), custom_call_target="tpu_custom_call" | custom-call | tf_op jit(solution)/shard_map/attention_backward/pallas_call | solution.py:170
  30.6 2.4 %collective-permute-start.1 = (bf16[8,384,128]{2,1,0:T(8,128)(2,1)S(1)}, bf16[8,384,128]{2,1,0:T(8,128)(2,1)S(1)}, u32[]{:S(2)}, u32[]{:S(2)}) collective-permute-start(bf16[8,384,128]{2,1,0:T(8,128)(2,1)S(1)} %get-tuple-element.10), channel_id=1, source_target_pairs={{0,1},{1,0},{2,3},{3,2},{4,5},{5,4},{6,7},{7,6},{8,9},{9,8},{10,11... | collective-permute-start | bytes 2359304 | tf_op jit(solution)/shard_map/ppermute | solution.py:353
  33.0 1.9 %collective-permute-done.1 = bf16[8,384,128]{2,1,0:T(8,128)(2,1)S(1)} collective-permute-done((bf16[8,384,128]{2,1,0:T(8,128)(2,1)S(1)}, bf16[8,384,128]{2,1,0:T(8,128)(2,1)S(1)}, u32[]{:S(2)}, u32[]{:S(2)}) %collective-permute-start.1) | collective-permute-done | bytes 786464 | tf_op jit(solution)/shard_map/ppermute | solution.py:353
  34.9 0.0 copy-start
  34.9 1.0 add_convert_fusion
  35.9 6.1 %all-to-all-start.1 = ((bf16[8,384,128]{2,1,0:T(8,128)(2,1)}), bf16[8,384,128]{2,1,0:T(8,128)(2,1)S(1)}, u32[]{:S(2)}, u32[]{:S(2)}) async-start(bf16[8,384,128]{2,1,0:T(8,128)(2,1)} %add_convert_fusion), calls=%async_computation.1 | async-start | bytes 1572864 | tf_op jit(solution)/shard_map/all_to_all | solution.py:354
  42.0 0.0 collective-permute-done.2.other_ref
  42.0 13.0 %all-to-all-done.1.parts_ref = bf16[8,384,128]{2,1,0:T(8,128)(2,1)S(1)} async-done(((bf16[8,384,128]{2,1,0:T(8,128)(2,1)}), bf16[8,384,128]{2,1,0:T(8,128)(2,1)S(1)}, u32[]{:S(2)}, u32[]{:S(2)}) %all-to-all-start.1) | async-done | bytes 786464 | tf_op jit(solution)/shard_map/all_to_all | solution.py:354
  54.9 0.0 copy-done
  54.9 3.2 %weight_gradient.1 = (bf16[128,256]{1,0:T(8,128)(2,1)}, bf16[8,2,256,128]{3,2,1,0:T(8,128)(2,1)S(1)}) custom-call(bf16[8,384,128]{2,1,0:T(8,128)(2,1)S(1)} %all-to-all-done.1.parts_ref, bf16[128,8192]{1,0:T(8,128)(2,1)S(1)} %bitcast.10, bf16[128,8192]{1,0:T(8,128)(2,1)} %collective-permute-done.2.other_ref), custom_call_target="tpu_custom_call" | custom-call | tf_op jit(solution)/shard_map/weight_gradient/pallas_call | solution.py:240
  58.1 0.0 copy-start.1
  58.1 19.4 %all_to_all.26.parts_ref = bf16[16,256,128]{2,1,0:T(8,128)(2,1)S(1)} all-to-all(bf16[16,256,128]{2,1,0:T(8,128)(2,1)S(1)} %bitcast.11), channel_id=1, replica_groups=mesh['yl'=2,'z'=16,'chip'=8,'core'=2] {'yl','chip'}, dimensions={0} | all-to-all | bytes 2097152 | tf_op jit(solution)/shard_map/all_to_all | solution.py:356
  77.5 0.0 copy-done.1
  77.5 1.6 %owner_slots.1 = bf16[16,32,128]{2,1,0:T(8,128)(2,1)S(1)} custom-call(s32[1,64]{1,0:T(1,128)S(1)} %bitcast.12, bf16[16,256,128]{2,1,0:T(8,128)(2,1)S(1)} %all_to_all.26.parts_ref), custom_call_target="tpu_custom_call" | custom-call | tf_op jit(solution)/shard_map/owner_slots/pallas_call | solution.py:277
  79.1 26.7 %all_to_all.27.parts_ref = bf16[16,32,128]{2,1,0:T(8,128)(2,1)S(1)} all-to-all(bf16[16,32,128]{2,1,0:T(8,128)(2,1)S(1)} %owner_slots.1), channel_id=1, replica_groups=mesh['yl'=2,'z'=16,'chip'=8,'core'=2] {'z'}, dimensions={0} | all-to-all | bytes 262144 | tf_op jit(solution)/shard_map/all_to_all | solution.py:358
  105.9 15.6 %all_to_all.28.pieces_ref = bf16[32,16,128]{2,1,0:T(8,128)(2,1)S(1)} all-to-all(bf16[32,16,128]{2,1,0:T(8,128)(2,1)S(1)} %owned_sum.1), channel_id=1, replica_groups=mesh['yl'=2,'z'=16,'chip'=8,'core'=2] {'yl','chip','core'}, dimensions={0} | all-to-all | bytes 262144 | tf_op jit(solution)/shard_map/all_to_all | solution.py:359
  121.4 1.1 factors.1
  (1 shorter events, 0.0 us)
Async XLA Ops:
  17.6 7.2 %collective-permute-start = (bf16[8,128,256]{2,1,0:T(8,128)(2,1)S(1)}, bf16[8,128,256]{2,1,0:T(8,128)(2,1)S(1)}, u32[]{:S(2)}, u32[]{:S(2)}) collective-permute-start(bf16[8,128,256]{2,1,0:T(8,128)(2,1)S(1)} %all_to_all.25.mine_ref), channel_id=1, source_target_pairs={{0,1},{1,0},{2,3},{3,2},{4,5},{5,4},{6,7},{7,6},{8,9},{9,8},{10,11... | collective-permute-start | bytes 1572872 | tf_op jit(solution)/shard_map/ppermute | solution.py:351
  22.9 19.1 %collective-permute-start.2 = (bf16[128,8192]{1,0:T(8,128)(2,1)}, bf16[128,8192]{1,0:T(8,128)(2,1)}, u32[]{:S(2)}, u32[]{:S(2)}) collective-permute-start(bf16[128,8192]{1,0:T(8,128)(2,1)} %bitcast.9), channel_id=1, source_target_pairs={{0,1},{1,0},{2,3},{3,2},{4,5},{5,4},{6,7},{7,6},{8,9},{9,8},{10,11... | collective-permute-start | bytes 6291464 | tf_op jit(solution)/shard_map/ppermute | solution.py:347
  30.6 4.3 %collective-permute-start.1 = (bf16[8,384,128]{2,1,0:T(8,128)(2,1)S(1)}, bf16[8,384,128]{2,1,0:T(8,128)(2,1)S(1)}, u32[]{:S(2)}, u32[]{:S(2)}) collective-permute-start(bf16[8,384,128]{2,1,0:T(8,128)(2,1)S(1)} %get-tuple-element.10), channel_id=1, source_target_pairs={{0,1},{1,0},{2,3},{3,2},{4,5},{5,4},{6,7},{7,6},{8,9},{9,8},{10,11... | collective-permute-start | bytes 2359304 | tf_op jit(solution)/shard_map/ppermute | solution.py:353
  34.9 20.1 %copy-start = (bf16[1,128,8192]{2,1,0:T(8,128)(2,1)S(1)}, bf16[1,128,8192]{2,1,0:T(8,128)(2,1)}, u32[]{:S(2)}) copy-start(bf16[1,128,8192]{2,1,0:T(8,128)(2,1)} %param.6) | copy-start | bytes 6291460
  35.9 19.1 %all-to-all-start.1 = ((bf16[8,384,128]{2,1,0:T(8,128)(2,1)}), bf16[8,384,128]{2,1,0:T(8,128)(2,1)S(1)}, u32[]{:S(2)}, u32[]{:S(2)}) async-start(bf16[8,384,128]{2,1,0:T(8,128)(2,1)} %add_convert_fusion), calls=%async_computation.1 | async-start | bytes 1572864 | tf_op jit(solution)/shard_map/all_to_all | solution.py:354
  58.1 19.4 %copy-start.1 = (s32[64,1]{0,1:T(1,128)S(1)}, s32[64,1]{0,1:T(1,128)}, u32[]{:S(2)}) copy-start(s32[64,1]{0,1:T(1,128)} %param.11) | copy-start | bytes 772

commit v4 on v3

v4 whole, which is shorter than its diff:
```python
import math

import jax
import jax.numpy as jnp
from jax import lax
from jax.experimental import pallas as pl
from jax.experimental.pallas import tpu as pltpu
from jax.sharding import Mesh
from jax.sharding import PartitionSpec as P

HEADS = 8
HD = 128
TILE = 128
ROWS = 128
CHIPS = 8
SEQ = 2048
TILES = 64
CAP = 4
N_DP = 32
MODEL = 8192
N_YL = 2
N_Z = 16
PLANE = N_YL * CHIPS
OWNED = N_YL * CAP * 4
GROUP = 2
HIDDEN_NEG = -1e30
SCALE = 1.0 / math.sqrt(HD)
EXP2_SCALE = SCALE * math.log2(math.e)
F32 = jnp.float32
BF16 = jnp.bfloat16


def prepare_kernel(
    lengths_hbm, q_hbm, go_hbm, q_rows, go_rows, low_ref, lengths_ref, q_ref, go_ref, sems
):
    copies = [
        pltpu.make_async_copy(lengths_hbm, lengths_ref, sems.at[0]),
        pltpu.make_async_copy(q_hbm, q_ref, sems.at[1]),
        pltpu.make_async_copy(go_hbm, go_ref, sems.at[2]),
    ]
    for copy in copies:
        copy.start()
    first = (2 * lax.axis_index("chip") + lax.axis_index("core")) * ROWS
    row_pos = first + lax.broadcasted_iota(jnp.int32, low_ref.shape, 1)
    row_low = jnp.zeros(low_ref.shape, jnp.int32)
    end = jnp.int32(0)
    copies[0].wait()
    for d in range(lengths_ref.shape[1]):
        end = end + lengths_ref[0, d]
        row_low = jnp.maximum(row_low, jnp.where(row_pos >= end, end, 0))
    low_ref[...] = row_low
    for copy, rows, ref in ((copies[1], q_rows, q_ref), (copies[2], go_rows, go_ref)):
        copy.wait()
        for h in range(HEADS):
            cols = pl.ds(h * HD, HD)
            rows[cols, :] = ref[:, cols]


def attention_kernel(
    q_rows, go_rows, low_ref, mine_ref, other_ref,
    dq_t, keep_ref, send_ref,
    k_all, v_all, scores, prob_grads, ds_buf, w_buf, top, total, delta,
):
    chip = lax.axis_index("chip")
    core = lax.axis_index("core")
    first = (2 * chip + core) * ROWS
    for ref, side in ((mine_ref, core), (other_ref, 1 - core)):
        for j in range(CHIPS):
            rows = pl.ds(pl.multiple_of((2 * j + side) * ROWS, ROWS), ROWS)
            k_all[rows, :] = ref[j, :, :HD]
            v_all[rows, :] = ref[j, :, HD:]
    row_pos = first + lax.broadcasted_iota(jnp.int32, (1, ROWS), 1)
    row_low = low_ref[0:1, :]

    def fold(values, op):
        return op(values.reshape(values.shape[0] // 8, 8, values.shape[1]), axis=0)

    def against(rows, ref, cols):
        return lax.dot_general(
            rows, ref[cols, :], (((1,), (1,)), ((), ())), preferred_element_type=F32
        )

    pos = lax.broadcasted_iota(jnp.int32, (SEQ, ROWS), 0)
    seen = (pos >= row_low) & (pos <= row_pos)
    seen = jnp.concatenate([seen] * GROUP, axis=1)
    keys = k_all[...]
    groups = [pl.ds(g * GROUP * HD, GROUP * HD) for g in range(HEADS // GROUP)]
    for cols in groups:
        s = jnp.where(seen, against(keys, q_rows, cols), HIDDEN_NEG)
        scores[:, cols] = s
        top[:, cols] = fold(s, jnp.max)
    top[0:1, :] = jnp.max(top[...], axis=0, keepdims=True)
    values = v_all[...]
    for cols in groups:
        pg = against(values, go_rows, cols)
        p = jnp.exp2((scores[:, cols] - top[0:1, cols]) * EXP2_SCALE)
        scores[:, cols] = p
        prob_grads[:, cols] = pg
        total[:, cols] = fold(p, jnp.sum)
        delta[:, cols] = fold(p * pg, jnp.sum)
    inverse = 1.0 / jnp.sum(total[...], axis=0, keepdims=True)
    total[0:1, :] = inverse
    delta[0:1, :] = jnp.sum(delta[...], axis=0, keepdims=True) * inverse
    for cols in groups:
        w = scores[:, cols] * total[0:1, cols]
        w_buf[:, cols] = w.astype(BF16)
        ds_buf[:, cols] = (w * (prob_grads[:, cols] - delta[0:1, cols])).astype(BF16)
    ds = ds_buf[...]
    dk = jnp.dot(ds, q_rows[...], preferred_element_type=F32) * SCALE
    dv = jnp.dot(w_buf[...], go_rows[...], preferred_element_type=F32)
    dq_t[...] = lax.dot_general(
        keys, ds, (((0,), (0,)), ((), ())), preferred_element_type=F32
    )
    for pair in range(CHIPS):
        for cols, grads in ((slice(0, HD), dk), (slice(HD, 2 * HD), dv)):
            even = grads[2 * pair * ROWS : (2 * pair + 1) * ROWS]
            odd = grads[(2 * pair + 1) * ROWS : (2 * pair + 2) * ROWS]
            keep_ref[pair, :, cols] = jnp.where(core == 0, even, odd)
            send_ref[pair, :, cols] = jnp.where(core == 0, odd, even).astype(BF16)


def query_kernel(dq_t, dq_ref):
    for h in range(HEADS):
        cols = pl.ds(h * HD, HD)
        dq_ref[:, cols] = (dq_t[:, cols].T * SCALE).astype(BF16)


VMEM = pl.BlockSpec(memory_space=pltpu.VMEM)


def in_hbm(x):
    return pltpu.with_memory_space_constraint(x, pltpu.HBM)


def limit(mib):
    return pltpu.CompilerParams(vmem_limit_bytes=mib * 1024 * 1024)


def prepare(lengths, query, grad_out):
    hbm = pl.BlockSpec(memory_space=pltpu.HBM)
    wide = HEADS * HD
    return pl.pallas_call(
        prepare_kernel,
        out_shape=(
            jax.ShapeDtypeStruct((wide, HD), BF16),
            jax.ShapeDtypeStruct((wide, HD), BF16),
            jax.ShapeDtypeStruct((8, ROWS), jnp.int32),
        ),
        in_specs=[hbm, hbm, hbm],
        out_specs=(VMEM, VMEM, VMEM),
        scratch_shapes=[
            pltpu.SMEM((1, 8), jnp.int32),
            pltpu.VMEM((ROWS, wide), BF16),
            pltpu.VMEM((ROWS, wide), BF16),
            pltpu.SemaphoreType.DMA((3,)),
        ],
        compiler_params=limit(8),
        name="prepare_rows",
    )(in_hbm(lengths), in_hbm(query), in_hbm(grad_out))


def attention(q_rows, go_rows, row_low, mine, other):
    wide = HEADS * HD
    return pl.pallas_call(
        attention_kernel,
        out_shape=(
            jax.ShapeDtypeStruct((HD, wide), F32),
            jax.ShapeDtypeStruct((CHIPS, ROWS, 2 * HD), F32),
            jax.ShapeDtypeStruct((CHIPS, ROWS, 2 * HD), BF16),
        ),
        in_specs=[VMEM] * 5,
        out_specs=(VMEM, VMEM, VMEM),
        scratch_shapes=[
            pltpu.VMEM((SEQ, HD), BF16),
            pltpu.VMEM((SEQ, HD), BF16),
            pltpu.VMEM((SEQ, wide), F32),
            pltpu.VMEM((SEQ, wide), F32),
            pltpu.VMEM((SEQ, wide), BF16),
            pltpu.VMEM((SEQ, wide), BF16),
            pltpu.VMEM((8, wide), F32),
            pltpu.VMEM((8, wide), F32),
            pltpu.VMEM((8, wide), F32),
        ],
        compiler_params=limit(36),
        name="attention_backward",
    )(q_rows, go_rows, row_low, mine, other)


def query_gradient(dq_t):
    return pl.pallas_call(
        query_kernel,
        out_shape=jax.ShapeDtypeStruct((ROWS, HEADS * HD), BF16),
        in_specs=[VMEM],
        out_specs=VMEM,
        compiler_params=limit(8),
        name="query_gradient",
    )(dq_t)


def low_half(shape, axis):
    return lax.broadcasted_iota(jnp.int32, shape, axis) < 4


def halves(keys):
    rows = keys.T.reshape(PLANE // 2, 2, 8, ROWS)
    even, odd = rows[:, 0], rows[:, 1]
    low = low_half(even.shape, 1)
    first = jnp.where(low, even, pltpu.roll(odd, 4, axis=1))
    second = jnp.where(low, pltpu.roll(even, 4, axis=1), odd)
    return first.reshape(HD // 2, ROWS), second.reshape(HD // 2, ROWS)


def half_tiles(k_t, hidden_ref, out_ref):
    shape = (PLANE // 2, 8, TILE)
    low = low_half(shape, 1)
    for quad in range(TILES // 4):
        hidden = hidden_ref[:, pl.ds(quad * 4 * TILE, 4 * TILE)]
        grad_t = jnp.dot(k_t, hidden, preferred_element_type=F32)
        tiles = [grad_t[:, i * TILE : (i + 1) * TILE].reshape(shape) for i in range(4)]
        evens, odds = [], []
        for even, odd in (tiles[:2], tiles[2:]):
            evens.append(jnp.where(low, even, pltpu.roll(odd, 4, axis=1)))
            odds.append(jnp.where(low, pltpu.roll(even, 4, axis=1), odd))
        rows = pl.ds(quad * 16, 16)
        out_ref[:, 0, rows, :] = jnp.concatenate(evens, axis=1).astype(out_ref.dtype)
        out_ref[:, 1, rows, :] = jnp.concatenate(odds, axis=1).astype(out_ref.dtype)


def weight_send_kernel(parts_ref, hidden_ref, kv_ref, k_ref, out_ref):
    core = lax.axis_index("core")
    low = jnp.sum(parts_ref[...].astype(F32), axis=0).astype(BF16)
    kv_ref[...] = low
    first, second = halves(low[:, :HD].astype(F32))
    k_ref[...] = jnp.where(core == 0, first, second).astype(BF16)
    half_tiles(jnp.where(core == 0, second, first).astype(BF16), hidden_ref, out_ref)


def weight_keep_kernel(k_ref, hidden_ref, out_ref):
    half_tiles(k_ref[...], hidden_ref, out_ref)


def weight_send(parts, hidden):
    return pl.pallas_call(
        weight_send_kernel,
        out_shape=(
            jax.ShapeDtypeStruct((ROWS, 2 * HD), BF16),
            jax.ShapeDtypeStruct((HD // 2, ROWS), BF16),
            jax.ShapeDtypeStruct((PLANE // 2, 2, TILES * 4, TILE), BF16),
        ),
        in_specs=[VMEM, VMEM],
        out_specs=(VMEM, VMEM, VMEM),
        compiler_params=limit(10),
        name="weight_tiles_to_send",
    )(parts, hidden)


def weight_keep(k_t, hidden):
    return pl.pallas_call(
        weight_keep_kernel,
        out_shape=jax.ShapeDtypeStruct((PLANE // 2, 2, TILES * 4, TILE), F32),
        in_specs=[VMEM, VMEM],
        out_specs=VMEM,
        compiler_params=limit(10),
        name="weight_tiles_to_keep",
    )(k_t, hidden)


def owner_kernel(owner_ref, parts_ref, out_ref, sums, placed, held):
    rows = TILES * 4
    own = jnp.sum(parts_ref[...].astype(F32), axis=0)
    sums[:rows, :] = own
    sums[rows:, :] = pltpu.roll(own.reshape(rows // 8, 8, TILE), 4, axis=1).reshape(rows, TILE)
    placed[...] = jnp.zeros(placed.shape, F32)
    for o in range(N_DP):
        held[o] = 0
    low = low_half((8, TILE), 0)
    for t in range(TILES):
        o = owner_ref[0, t]
        slot = held[o]
        held[o] = slot + 1
        half = slot & 1
        block = ((o & (N_Z - 1)) * N_YL + o // N_Z) * (CAP // 2) + slot // 2
        at = pl.ds(pl.multiple_of(block * 8, 8), 8)
        source = pl.multiple_of((half ^ (t & 1)) * rows + (t // 2) * 8, 8)
        placed[at, :] = jnp.where(low == (half == 0), sums[pl.ds(source, 8), :], placed[at, :])
    out_ref[...] = placed[...].astype(BF16).reshape(out_ref.shape)


def to_owners(owner, parts):
    return pl.pallas_call(
        owner_kernel,
        out_shape=jax.ShapeDtypeStruct((N_Z, OWNED, TILE), BF16),
        in_specs=[pl.BlockSpec(memory_space=pltpu.SMEM), VMEM],
        out_specs=VMEM,
        scratch_shapes=[
            pltpu.VMEM((2 * TILES * 4, TILE), F32),
            pltpu.VMEM((N_Z * OWNED, TILE), F32),
            pltpu.SMEM((N_DP,), jnp.int32),
        ],
        compiler_params=limit(12),
        name="owner_slots",
    )(owner, parts)


def sum_kernel(parts_ref, out_ref):
    gradient = jnp.sum(parts_ref[...].astype(F32), axis=0) * (1.0 / math.sqrt(N_DP * SEQ))
    gradient = gradient.astype(BF16)
    rows = OWNED // N_YL
    for yl in range(N_YL):
        piece = gradient[yl * rows : (yl + 1) * rows]
        out_ref[yl * PLANE : (yl + 1) * PLANE] = jnp.broadcast_to(piece[None], (PLANE, rows, TILE))


def owned_sum(parts):
    return pl.pallas_call(
        sum_kernel,
        out_shape=jax.ShapeDtypeStruct((2 * PLANE, OWNED // N_YL, TILE), BF16),
        in_specs=[VMEM],
        out_specs=VMEM,
        compiler_params=limit(8),
        name="owned_sum",
    )(parts)


def factor_kernel(pieces_ref, out_ref):
    pieces = pieces_ref[...].astype(F32)
    low = low_half((PLANE, 8, TILE), 1)
    for two in range(CAP // 2):
        pair = pieces[:, two * 8 : (two + 1) * 8, :].reshape(PLANE, 2, 8, TILE)
        even, odd = pair[:, 0], pair[:, 1]
        both = (
            jnp.where(low, even, pltpu.roll(odd, 4, axis=1)),
            jnp.where(low, pltpu.roll(even, 4, axis=1), odd),
        )
        for i in range(2):
            grad_t = both[i].reshape(TILE, TILE)
            flat = grad_t.astype(BF16)
            flat_t = grad_t.T.astype(BF16)
            s = 2 * two + i
            out_ref[s, 0] = jnp.dot(flat_t, flat, preferred_element_type=F32) * (1.0 / TILE)
            out_ref[s, 1] = jnp.dot(flat, flat_t, preferred_element_type=F32) * (1.0 / TILE)


def factors_of(pieces):
    return pl.pallas_call(
        factor_kernel,
        out_shape=jax.ShapeDtypeStruct((CAP, 2, TILE, TILE), F32),
        in_specs=[VMEM],
        out_specs=VMEM,
        compiler_params=limit(8),
        name="factors",
    )(pieces)


SWAP = ((0, 1), (1, 0))


def body(hidden_in, query, key_value, grad_out, lengths, owner):
    mine = lax.all_to_all(
        jnp.broadcast_to(key_value, (CHIPS, ROWS, 2 * HD)), "chip", 0, 0, tiled=True
    )
    other = lax.ppermute(mine, "core", SWAP)
    q_rows, go_rows, row_low = prepare(lengths, query[0], grad_out[0])
    dq_t, keep, send = attention(q_rows, go_rows, row_low, mine, other)
    dkv = (keep + lax.ppermute(send, "core", SWAP).astype(F32)).astype(BF16)
    grad_query = query_gradient(dq_t)
    dkv = lax.all_to_all(dkv, "chip", 0, 0, tiled=True)
    hidden = hidden_in[0]
    grad_kv, k_t, send = weight_send(dkv, hidden)
    arrived = lax.ppermute(send, "core", SWAP)
    keep = weight_keep(k_t, hidden)
    wg = (keep + arrived.astype(F32)).astype(BF16).reshape(PLANE, TILES * 4, TILE)
    wg = lax.all_to_all(wg, ("yl", "chip"), 0, 0, tiled=True)
    outgoing = to_owners(owner.reshape(1, TILES), wg)
    incoming = lax.all_to_all(outgoing, "z", 0, 0, tiled=True)
    pieces = lax.all_to_all(owned_sum(incoming), ("yl", "chip", "core"), 0, 0, tiled=True)
    return grad_query[None], grad_kv[None], factors_of(pieces)[None]


def solution(mesh):
    fine = Mesh(mesh.devices.reshape(N_YL, N_Z, CHIPS, 2), ("yl", "z", "chip", "core"))
    dp, ctx = ("yl", "z"), ("chip", "core")
    split = P(dp, ctx, None)
    return jax.shard_map(
        body,
        mesh=fine,
        in_specs=(split, split, split, split, P(dp, None), P()),
        out_specs=(split, split, P(dp, None, None, None, None)),
        check_vma=False,
    )
```

time: 123 us -> 122 us (level)
  waiting for transfers between devices: 14.8 us -> 10.4 us
  Pallas kernels: 11.5 us -> 15.5 us
  starting transfers between devices: 15.7 us -> 19.7 us
  blocking collectives: 77.8 us -> 74.1 us
    all_to_all x1, waiting for transfers between devices: 13 us -> 6.64 us  [body(): lax.all_to_all(owned_sum(incoming), ('yl', 'chip', 'core'), 0, 0, tiled=T...]
    pallas_call x2 -> x5, Pallas kernels: 8.86 us -> 12.1 us  [the longest x1 8.88 us: attention(): pl.pallas_call(attention_kernel, out_shape=(jax.ShapeDtypeStruct((HD, wid...]
    all_to_all x1, blocking collectives: 15.6 us -> 12.6 us  [body(): dkv = lax.all_to_all(dkv, 'chip', 0, 0, tiled=True)]
    ppermute x1, starting transfers between devices: 1.92 us -> 4.07 us  [body(): arrived = lax.ppermute(send, 'core', SWAP)]
    all_to_all x1, starting transfers between devices: 6.09 us -> 8.11 us  [body(): lax.all_to_all(owned_sum(incoming), ('yl', 'chip', 'core'), 0, 0, tiled=T...]
    ppermute x1, waiting for transfers between devices: 0.01 us -> 1.82 us  [body(): arrived = lax.ppermute(send, 'core', SWAP)]
  transfers between devices with their start and end apart: 4 -> 4, of which waited for: 2 -> 4; matrix products, arithmetic and copies ran while one was open for 1% -> 0% of each run, Pallas kernels for 5% -> 2%
where the time goes in v4:
time: 122 us
  blocking collectives  74.1 us (61%)
  starting transfers between devices  19.7 us (16%)
  Pallas kernels  15.5 us (13%)
  waiting for transfers between devices  10.4 us (9%)
    all_to_all x1, blocking collectives, body(): incoming = lax.all_to_all(outgoing, 'z', 0, 0, tiled=True)  26.7 us
    all_to_all x1, blocking collectives, body(): wg = lax.all_to_all(wg, ('yl', 'chip'), 0, 0, tiled=True)  18.6 us
    all_to_all x1, blocking collectives, body(): lax.all_to_all(jnp.broadcast_to(key_value, (CHIPS, ROWS, 2 * HD)), 'chip'...  16.1 us
    all_to_all x1, blocking collectives, body(): dkv = lax.all_to_all(dkv, 'chip', 0, 0, tiled=True)  12.6 us
    pallas_call x1, Pallas kernels, attention(): pl.pallas_call(attention_kernel, out_shape=(jax.ShapeDtypeStruct((HD, wid...  8.88 us
    all_to_all x1, starting transfers between devices, body(): lax.all_to_all(owned_sum(incoming), ('yl', 'chip', 'core'), 0, 0, tiled=T...  8.11 us
    all_to_all x1, waiting for transfers between devices, body(): lax.all_to_all(owned_sum(incoming), ('yl', 'chip', 'core'), 0, 0, tiled=T...  6.64 us
    ppermute x1, starting transfers between devices, body(): other = lax.ppermute(mine, 'core', SWAP)  5.25 us
  transfers between devices with their start and end apart: 4, of which 4 were waited for; matrix products, arithmetic and copies ran while one was open for 0% of the time, Pallas kernels for 2%

profile of v4, /device:TPU:1, one launch (start us, length us, event | category | flops | bytes accessed | tf_op | source)
XLA Modules:
  0.0 121.6 jit_solution(4872909691954180355)
XLA Ops:
  0.6 0.9 broadcast_in_dim.17
  1.5 16.1 %all_to_all.25.mine_ref = bf16[8,128,256]{2,1,0:T(8,128)(2,1)S(1)} all-to-all(bf16[8,128,256]{2,1,0:T(8,128)(2,1)S(1)} %broadcast_in_dim.17), channel_id=1, replica_groups=mesh['yl'=2,'z'=16,'chip'=8,'core'=2] {'chip'}, dimensions={0} | all-to-all | bytes 1048576 | tf_op jit(solution)/shard_map/all_to_all | solution.py:359
  17.6 5.3 %collective-permute-start = (bf16[8,128,256]{2,1,0:T(8,128)(2,1)S(1)}, bf16[8,128,256]{2,1,0:T(8,128)(2,1)S(1)}, u32[]{:S(2)}, u32[]{:S(2)}) collective-permute-start(bf16[8,128,256]{2,1,0:T(8,128)(2,1)S(1)} %all_to_all.25.mine_ref), channel_id=1, source_target_pairs={{0,1},{1,0},{2,3},{3,2},{4,5},{5,4},{6,7},{7,6},{8,9},{9,8},{10,11... | collective-permute-start | bytes 1572872 | tf_op jit(solution)/shard_map/ppermute | solution.py:362
  22.9 1.1 prepare_rows.1
  24.0 0.4 collective-permute-done.other_ref
  24.4 8.9 %attention_backward.1 = (f32[128,1024]{1,0:T(8,128)S(1)}, f32[8,128,256]{2,1,0:T(8,128)S(1)}, bf16[8,128,256]{2,1,0:T(8,128)(2,1)S(1)}) custom-call(bf16[1024,128]{1,0:T(8,128)(2,1)S(1)} %get-tuple-element.12.q_rows, bf16[1024,128]{1,0:T(8,128)(2,1)S(1)} %get-tuple-element.13.go_rows, s32[8,128]{1,0:T(8,128)S(1)} %get-tuple-element.14.low_ref, ...), custom_call_target="tpu_custom_call" | custom-call | tf_op jit(solution)/shard_map/attention_backward/pallas_call | solution.py:164
  33.3 2.2 %collective-permute-start.1 = (bf16[8,128,256]{2,1,0:T(8,128)(2,1)S(1)}, bf16[8,128,256]{2,1,0:T(8,128)(2,1)S(1)}, u32[]{:S(2)}, u32[]{:S(2)}) collective-permute-start(bf16[8,128,256]{2,1,0:T(8,128)(2,1)S(1)} %get-tuple-element.17), channel_id=1, source_target_pairs={{0,1},{1,0},{2,3},{3,2},{4,5},{5,4},{6,7},{7,6},{8,9},{9,8},{10,11... | collective-permute-start | bytes 1572872 | tf_op jit(solution)/shard_map/ppermute | solution.py:365
  35.6 1.6 %collective-permute-done.1 = bf16[8,128,256]{2,1,0:T(8,128)(2,1)S(1)} collective-permute-done((bf16[8,128,256]{2,1,0:T(8,128)(2,1)S(1)}, bf16[8,128,256]{2,1,0:T(8,128)(2,1)S(1)}, u32[]{:S(2)}, u32[]{:S(2)}) %collective-permute-start.1) | collective-permute-done | bytes 524320 | tf_op jit(solution)/shard_map/ppermute | solution.py:365
  37.1 0.1 add_convert_fusion.1
  37.2 12.6 %all_to_all.26.parts_ref = bf16[8,128,256]{2,1,0:T(8,128)(2,1)S(1)} all-to-all(bf16[8,128,256]{2,1,0:T(8,128)(2,1)S(1)} %add_convert_fusion.1), channel_id=1, replica_groups=mesh['yl'=2,'z'=16,'chip'=8,'core'=2] {'chip'}, dimensions={0} | all-to-all | bytes 1048576 | tf_op jit(solution)/shard_map/all_to_all | solution.py:367
  49.9 0.8 weight_tiles_to_send.1
  50.6 4.1 %collective-permute-start.2 = (bf16[8,2,256,128]{3,2,1,0:T(8,128)(2,1)S(1)}, bf16[8,2,256,128]{3,2,1,0:T(8,128)(2,1)S(1)}, u32[]{:S(2)}, u32[]{:S(2)}) collective-permute-start(bf16[8,2,256,128]{3,2,1,0:T(8,128)(2,1)S(1)} %get-tuple-element.20), channel_id=1, source_target_pairs={{0,1},{1,0},{2,3},{3,2},{4,5},{5,4},{6,7},{7,6},{8,9},{9,8},{10,11... | collective-permute-start | bytes 3145736 | tf_op jit(solution)/shard_map/ppermute | solution.py:370
  54.7 0.4 weight_tiles_to_keep.1
  55.2 1.8 %collective-permute-done.2 = bf16[8,2,256,128]{3,2,1,0:T(8,128)(2,1)S(1)} collective-permute-done((bf16[8,2,256,128]{3,2,1,0:T(8,128)(2,1)S(1)}, bf16[8,2,256,128]{3,2,1,0:T(8,128)(2,1)S(1)}, u32[]{:S(2)}, u32[]{:S(2)}) %collective-permute-start.2) | collective-permute-done | bytes 1048608 | tf_op jit(solution)/shard_map/ppermute | solution.py:370
  57.0 0.3 add_convert_fusion
  57.2 0.0 copy-start.1
  57.3 18.6 %all_to_all.27.parts_ref = bf16[16,256,128]{2,1,0:T(8,128)(2,1)S(1)} all-to-all(bf16[16,256,128]{2,1,0:T(8,128)(2,1)S(1)} %bitcast.12), channel_id=1, replica_groups=mesh['yl'=2,'z'=16,'chip'=8,'core'=2] {'yl','chip'}, dimensions={0} | all-to-all | bytes 2097152 | tf_op jit(solution)/shard_map/all_to_all | solution.py:373
  75.9 1.6 %owner_slots.1 = bf16[16,32,128]{2,1,0:T(8,128)(2,1)S(1)} custom-call(s32[1,64]{1,0:T(1,128)S(1)} %bitcast.11, bf16[16,256,128]{2,1,0:T(8,128)(2,1)S(1)} %all_to_all.27.parts_ref), custom_call_target="tpu_custom_call" | custom-call | tf_op jit(solution)/shard_map/owner_slots/pallas_call | solution.py:290
  77.4 26.7 %all_to_all.28.parts_ref = bf16[16,32,128]{2,1,0:T(8,128)(2,1)S(1)} all-to-all(bf16[16,32,128]{2,1,0:T(8,128)(2,1)S(1)} %owner_slots.1), channel_id=1, replica_groups=mesh['yl'=2,'z'=16,'chip'=8,'core'=2] {'z'}, dimensions={0} | all-to-all | bytes 262144 | tf_op jit(solution)/shard_map/all_to_all | solution.py:375
  104.2 0.7 owned_sum.1
  104.9 8.1 %all-to-all-start.4 = ((bf16[32,16,128]{2,1,0:T(8,128)(2,1)}), bf16[32,16,128]{2,1,0:T(8,128)(2,1)S(1)}, u32[]{:S(2)}, u32[]{:S(2)}) async-start(bf16[32,16,128]{2,1,0:T(8,128)(2,1)} %owned_sum.1), calls=%async_computation.4 | async-start | bytes 262144 | tf_op jit(solution)/shard_map/all_to_all | solution.py:376
  113.0 0.9 query_gradient.1
  113.9 6.6 %all-to-all-done.4.pieces_ref = bf16[32,16,128]{2,1,0:T(8,128)(2,1)S(1)} async-done(((bf16[32,16,128]{2,1,0:T(8,128)(2,1)}), bf16[32,16,128]{2,1,0:T(8,128)(2,1)S(1)}, u32[]{:S(2)}, u32[]{:S(2)}) %all-to-all-start.4) | async-done | bytes 131104 | tf_op jit(solution)/shard_map/all_to_all | solution.py:376
  120.5 1.1 factors.1
  (3 shorter events, 0.0 us)
Async XLA Ops:
  17.6 6.8 %collective-permute-start = (bf16[8,128,256]{2,1,0:T(8,128)(2,1)S(1)}, bf16[8,128,256]{2,1,0:T(8,128)(2,1)S(1)}, u32[]{:S(2)}, u32[]{:S(2)}) collective-permute-start(bf16[8,128,256]{2,1,0:T(8,128)(2,1)S(1)} %all_to_all.25.mine_ref), channel_id=1, source_target_pairs={{0,1},{1,0},{2,3},{3,2},{4,5},{5,4},{6,7},{7,6},{8,9},{9,8},{10,11... | collective-permute-start | bytes 1572872 | tf_op jit(solution)/shard_map/ppermute | solution.py:362
  24.4 25.4 %copy-start = (bf16[1,128,8192]{2,1,0:T(8,128)(2,1)S(1)}, bf16[1,128,8192]{2,1,0:T(8,128)(2,1)}, u32[]{:S(2)}) copy-start(bf16[1,128,8192]{2,1,0:T(8,128)(2,1)} %param.6) | copy-start | bytes 6291460
  33.3 3.8 %collective-permute-start.1 = (bf16[8,128,256]{2,1,0:T(8,128)(2,1)S(1)}, bf16[8,128,256]{2,1,0:T(8,128)(2,1)S(1)}, u32[]{:S(2)}, u32[]{:S(2)}) collective-permute-start(bf16[8,128,256]{2,1,0:T(8,128)(2,1)S(1)} %get-tuple-element.17), channel_id=1, source_target_pairs={{0,1},{1,0},{2,3},{3,2},{4,5},{5,4},{6,7},{7,6},{8,9},{9,8},{10,11... | collective-permute-start | bytes 1572872 | tf_op jit(solution)/shard_map/ppermute | solution.py:365
  50.6 6.3 %collective-permute-start.2 = (bf16[8,2,256,128]{3,2,1,0:T(8,128)(2,1)S(1)}, bf16[8,2,256,128]{3,2,1,0:T(8,128)(2,1)S(1)}, u32[]{:S(2)}, u32[]{:S(2)}) collective-permute-start(bf16[8,2,256,128]{3,2,1,0:T(8,128)(2,1)S(1)} %get-tuple-element.20), channel_id=1, source_target_pairs={{0,1},{1,0},{2,3},{3,2},{4,5},{5,4},{6,7},{7,6},{8,9},{9,8},{10,11... | collective-permute-start | bytes 3145736 | tf_op jit(solution)/shard_map/ppermute | solution.py:370
  57.2 18.6 %copy-start.1 = (s32[64,1]{0,1:T(1,128)S(1)}, s32[64,1]{0,1:T(1,128)}, u32[]{:S(2)}) copy-start(s32[64,1]{0,1:T(1,128)} %param.11) | copy-start | bytes 772
  104.9 15.7 %all-to-all-start.4 = ((bf16[32,16,128]{2,1,0:T(8,128)(2,1)}), bf16[32,16,128]{2,1,0:T(8,128)(2,1)S(1)}, u32[]{:S(2)}, u32[]{:S(2)}) async-start(bf16[32,16,128]{2,1,0:T(8,128)(2,1)} %owned_sum.1), calls=%async_computation.4 | async-start | bytes 262144 | tf_op jit(solution)/shard_map/all_to_all | solution.py:376

commit v5 on v4

--- a/solution.py
+++ b/solution.py
@@ -14,6 +14,7 @@
 ROWS = 128
 CHIPS = 8
 SEQ = 2048
+HALF = SEQ // 2
 TILES = 64
 CAP = 4
 N_DP = 32
@@ -56,21 +57,30 @@
             rows[cols, :] = ref[:, cols]
 
 
+def side_of(ref, part):
+    return ref[:, :, part * HD : (part + 1) * HD].reshape(HALF, HD)
+
+
+def products(w, ds, q_rows, go_rows, ref):
+    dk = jnp.dot(ds[...], q_rows[...], preferred_element_type=F32) * SCALE
+    dv = jnp.dot(w[...], go_rows[...], preferred_element_type=F32)
+    dq_t = lax.dot_general(
+        side_of(ref, 0), ds[...], (((0,), (0,)), ((), ())), preferred_element_type=F32
+    )
+    return dk.reshape(CHIPS, ROWS, HD), dv.reshape(CHIPS, ROWS, HD), dq_t
+
+
 def attention_kernel(
     q_rows, go_rows, low_ref, mine_ref, other_ref,
-    dq_t, keep_ref, send_ref,
-    k_all, v_all, scores, prob_grads, ds_buf, w_buf, top, total, delta,
+    send_ref, dq_t, w_mine, ds_mine,
+    w_other, ds_other, scores, prob_grads, top, total, delta,
 ):
-    chip = lax.axis_index("chip")
     core = lax.axis_index("core")
-    first = (2 * chip + core) * ROWS
-    for ref, side in ((mine_ref, core), (other_ref, 1 - core)):
-        for j in range(CHIPS):
-            rows = pl.ds(pl.multiple_of((2 * j + side) * ROWS, ROWS), ROWS)
-            k_all[rows, :] = ref[j, :, :HD]
-            v_all[rows, :] = ref[j, :, HD:]
+    first = (2 * lax.axis_index("chip") + core) * ROWS
     row_pos = first + lax.broadcasted_iota(jnp.int32, (1, ROWS), 1)
     row_low = low_ref[0:1, :]
+    groups = [pl.ds(g * GROUP * HD, GROUP * HD) for g in range(HEADS // GROUP)]
+    sides = ((0, other_ref, 1 - core), (1, mine_ref, core))
 
     def fold(values, op):
         return op(values.reshape(values.shape[0] // 8, 8, values.shape[1]), axis=0)
@@ -80,49 +90,52 @@
             rows, ref[cols, :], (((1,), (1,)), ((), ())), preferred_element_type=F32
         )
 
-    pos = lax.broadcasted_iota(jnp.int32, (SEQ, ROWS), 0)
-    seen = (pos >= row_low) & (pos <= row_pos)
-    seen = jnp.concatenate([seen] * GROUP, axis=1)
-    keys = k_all[...]
-    groups = [pl.ds(g * GROUP * HD, GROUP * HD) for g in range(HEADS // GROUP)]
-    for cols in groups:
-        s = jnp.where(seen, against(keys, q_rows, cols), HIDDEN_NEG)
-        scores[:, cols] = s
-        top[:, cols] = fold(s, jnp.max)
+    for i, ref, side in sides:
+        rows = pl.ds(i * HALF, HALF)
+        shape = (CHIPS, ROWS, ROWS)
+        chip = lax.broadcasted_iota(jnp.int32, shape, 0)
+        pos = (2 * chip + side) * ROWS + lax.broadcasted_iota(jnp.int32, shape, 1)
+        pos = pos.reshape(HALF, ROWS)
+        seen = (pos >= row_low) & (pos <= row_pos)
+        seen = jnp.concatenate([seen] * GROUP, axis=1)
+        keys = side_of(ref, 0)
+        for cols in groups:
+            s = jnp.where(seen, against(keys, q_rows, cols), HIDDEN_NEG)
+            scores[rows, cols] = s
+            best = fold(s, jnp.max)
+            top[:, cols] = best if i == 0 else jnp.maximum(top[:, cols], best)
     top[0:1, :] = jnp.max(top[...], axis=0, keepdims=True)
-    values = v_all[...]
-    for cols in groups:
-        pg = against(values, go_rows, cols)
-        p = jnp.exp2((scores[:, cols] - top[0:1, cols]) * EXP2_SCALE)
-        scores[:, cols] = p
-        prob_grads[:, cols] = pg
-        total[:, cols] = fold(p, jnp.sum)
-        delta[:, cols] = fold(p * pg, jnp.sum)
+    for i, ref, side in sides:
+        rows = pl.ds(i * HALF, HALF)
+        values = side_of(ref, 1)
+        for cols in groups:
+            pg = against(values, go_rows, cols)
+            p = jnp.exp2((scores[rows, cols] - top[0:1, cols]) * EXP2_SCALE)
+            scores[rows, cols] = p
+            prob_grads[rows, cols] = pg
+            p_sum, pg_sum = fold(p, jnp.sum), fold(p * pg, jnp.sum)
+            total[:, cols] = p_sum if i == 0 else total[:, cols] + p_sum
+            delta[:, cols] = pg_sum if i == 0 else delta[:, cols] + pg_sum
     inverse = 1.0 / jnp.sum(total[...], axis=0, keepdims=True)
     total[0:1, :] = inverse
     delta[0:1, :] = jnp.sum(delta[...], axis=0, keepdims=True) * inverse
-    for cols in groups:
-        w = scores[:, cols] * total[0:1, cols]
-        w_buf[:, cols] = w.astype(BF16)
-        ds_buf[:, cols] = (w * (prob_grads[:, cols] - delta[0:1, cols])).astype(BF16)
-    ds = ds_buf[...]
-    dk = jnp.dot(ds, q_rows[...], preferred_element_type=F32) * SCALE
-    dv = jnp.dot(w_buf[...], go_rows[...], preferred_element_type=F32)
-    dq_t[...] = lax.dot_general(
-        keys, ds, (((0,), (0,)), ((), ())), preferred_element_type=F32
-    )
-    for pair in range(CHIPS):
-        for cols, grads in ((slice(0, HD), dk), (slice(HD, 2 * HD), dv)):
-            even = grads[2 * pair * ROWS : (2 * pair + 1) * ROWS]
-            odd = grads[(2 * pair + 1) * ROWS : (2 * pair + 2) * ROWS]
-            keep_ref[pair, :, cols] = jnp.where(core == 0, even, odd)
-            send_ref[pair, :, cols] = jnp.where(core == 0, odd, even).astype(BF16)
-
-
-def query_kernel(dq_t, dq_ref):
-    for h in range(HEADS):
-        cols = pl.ds(h * HD, HD)
-        dq_ref[:, cols] = (dq_t[:, cols].T * SCALE).astype(BF16)
+    for i, w_ref, ds_ref in ((0, w_other, ds_other), (1, w_mine, ds_mine)):
+        rows = pl.ds(i * HALF, HALF)
+        for cols in groups:
+            w = scores[rows, cols] * total[0:1, cols]
+            w_ref[:, cols] = w.astype(BF16)
+            ds_ref[:, cols] = (w * (prob_grads[rows, cols] - delta[0:1, cols])).astype(BF16)
+    dk, dv, dq = products(w_other, ds_other, q_rows, go_rows, other_ref)
+    send_ref[:, :, :HD] = dk.astype(BF16)
+    send_ref[:, :, HD:] = dv.astype(BF16)
+    dq_t[...] = dq
+
+
+def own_kernel(q_rows, go_rows, mine_ref, dq_in, w_mine, ds_mine, keep_ref, dq_t):
+    dk, dv, dq = products(w_mine, ds_mine, q_rows, go_rows, mine_ref)
+    keep_ref[:, :, :HD] = dk
+    keep_ref[:, :, HD:] = dv
+    dq_t[...] = dq_in[...] + dq
 
 
 VMEM = pl.BlockSpec(memory_space=pltpu.VMEM)
@@ -164,37 +177,39 @@
     return pl.pallas_call(
         attention_kernel,
         out_shape=(
+            jax.ShapeDtypeStruct((CHIPS, ROWS, 2 * HD), BF16),
             jax.ShapeDtypeStruct((HD, wide), F32),
-            jax.ShapeDtypeStruct((CHIPS, ROWS, 2 * HD), F32),
-            jax.ShapeDtypeStruct((CHIPS, ROWS, 2 * HD), BF16),
+            jax.ShapeDtypeStruct((HALF, wide), BF16),
+            jax.ShapeDtypeStruct((HALF, wide), BF16),
         ),
         in_specs=[VMEM] * 5,
-        out_specs=(VMEM, VMEM, VMEM),
+        out_specs=(VMEM,) * 4,
         scratch_shapes=[
-            pltpu.VMEM((SEQ, HD), BF16),
-            pltpu.VMEM((SEQ, HD), BF16),
+            pltpu.VMEM((HALF, wide), BF16),
+            pltpu.VMEM((HALF, wide), BF16),
             pltpu.VMEM((SEQ, wide), F32),
             pltpu.VMEM((SEQ, wide), F32),
-            pltpu.VMEM((SEQ, wide), BF16),
-            pltpu.VMEM((SEQ, wide), BF16),
             pltpu.VMEM((8, wide), F32),
             pltpu.VMEM((8, wide), F32),
             pltpu.VMEM((8, wide), F32),
         ],
-        compiler_params=limit(36),
+        compiler_params=limit(30),
         name="attention_backward",
     )(q_rows, go_rows, row_low, mine, other)
 
 
-def query_gradient(dq_t):
-    return pl.pallas_call(
-        query_kernel,
-        out_shape=jax.ShapeDtypeStruct((ROWS, HEADS * HD), BF16),
-        in_specs=[VMEM],
-        out_specs=VMEM,
-        compiler_params=limit(8),
-        name="query_gradient",
-    )(dq_t)
+def own_keys(q_rows, go_rows, mine, dq_t, w, ds):
+    return pl.pallas_call(
+        own_kernel,
+        out_shape=(
+            jax.ShapeDtypeStruct((CHIPS, ROWS, 2 * HD), F32),
+            jax.ShapeDtypeStruct((HD, HEADS * HD), F32),
+        ),
+        in_specs=[VMEM] * 6,
+        out_specs=(VMEM, VMEM),
+        compiler_params=limit(12),
+        name="own_keys",
+    )(q_rows, go_rows, mine, dq_t, w, ds)
 
 
 def low_half(shape, axis):
@@ -235,8 +250,20 @@
     half_tiles(jnp.where(core == 0, second, first).astype(BF16), hidden_ref, out_ref)
 
 
-def weight_keep_kernel(k_ref, hidden_ref, out_ref):
+def weight_keep_kernel(
+    owner_ref, k_ref, hidden_ref, dq_t, out_ref, dq_ref, place_ref, held
+):
+    for o in range(N_DP):
+        held[o] = 0
+    for t in range(TILES):
+        o = owner_ref[0, t]
+        slot = held[o]
+        held[o] = slot + 1
+        place_ref[0, t] = ((o & (N_Z - 1)) * N_YL + o // N_Z) * CAP + slot
     half_tiles(k_ref[...], hidden_ref, out_ref)
+    for h in range(HEADS):
+        cols = pl.ds(h * HD, HD)
+        dq_ref[:, cols] = (dq_t[:, cols].T * SCALE).astype(BF16)
 
 
 def weight_send(parts, hidden):
@@ -254,39 +281,40 @@
     )(parts, hidden)
 
 
-def weight_keep(k_t, hidden):
+def weight_keep(owner, k_t, hidden, dq_t):
+    smem = pl.BlockSpec(memory_space=pltpu.SMEM)
     return pl.pallas_call(
         weight_keep_kernel,
-        out_shape=jax.ShapeDtypeStruct((PLANE // 2, 2, TILES * 4, TILE), F32),
-        in_specs=[VMEM, VMEM],
-        out_specs=VMEM,
+        out_shape=(
+            jax.ShapeDtypeStruct((PLANE // 2, 2, TILES * 4, TILE), F32),
+            jax.ShapeDtypeStruct((ROWS, HEADS * HD), BF16),
+            jax.ShapeDtypeStruct((1, TILES), jnp.int32),
+        ),
+        in_specs=[smem, VMEM, VMEM, VMEM],
+        out_specs=(VMEM, VMEM, smem),
+        scratch_shapes=[pltpu.SMEM((N_DP,), jnp.int32)],
         compiler_params=limit(10),
         name="weight_tiles_to_keep",
-    )(k_t, hidden)
-
-
-def owner_kernel(owner_ref, parts_ref, out_ref, sums, placed, held):
+    )(owner, k_t, hidden, dq_t)
+
+
+def owner_kernel(place_ref, parts_ref, out_ref, sums, placed):
     rows = TILES * 4
     own = jnp.sum(parts_ref[...].astype(F32), axis=0)
     sums[:rows, :] = own
     sums[rows:, :] = pltpu.roll(own.reshape(rows // 8, 8, TILE), 4, axis=1).reshape(rows, TILE)
     placed[...] = jnp.zeros(placed.shape, F32)
-    for o in range(N_DP):
-        held[o] = 0
     low = low_half((8, TILE), 0)
     for t in range(TILES):
-        o = owner_ref[0, t]
-        slot = held[o]
-        held[o] = slot + 1
-        half = slot & 1
-        block = ((o & (N_Z - 1)) * N_YL + o // N_Z) * (CAP // 2) + slot // 2
-        at = pl.ds(pl.multiple_of(block * 8, 8), 8)
+        place = place_ref[0, t]
+        half = place & 1
+        at = pl.ds(pl.multiple_of((place >> 1) * 8, 8), 8)
         source = pl.multiple_of((half ^ (t & 1)) * rows + (t // 2) * 8, 8)
         placed[at, :] = jnp.where(low == (half == 0), sums[pl.ds(source, 8), :], placed[at, :])
     out_ref[...] = placed[...].astype(BF16).reshape(out_ref.shape)
 
 
-def to_owners(owner, parts):
+def to_owners(place, parts):
     return pl.pallas_call(
         owner_kernel,
         out_shape=jax.ShapeDtypeStruct((N_Z, OWNED, TILE), BF16),
@@ -295,11 +323,10 @@
         scratch_shapes=[
             pltpu.VMEM((2 * TILES * 4, TILE), F32),
             pltpu.VMEM((N_Z * OWNED, TILE), F32),
-            pltpu.SMEM((N_DP,), jnp.int32),
         ],
         compiler_params=limit(12),
         name="owner_slots",
-    )(owner, parts)
+    )(place, parts)
 
 
 def sum_kernel(parts_ref, out_ref):
@@ -361,17 +388,18 @@
     )
     other = lax.ppermute(mine, "core", SWAP)
     q_rows, go_rows, row_low = prepare(lengths, query[0], grad_out[0])
-    dq_t, keep, send = attention(q_rows, go_rows, row_low, mine, other)
-    dkv = (keep + lax.ppermute(send, "core", SWAP).astype(F32)).astype(BF16)
-    grad_query = query_gradient(dq_t)
+    send, dq_t, w, ds = attention(q_rows, go_rows, row_low, mine, other)
+    arrived = lax.ppermute(send, "core", SWAP)
+    keep, dq_t = own_keys(q_rows, go_rows, mine, dq_t, w, ds)
+    dkv = (keep + arrived.astype(F32)).astype(BF16)
     dkv = lax.all_to_all(dkv, "chip", 0, 0, tiled=True)
     hidden = hidden_in[0]
     grad_kv, k_t, send = weight_send(dkv, hidden)
     arrived = lax.ppermute(send, "core", SWAP)
-    keep = weight_keep(k_t, hidden)
+    keep, grad_query, place = weight_keep(owner.reshape(1, TILES), k_t, hidden, dq_t)
     wg = (keep + arrived.astype(F32)).astype(BF16).reshape(PLANE, TILES * 4, TILE)
     wg = lax.all_to_all(wg, ("yl", "chip"), 0, 0, tiled=True)
-    outgoing = to_owners(owner.reshape(1, TILES), wg)
+    outgoing = to_owners(place, wg)
     incoming = lax.all_to_all(outgoing, "z", 0, 0, tiled=True)
     pieces = lax.all_to_all(owned_sum(incoming), ("yl", "chip", "core"), 0, 0, tiled=True)
     return grad_query[None], grad_kv[None], factors_of(pieces)[None]

time: 122 us -> 119 us (0.975)
  blocking collectives: 74.1 us -> 89.7 us
  waiting for transfers between devices: 10.4 us -> 0.72 us
  starting transfers between devices: 19.7 us -> 11.6 us
    all_to_all x0 -> x1, blocking collectives: none -> 15.5 us  [body(): lax.all_to_all(owned_sum(incoming), ('yl', 'chip', 'core'), 0, 0, tiled=T...]
    all_to_all x1 -> x0, starting transfers between devices: 8.11 us -> none  [body(): lax.all_to_all(owned_sum(incoming), ('yl', 'chip', 'core'), 0, 0, tiled=T...]
    all_to_all x1 -> x0, waiting for transfers between devices: 6.64 us -> none  [body(): lax.all_to_all(owned_sum(incoming), ('yl', 'chip', 'core'), 0, 0, tiled=T...]
    ppermute x1 -> x2, starting transfers between devices: 4.07 us -> 6.33 us  [body(): arrived = lax.ppermute(send, 'core', SWAP)]
    ppermute x1 -> x0, starting transfers between devices: 2.24 us -> none  [body(): dkv = (keep + lax.ppermute(send, 'core', SWAP).astype(F32)).astype(BF16)]
    ppermute x1 -> x0, waiting for transfers between devices: 1.55 us -> none  [body(): dkv = (keep + lax.ppermute(send, 'core', SWAP).astype(F32)).astype(BF16)]
    ppermute x1 -> x2, waiting for transfers between devices: 1.82 us -> 0.32 us  [body(): arrived = lax.ppermute(send, 'core', SWAP)]
  transfers between devices with their start and end apart: 4 -> 3, of which waited for: 4 -> 2; matrix products, arithmetic and copies ran while one was open for 0% -> 0% of each run, Pallas kernels for 2% -> 4%
where the time goes in v5:
time: 119 us
  blocking collectives  89.7 us (75%)
  Pallas kernels  14.8 us (12%)
  starting transfers between devices  11.6 us (10%)
    all_to_all x1, blocking collectives, body(): incoming = lax.all_to_all(outgoing, 'z', 0, 0, tiled=True)  26.7 us
    all_to_all x1, blocking collectives, body(): wg = lax.all_to_all(wg, ('yl', 'chip'), 0, 0, tiled=True)  18.6 us
    all_to_all x1, blocking collectives, body(): lax.all_to_all(jnp.broadcast_to(key_value, (CHIPS, ROWS, 2 * HD)), 'chip'...  16.1 us
    all_to_all x1, blocking collectives, body(): lax.all_to_all(owned_sum(incoming), ('yl', 'chip', 'core'), 0, 0, tiled=T...  15.5 us
    all_to_all x1, blocking collectives, body(): dkv = lax.all_to_all(dkv, 'chip', 0, 0, tiled=True)  12.8 us
    pallas_call x1, Pallas kernels, attention(): pl.pallas_call(attention_kernel, out_shape=(jax.ShapeDtypeStruct((CHIPS,...  7.24 us
    ppermute x2, starting transfers between devices, body(): arrived = lax.ppermute(send, 'core', SWAP)  6.33 us
    ppermute x1, starting transfers between devices, body(): other = lax.ppermute(mine, 'core', SWAP)  5.25 us
  transfers between devices with their start and end apart: 3, of which 2 were waited for; matrix products, arithmetic and copies ran while one was open for 0% of the time, Pallas kernels for 4%

profile of v5, /device:TPU:1, one launch (start us, length us, event | category | flops | bytes accessed | tf_op | source)
XLA Modules:
  0.0 118.8 jit_solution(6772970356465791305)
XLA Ops:
  0.6 0.9 broadcast_in_dim.17
  1.5 16.1 %all_to_all.25.mine_ref = bf16[8,128,256]{2,1,0:T(8,128)(2,1)S(1)} all-to-all(bf16[8,128,256]{2,1,0:T(8,128)(2,1)S(1)} %broadcast_in_dim.17), channel_id=1, replica_groups=mesh['yl'=2,'z'=16,'chip'=8,'core'=2] {'chip'}, dimensions={0} | all-to-all | bytes 1048576 | tf_op jit(solution)/shard_map/all_to_all | solution.py:386
  17.6 5.3 %collective-permute-start = (bf16[8,128,256]{2,1,0:T(8,128)(2,1)S(1)}, bf16[8,128,256]{2,1,0:T(8,128)(2,1)S(1)}, u32[]{:S(2)}, u32[]{:S(2)}) collective-permute-start(bf16[8,128,256]{2,1,0:T(8,128)(2,1)S(1)} %all_to_all.25.mine_ref), channel_id=1, source_target_pairs={{0,1},{1,0},{2,3},{3,2},{4,5},{5,4},{6,7},{7,6},{8,9},{9,8},{10,11... | collective-permute-start | bytes 1572872 | tf_op jit(solution)/shard_map/ppermute | solution.py:389
  22.9 1.1 prepare_rows.1
  24.0 0.4 collective-permute-done.other_ref
  24.4 7.2 %attention_backward.1 = (bf16[8,128,256]{2,1,0:T(8,128)(2,1)S(1)}, f32[128,1024]{1,0:T(8,128)S(1)}, bf16[1024,1024]{1,0:T(8,128)(2,1)S(1)}, bf16[1024,1024]{1,0:T(8,128)(2,1)S(1)}) custom-call(bf16[1024,128]{1,0:T(8,128)(2,1)S(1)} %get-tuple-element.18.q_rows, bf16[1024,128]{1,0:T(8,128)(2,1)S(1)} %get-tuple-element.19.go_rows, ...), custom_call_target="tpu_custom_call" | custom-call | tf_op jit(solution)/shard_map/attention_backward/pallas_call | solution.py:177
  31.7 2.3 %collective-permute-start.1 = (bf16[8,128,256]{2,1,0:T(8,128)(2,1)S(1)}, bf16[8,128,256]{2,1,0:T(8,128)(2,1)S(1)}, u32[]{:S(2)}, u32[]{:S(2)}) collective-permute-start(bf16[8,128,256]{2,1,0:T(8,128)(2,1)S(1)} %get-tuple-element.25), channel_id=1, source_target_pairs={{0,1},{1,0},{2,3},{3,2},{4,5},{5,4},{6,7},{7,6},{8,9},{9,8},{10,11... | collective-permute-start | bytes 1572872 | tf_op jit(solution)/shard_map/ppermute | solution.py:392
  33.9 1.5 %own_keys.1 = (f32[8,128,256]{2,1,0:T(8,128)S(1)}, f32[128,1024]{1,0:T(8,128)S(1)}) custom-call(bf16[1024,128]{1,0:T(8,128)(2,1)S(1)} %get-tuple-element.18.q_rows, bf16[1024,128]{1,0:T(8,128)(2,1)S(1)} %get-tuple-element.19.go_rows, bf16[8,128,256]{2,1,0:T(8,128)(2,1)S(1)} %all_to_all.25.mine_ref, f32[128,1024]{1,0:T(8,128)S(1)} %get-tuple-element.21.dq_in, ...), custom_call_target="tpu_custom_call" | custom-call | tf_op jit(solution)/shard_map/own_keys/pallas_call | solution.py:202
  35.5 0.0 copy-start
  35.5 0.0 collective-permute-done.1
  35.5 0.2 add_convert_fusion.1
  35.7 0.0 copy-start.1
  35.7 12.8 %all_to_all.26.parts_ref = bf16[8,128,256]{2,1,0:T(8,128)(2,1)S(1)} all-to-all(bf16[8,128,256]{2,1,0:T(8,128)(2,1)S(1)} %add_convert_fusion.1), channel_id=1, replica_groups=mesh['yl'=2,'z'=16,'chip'=8,'core'=2] {'chip'}, dimensions={0} | all-to-all | bytes 1048576 | tf_op jit(solution)/shard_map/all_to_all | solution.py:395
  48.4 0.8 weight_tiles_to_send.1
  49.2 4.1 %collective-permute-start.2 = (bf16[8,2,256,128]{3,2,1,0:T(8,128)(2,1)S(1)}, bf16[8,2,256,128]{3,2,1,0:T(8,128)(2,1)S(1)}, u32[]{:S(2)}, u32[]{:S(2)}) collective-permute-start(bf16[8,2,256,128]{3,2,1,0:T(8,128)(2,1)S(1)} %get-tuple-element.32), channel_id=1, source_target_pairs={{0,1},{1,0},{2,3},{3,2},{4,5},{5,4},{6,7},{7,6},{8,9},{9,8},{10,11... | collective-permute-start | bytes 3145736 | tf_op jit(solution)/shard_map/ppermute | solution.py:398
  53.3 0.0 copy-done.1
  53.3 1.9 %weight_tiles_to_keep.1 = (f32[8,2,256,128]{3,2,1,0:T(8,128)S(1)}, bf16[128,1024]{1,0:T(8,128)(2,1)}, s32[1,64]{1,0:T(1,128)S(1)}) custom-call(s32[1,64]{1,0:T(1,128)S(1)} %bitcast.11, bf16[64,128]{1,0:T(8,128)(2,1)S(1)} %get-tuple-element.26.k_ref, bf16[128,8192]{1,0:T(8,128)(2,1)S(1)} %bitcast.10, f32[128,1024]{1,0:T(8,128)S(1)} %get-tuple-element.27.dq_t), custom_call_target="tpu_custom_call" | custom-call | tf_op jit(solution)/shard_map/weight_tiles_to_keep/pallas_call | solution.py:286
  55.2 0.3 collective-permute-done.2
  55.5 0.3 add_convert_fusion
  55.8 18.6 %all_to_all.27.parts_ref = bf16[16,256,128]{2,1,0:T(8,128)(2,1)S(1)} all-to-all(bf16[16,256,128]{2,1,0:T(8,128)(2,1)S(1)} %bitcast.12), channel_id=1, replica_groups=mesh['yl'=2,'z'=16,'chip'=8,'core'=2] {'yl','chip'}, dimensions={0} | all-to-all | bytes 2097152 | tf_op jit(solution)/shard_map/all_to_all | solution.py:401
  74.5 1.1 owner_slots.1
  75.5 26.7 %all_to_all.28.parts_ref = bf16[16,32,128]{2,1,0:T(8,128)(2,1)S(1)} all-to-all(bf16[16,32,128]{2,1,0:T(8,128)(2,1)S(1)} %owner_slots.1), channel_id=1, replica_groups=mesh['yl'=2,'z'=16,'chip'=8,'core'=2] {'z'}, dimensions={0} | all-to-all | bytes 262144 | tf_op jit(solution)/shard_map/all_to_all | solution.py:403
  102.3 15.5 %all_to_all.29.pieces_ref = bf16[32,16,128]{2,1,0:T(8,128)(2,1)S(1)} all-to-all(bf16[32,16,128]{2,1,0:T(8,128)(2,1)S(1)} %owned_sum.1), channel_id=1, replica_groups=mesh['yl'=2,'z'=16,'chip'=8,'core'=2] {'yl','chip','core'}, dimensions={0} | all-to-all | bytes 262144 | tf_op jit(solution)/shard_map/all_to_all | solution.py:404
  117.7 1.1 factors.1
  (2 shorter events, 0.0 us)
Async XLA Ops:
  17.6 6.8 %collective-permute-start = (bf16[8,128,256]{2,1,0:T(8,128)(2,1)S(1)}, bf16[8,128,256]{2,1,0:T(8,128)(2,1)S(1)}, u32[]{:S(2)}, u32[]{:S(2)}) collective-permute-start(bf16[8,128,256]{2,1,0:T(8,128)(2,1)S(1)} %all_to_all.25.mine_ref), channel_id=1, source_target_pairs={{0,1},{1,0},{2,3},{3,2},{4,5},{5,4},{6,7},{7,6},{8,9},{9,8},{10,11... | collective-permute-start | bytes 1572872 | tf_op jit(solution)/shard_map/ppermute | solution.py:389
  31.7 3.8 %collective-permute-start.1 = (bf16[8,128,256]{2,1,0:T(8,128)(2,1)S(1)}, bf16[8,128,256]{2,1,0:T(8,128)(2,1)S(1)}, u32[]{:S(2)}, u32[]{:S(2)}) collective-permute-start(bf16[8,128,256]{2,1,0:T(8,128)(2,1)S(1)} %get-tuple-element.25), channel_id=1, source_target_pairs={{0,1},{1,0},{2,3},{3,2},{4,5},{5,4},{6,7},{7,6},{8,9},{9,8},{10,11... | collective-permute-start | bytes 1572872 | tf_op jit(solution)/shard_map/ppermute | solution.py:392
  35.5 12.9 %copy-start = (bf16[1,128,8192]{2,1,0:T(8,128)(2,1)S(1)}, bf16[1,128,8192]{2,1,0:T(8,128)(2,1)}, u32[]{:S(2)}) copy-start(bf16[1,128,8192]{2,1,0:T(8,128)(2,1)} %param.6) | copy-start | bytes 6291460
  35.7 17.6 %copy-start.1 = (s32[64,1]{0,1:T(1,128)S(1)}, s32[64,1]{0,1:T(1,128)}, u32[]{:S(2)}) copy-start(s32[64,1]{0,1:T(1,128)} %param.11) | copy-start | bytes 772
  49.2 6.3 %collective-permute-start.2 = (bf16[8,2,256,128]{3,2,1,0:T(8,128)(2,1)S(1)}, bf16[8,2,256,128]{3,2,1,0:T(8,128)(2,1)S(1)}, u32[]{:S(2)}, u32[]{:S(2)}) collective-permute-start(bf16[8,2,256,128]{3,2,1,0:T(8,128)(2,1)S(1)} %get-tuple-element.32), channel_id=1, source_target_pairs={{0,1},{1,0},{2,3},{3,2},{4,5},{5,4},{6,7},{7,6},{8,9},{9,8},{10,11... | collective-permute-start | bytes 3145736 | tf_op jit(solution)/shard_map/ppermute | solution.py:398

commit v6 on v5

--- a/solution.py
+++ b/solution.py
@@ -61,26 +61,26 @@
     return ref[:, :, part * HD : (part + 1) * HD].reshape(HALF, HD)
 
 
-def products(w, ds, q_rows, go_rows, ref):
+def products(w, ds, q_rows, go_rows):
     dk = jnp.dot(ds[...], q_rows[...], preferred_element_type=F32) * SCALE
     dv = jnp.dot(w[...], go_rows[...], preferred_element_type=F32)
-    dq_t = lax.dot_general(
-        side_of(ref, 0), ds[...], (((0,), (0,)), ((), ())), preferred_element_type=F32
-    )
-    return dk.reshape(CHIPS, ROWS, HD), dv.reshape(CHIPS, ROWS, HD), dq_t
+    return dk.reshape(CHIPS, ROWS, HD), dv.reshape(CHIPS, ROWS, HD)
 
 
 def attention_kernel(
     q_rows, go_rows, low_ref, mine_ref, other_ref,
-    send_ref, dq_t, w_mine, ds_mine,
-    w_other, ds_other, scores, prob_grads, top, total, delta,
+    send_ref, w_mine, ds_mine, ds_other,
+    w_other, probs, top, total, delta,
 ):
     core = lax.axis_index("core")
     first = (2 * lax.axis_index("chip") + core) * ROWS
     row_pos = first + lax.broadcasted_iota(jnp.int32, (1, ROWS), 1)
     row_low = low_ref[0:1, :]
     groups = [pl.ds(g * GROUP * HD, GROUP * HD) for g in range(HEADS // GROUP)]
-    sides = ((0, other_ref, 1 - core), (1, mine_ref, core))
+    sides = (
+        (0, other_ref, 1 - core, w_other, ds_other),
+        (1, mine_ref, core, w_mine, ds_mine),
+    )
 
     def fold(values, op):
         return op(values.reshape(values.shape[0] // 8, 8, values.shape[1]), axis=0)
@@ -90,8 +90,7 @@
             rows, ref[cols, :], (((1,), (1,)), ((), ())), preferred_element_type=F32
         )
 
-    for i, ref, side in sides:
-        rows = pl.ds(i * HALF, HALF)
+    def scores_of(ref, side):
         shape = (CHIPS, ROWS, ROWS)
         chip = lax.broadcasted_iota(jnp.int32, shape, 0)
         pos = (2 * chip + side) * ROWS + lax.broadcasted_iota(jnp.int32, shape, 1)
@@ -99,43 +98,43 @@
         seen = (pos >= row_low) & (pos <= row_pos)
         seen = jnp.concatenate([seen] * GROUP, axis=1)
         keys = side_of(ref, 0)
+        return lambda cols: jnp.where(seen, against(keys, q_rows, cols), HIDDEN_NEG)
+
+    for i, ref, side, _, _ in sides:
+        scores = scores_of(ref, side)
         for cols in groups:
-            s = jnp.where(seen, against(keys, q_rows, cols), HIDDEN_NEG)
-            scores[rows, cols] = s
-            best = fold(s, jnp.max)
+            best = fold(scores(cols), jnp.max)
             top[:, cols] = best if i == 0 else jnp.maximum(top[:, cols], best)
     top[0:1, :] = jnp.max(top[...], axis=0, keepdims=True)
-    for i, ref, side in sides:
-        rows = pl.ds(i * HALF, HALF)
+    for i, ref, side, _, _ in sides:
+        scores = scores_of(ref, side)
         values = side_of(ref, 1)
         for cols in groups:
             pg = against(values, go_rows, cols)
-            p = jnp.exp2((scores[rows, cols] - top[0:1, cols]) * EXP2_SCALE)
-            scores[rows, cols] = p
-            prob_grads[rows, cols] = pg
+            p = jnp.exp2((scores(cols) - top[0:1, cols]) * EXP2_SCALE)
+            probs[pl.ds(i * HALF, HALF), cols] = p
             p_sum, pg_sum = fold(p, jnp.sum), fold(p * pg, jnp.sum)
             total[:, cols] = p_sum if i == 0 else total[:, cols] + p_sum
             delta[:, cols] = pg_sum if i == 0 else delta[:, cols] + pg_sum
     inverse = 1.0 / jnp.sum(total[...], axis=0, keepdims=True)
     total[0:1, :] = inverse
     delta[0:1, :] = jnp.sum(delta[...], axis=0, keepdims=True) * inverse
-    for i, w_ref, ds_ref in ((0, w_other, ds_other), (1, w_mine, ds_mine)):
-        rows = pl.ds(i * HALF, HALF)
+    for i, ref, _, w_ref, ds_ref in sides:
+        values = side_of(ref, 1)
         for cols in groups:
-            w = scores[rows, cols] * total[0:1, cols]
+            w = probs[pl.ds(i * HALF, HALF), cols] * total[0:1, cols]
             w_ref[:, cols] = w.astype(BF16)
-            ds_ref[:, cols] = (w * (prob_grads[rows, cols] - delta[0:1, cols])).astype(BF16)
-    dk, dv, dq = products(w_other, ds_other, q_rows, go_rows, other_ref)
+            pg = against(values, go_rows, cols)
+            ds_ref[:, cols] = (w * (pg - delta[0:1, cols])).astype(BF16)
+    dk, dv = products(w_other, ds_other, q_rows, go_rows)
     send_ref[:, :, :HD] = dk.astype(BF16)
     send_ref[:, :, HD:] = dv.astype(BF16)
-    dq_t[...] = dq
-
-
-def own_kernel(q_rows, go_rows, mine_ref, dq_in, w_mine, ds_mine, keep_ref, dq_t):
-    dk, dv, dq = products(w_mine, ds_mine, q_rows, go_rows, mine_ref)
+
+
+def own_kernel(q_rows, go_rows, w_mine, ds_mine, keep_ref):
+    dk, dv = products(w_mine, ds_mine, q_rows, go_rows)
     keep_ref[:, :, :HD] = dk
     keep_ref[:, :, HD:] = dv
-    dq_t[...] = dq_in[...] + dq
 
 
 VMEM = pl.BlockSpec(memory_space=pltpu.VMEM)
@@ -172,44 +171,38 @@
     )(in_hbm(lengths), in_hbm(query), in_hbm(grad_out))
 
 
+SMEM = pl.BlockSpec(memory_space=pltpu.SMEM)
+
+
 def attention(q_rows, go_rows, row_low, mine, other):
     wide = HEADS * HD
+    half = jax.ShapeDtypeStruct((HALF, wide), BF16)
     return pl.pallas_call(
         attention_kernel,
-        out_shape=(
-            jax.ShapeDtypeStruct((CHIPS, ROWS, 2 * HD), BF16),
-            jax.ShapeDtypeStruct((HD, wide), F32),
-            jax.ShapeDtypeStruct((HALF, wide), BF16),
-            jax.ShapeDtypeStruct((HALF, wide), BF16),
-        ),
+        out_shape=(jax.ShapeDtypeStruct((CHIPS, ROWS, 2 * HD), BF16), half, half, half),
         in_specs=[VMEM] * 5,
         out_specs=(VMEM,) * 4,
         scratch_shapes=[
             pltpu.VMEM((HALF, wide), BF16),
-            pltpu.VMEM((HALF, wide), BF16),
-            pltpu.VMEM((SEQ, wide), F32),
             pltpu.VMEM((SEQ, wide), F32),
             pltpu.VMEM((8, wide), F32),
             pltpu.VMEM((8, wide), F32),
             pltpu.VMEM((8, wide), F32),
         ],
-        compiler_params=limit(30),
+        compiler_params=limit(24),
         name="attention_backward",
     )(q_rows, go_rows, row_low, mine, other)
 
 
-def own_keys(q_rows, go_rows, mine, dq_t, w, ds):
+def own_keys(q_rows, go_rows, w, ds):
     return pl.pallas_call(
         own_kernel,
-        out_shape=(
-            jax.ShapeDtypeStruct((CHIPS, ROWS, 2 * HD), F32),
-            jax.ShapeDtypeStruct((HD, HEADS * HD), F32),
-        ),
-        in_specs=[VMEM] * 6,
-        out_specs=(VMEM, VMEM),
+        out_shape=jax.ShapeDtypeStruct((CHIPS, ROWS, 2 * HD), F32),
+        in_specs=[VMEM] * 4,
+        out_specs=VMEM,
         compiler_params=limit(12),
         name="own_keys",
-    )(q_rows, go_rows, mine, dq_t, w, ds)
+    )(q_rows, go_rows, w, ds)
 
 
 def low_half(shape, axis):
@@ -250,19 +243,33 @@
     half_tiles(jnp.where(core == 0, second, first).astype(BF16), hidden_ref, out_ref)
 
 
-def weight_keep_kernel(
-    owner_ref, k_ref, hidden_ref, dq_t, out_ref, dq_ref, place_ref, held
-):
-    for o in range(N_DP):
-        held[o] = 0
+def slot_table(owner_ref, place_ref):
+    held = [jnp.int32(0)] * 4
     for t in range(TILES):
         o = owner_ref[0, t]
-        slot = held[o]
-        held[o] = slot + 1
+        word, shift = o >> 3, (o & 7) * 4
+        count = jnp.int32(0)
+        for i in range(4):
+            count = jnp.where(word == i, held[i], count)
+            held[i] = held[i] + jnp.where(word == i, 1 << shift, 0)
+        slot = (count >> shift) & 15
         place_ref[0, t] = ((o & (N_Z - 1)) * N_YL + o // N_Z) * CAP + slot
+
+
+def weight_keep_kernel(
+    owner_ref, k_ref, hidden_ref, mine_ref, other_ref, ds_mine, ds_other,
+    out_ref, dq_ref, place_ref,
+):
+    slot_table(owner_ref, place_ref)
     half_tiles(k_ref[...], hidden_ref, out_ref)
+    dq_t = sum(
+        lax.dot_general(
+            side_of(ref, 0), ds[...], (((0,), (0,)), ((), ())), preferred_element_type=F32
+        )
+        for ref, ds in ((mine_ref, ds_mine), (other_ref, ds_other))
+    )
     for h in range(HEADS):
-        cols = pl.ds(h * HD, HD)
+        cols = slice(h * HD, (h + 1) * HD)
         dq_ref[:, cols] = (dq_t[:, cols].T * SCALE).astype(BF16)
 
 
@@ -281,8 +288,7 @@
     )(parts, hidden)
 
 
-def weight_keep(owner, k_t, hidden, dq_t):
-    smem = pl.BlockSpec(memory_space=pltpu.SMEM)
+def weight_keep(owner, k_t, hidden, mine, other, ds_mine, ds_other):
     return pl.pallas_call(
         weight_keep_kernel,
         out_shape=(
@@ -290,12 +296,11 @@
             jax.ShapeDtypeStruct((ROWS, HEADS * HD), BF16),
             jax.ShapeDtypeStruct((1, TILES), jnp.int32),
         ),
-        in_specs=[smem, VMEM, VMEM, VMEM],
-        out_specs=(VMEM, VMEM, smem),
-        scratch_shapes=[pltpu.SMEM((N_DP,), jnp.int32)],
-        compiler_params=limit(10),
+        in_specs=[SMEM] + [VMEM] * 6,
+        out_specs=(VMEM, VMEM, SMEM),
+        compiler_params=limit(12),
         name="weight_tiles_to_keep",
-    )(owner, k_t, hidden, dq_t)
+    )(owner, k_t, hidden, mine, other, ds_mine, ds_other)
 
 
 def owner_kernel(place_ref, parts_ref, out_ref, sums, placed):
@@ -388,15 +393,17 @@
     )
     other = lax.ppermute(mine, "core", SWAP)
     q_rows, go_rows, row_low = prepare(lengths, query[0], grad_out[0])
-    send, dq_t, w, ds = attention(q_rows, go_rows, row_low, mine, other)
+    send, w, ds_mine, ds_other = attention(q_rows, go_rows, row_low, mine, other)
     arrived = lax.ppermute(send, "core", SWAP)
-    keep, dq_t = own_keys(q_rows, go_rows, mine, dq_t, w, ds)
+    keep = own_keys(q_rows, go_rows, w, ds_mine)
     dkv = (keep + arrived.astype(F32)).astype(BF16)
     dkv = lax.all_to_all(dkv, "chip", 0, 0, tiled=True)
     hidden = hidden_in[0]
     grad_kv, k_t, send = weight_send(dkv, hidden)
     arrived = lax.ppermute(send, "core", SWAP)
-    keep, grad_query, place = weight_keep(owner.reshape(1, TILES), k_t, hidden, dq_t)
+    keep, grad_query, place = weight_keep(
+        owner.reshape(1, TILES), k_t, hidden, mine, other, ds_mine, ds_other
+    )
     wg = (keep + arrived.astype(F32)).astype(BF16).reshape(PLANE, TILES * 4, TILE)
     wg = lax.all_to_all(wg, ("yl", "chip"), 0, 0, tiled=True)
     outgoing = to_owners(place, wg)

time: 119 us -> 119 us (level)
    pallas_call x1, Pallas kernels: 7.24 us -> 5.86 us  [attention(): pl.pallas_call(attention_kernel, out_shape=(jax.ShapeDtypeStruct((CHIPS,...]
  transfers between devices with their start and end apart: 3 -> 3, of which waited for: 2 -> 2; matrix products, arithmetic and copies ran while one was open for 0% -> 0% of each run, Pallas kernels for 4% -> 5%
where the time goes in v6:
time: 119 us
  blocking collectives  90.1 us (76%)
  Pallas kernels  14.2 us (12%)
  starting transfers between devices  11.6 us (10%)
    all_to_all x1, blocking collectives, body(): incoming = lax.all_to_all(outgoing, 'z', 0, 0, tiled=True)  26.7 us
    all_to_all x1, blocking collectives, body(): wg = lax.all_to_all(wg, ('yl', 'chip'), 0, 0, tiled=True)  19.5 us
    all_to_all x1, blocking collectives, body(): lax.all_to_all(jnp.broadcast_to(key_value, (CHIPS, ROWS, 2 * HD)), 'chip'...  16.1 us
    all_to_all x1, blocking collectives, body(): lax.all_to_all(owned_sum(incoming), ('yl', 'chip', 'core'), 0, 0, tiled=T...  15 us
    all_to_all x1, blocking collectives, body(): dkv = lax.all_to_all(dkv, 'chip', 0, 0, tiled=True)  12.8 us
    ppermute x2, starting transfers between devices, body(): arrived = lax.ppermute(send, 'core', SWAP)  6.31 us
    pallas_call x1, Pallas kernels, attention(): pl.pallas_call(attention_kernel, out_shape=(jax.ShapeDtypeStruct((CHIPS,...  5.86 us
    ppermute x1, starting transfers between devices, body(): other = lax.ppermute(mine, 'core', SWAP)  5.25 us
  transfers between devices with their start and end apart: 3, of which 2 were waited for; matrix products, arithmetic and copies ran while one was open for 0% of the time, Pallas kernels for 5%

profile of v6, /device:TPU:1, one launch (start us, length us, event | category | flops | bytes accessed | tf_op | source)
XLA Modules:
  0.0 118.6 jit_solution(11004296784595462735)
XLA Ops:
  0.6 0.9 broadcast_in_dim.17
  1.5 16.1 %all_to_all.25.mine_ref = bf16[8,128,256]{2,1,0:T(8,128)(2,1)S(1)} all-to-all(bf16[8,128,256]{2,1,0:T(8,128)(2,1)S(1)} %broadcast_in_dim.17), channel_id=1, replica_groups=mesh['yl'=2,'z'=16,'chip'=8,'core'=2] {'chip'}, dimensions={0} | all-to-all | bytes 1048576 | tf_op jit(solution)/shard_map/all_to_all | solution.py:391
  17.6 5.3 %collective-permute-start = (bf16[8,128,256]{2,1,0:T(8,128)(2,1)S(1)}, bf16[8,128,256]{2,1,0:T(8,128)(2,1)S(1)}, u32[]{:S(2)}, u32[]{:S(2)}) collective-permute-start(bf16[8,128,256]{2,1,0:T(8,128)(2,1)S(1)} %all_to_all.25.mine_ref), channel_id=1, source_target_pairs={{0,1},{1,0},{2,3},{3,2},{4,5},{5,4},{6,7},{7,6},{8,9},{9,8},{10,11... | collective-permute-start | bytes 1572872 | tf_op jit(solution)/shard_map/ppermute | solution.py:394
  22.9 1.1 prepare_rows.1
  24.0 0.4 collective-permute-done.other_ref
  24.4 5.9 %attention_backward.1 = (bf16[8,128,256]{2,1,0:T(8,128)(2,1)S(1)}, bf16[1024,1024]{1,0:T(8,128)(2,1)S(1)}, bf16[1024,1024]{1,0:T(8,128)(2,1)S(1)}, bf16[1024,1024]{1,0:T(8,128)(2,1)S(1)}) custom-call(bf16[1024,128]{1,0:T(8,128)(2,1)S(1)} %get-tuple-element.16.q_rows, bf16[1024,128]{1,0:T(8,128)(2,1)S(1)} %get-tuple-element.17.go_rows, ...), custom_call_target="tpu_custom_call" | custom-call | tf_op jit(solution)/shard_map/attention_backward/pallas_call | solution.py:180
  30.3 2.3 %collective-permute-start.1 = (bf16[8,128,256]{2,1,0:T(8,128)(2,1)S(1)}, bf16[8,128,256]{2,1,0:T(8,128)(2,1)S(1)}, u32[]{:S(2)}, u32[]{:S(2)}) collective-permute-start(bf16[8,128,256]{2,1,0:T(8,128)(2,1)S(1)} %get-tuple-element.21), channel_id=1, source_target_pairs={{0,1},{1,0},{2,3},{3,2},{4,5},{5,4},{6,7},{7,6},{8,9},{9,8},{10,11... | collective-permute-start | bytes 1572872 | tf_op jit(solution)/shard_map/ppermute | solution.py:397
  32.6 1.2 %own_keys.1 = f32[8,128,256]{2,1,0:T(8,128)S(1)} custom-call(bf16[1024,128]{1,0:T(8,128)(2,1)S(1)} %get-tuple-element.16.q_rows, bf16[1024,128]{1,0:T(8,128)(2,1)S(1)} %get-tuple-element.17.go_rows, bf16[1024,1024]{1,0:T(8,128)(2,1)S(1)} %get-tuple-element.19.w_mine, bf16[1024,1024]{1,0:T(8,128)(2,1)S(1)} %get-tuple-element.20.ds_mine), custom_call_target="tpu_custom_call" | custom-call | tf_op jit(solution)/shard_map/own_keys/pallas_call | solution.py:198
  33.8 0.0 copy-start
  33.8 0.3 collective-permute-done.1
  34.1 0.1 add_convert_fusion.1
  34.2 0.0 copy-start.1
  34.2 12.8 %all_to_all.26.parts_ref = bf16[8,128,256]{2,1,0:T(8,128)(2,1)S(1)} all-to-all(bf16[8,128,256]{2,1,0:T(8,128)(2,1)S(1)} %add_convert_fusion.1), channel_id=1, replica_groups=mesh['yl'=2,'z'=16,'chip'=8,'core'=2] {'chip'}, dimensions={0} | all-to-all | bytes 1048576 | tf_op jit(solution)/shard_map/all_to_all | solution.py:400
  47.0 0.0 copy-done
  47.0 0.8 weight_tiles_to_send.1
  47.8 4.0 %collective-permute-start.2 = (bf16[8,2,256,128]{3,2,1,0:T(8,128)(2,1)S(1)}, bf16[8,2,256,128]{3,2,1,0:T(8,128)(2,1)S(1)}, u32[]{:S(2)}, u32[]{:S(2)}) collective-permute-start(bf16[8,2,256,128]{3,2,1,0:T(8,128)(2,1)S(1)} %get-tuple-element.28), channel_id=1, source_target_pairs={{0,1},{1,0},{2,3},{3,2},{4,5},{5,4},{6,7},{7,6},{8,9},{9,8},{10,11... | collective-permute-start | bytes 3145736 | tf_op jit(solution)/shard_map/ppermute | solution.py:403
  51.8 3.0 %weight_tiles_to_keep.1 = (f32[8,2,256,128]{3,2,1,0:T(8,128)S(1)}, bf16[128,1024]{1,0:T(8,128)(2,1)}, s32[1,64]{1,0:T(1,128)S(1)}) custom-call(s32[1,64]{1,0:T(1,128)S(1)} %bitcast.11, bf16[64,128]{1,0:T(8,128)(2,1)S(1)} %get-tuple-element.22.k_ref, bf16[128,8192]{1,0:T(8,128)(2,1)S(1)} %bitcast.10, bf16[8,128,256]{2,1,0:T(8,128)(2,1)S(1)} %all_to_all.25.mine_ref, ...), custom_call_target="tpu_custom_call" | custom-call | tf_op jit(solution)/shard_map/weight_tiles_to_keep/pallas_call | solution.py:292
  54.9 0.0 collective-permute-done.2
  54.9 0.3 add_convert_fusion
  55.2 19.5 %all_to_all.27.parts_ref = bf16[16,256,128]{2,1,0:T(8,128)(2,1)S(1)} all-to-all(bf16[16,256,128]{2,1,0:T(8,128)(2,1)S(1)} %bitcast.12), channel_id=1, replica_groups=mesh['yl'=2,'z'=16,'chip'=8,'core'=2] {'yl','chip'}, dimensions={0} | all-to-all | bytes 2097152 | tf_op jit(solution)/shard_map/all_to_all | solution.py:408
  74.8 1.1 owner_slots.1
  75.8 26.7 %all_to_all.28.parts_ref = bf16[16,32,128]{2,1,0:T(8,128)(2,1)S(1)} all-to-all(bf16[16,32,128]{2,1,0:T(8,128)(2,1)S(1)} %owner_slots.1), channel_id=1, replica_groups=mesh['yl'=2,'z'=16,'chip'=8,'core'=2] {'z'}, dimensions={0} | all-to-all | bytes 262144 | tf_op jit(solution)/shard_map/all_to_all | solution.py:410
  102.6 15.0 %all_to_all.29.pieces_ref = bf16[32,16,128]{2,1,0:T(8,128)(2,1)S(1)} all-to-all(bf16[32,16,128]{2,1,0:T(8,128)(2,1)S(1)} %owned_sum.1), channel_id=1, replica_groups=mesh['yl'=2,'z'=16,'chip'=8,'core'=2] {'yl','chip','core'}, dimensions={0} | all-to-all | bytes 262144 | tf_op jit(solution)/shard_map/all_to_all | solution.py:411
  117.5 1.1 factors.1
  (2 shorter events, 0.0 us)
Async XLA Ops:
  17.6 6.8 %collective-permute-start = (bf16[8,128,256]{2,1,0:T(8,128)(2,1)S(1)}, bf16[8,128,256]{2,1,0:T(8,128)(2,1)S(1)}, u32[]{:S(2)}, u32[]{:S(2)}) collective-permute-start(bf16[8,128,256]{2,1,0:T(8,128)(2,1)S(1)} %all_to_all.25.mine_ref), channel_id=1, source_target_pairs={{0,1},{1,0},{2,3},{3,2},{4,5},{5,4},{6,7},{7,6},{8,9},{9,8},{10,11... | collective-permute-start | bytes 1572872 | tf_op jit(solution)/shard_map/ppermute | solution.py:394
  30.3 3.8 %collective-permute-start.1 = (bf16[8,128,256]{2,1,0:T(8,128)(2,1)S(1)}, bf16[8,128,256]{2,1,0:T(8,128)(2,1)S(1)}, u32[]{:S(2)}, u32[]{:S(2)}) collective-permute-start(bf16[8,128,256]{2,1,0:T(8,128)(2,1)S(1)} %get-tuple-element.21), channel_id=1, source_target_pairs={{0,1},{1,0},{2,3},{3,2},{4,5},{5,4},{6,7},{7,6},{8,9},{9,8},{10,11... | collective-permute-start | bytes 1572872 | tf_op jit(solution)/shard_map/ppermute | solution.py:397
  33.8 13.2 %copy-start = (bf16[1,128,8192]{2,1,0:T(8,128)(2,1)S(1)}, bf16[1,128,8192]{2,1,0:T(8,128)(2,1)}, u32[]{:S(2)}) copy-start(bf16[1,128,8192]{2,1,0:T(8,128)(2,1)} %param.6) | copy-start | bytes 6291460
  34.2 17.6 %copy-start.1 = (s32[64,1]{0,1:T(1,128)S(1)}, s32[64,1]{0,1:T(1,128)}, u32[]{:S(2)}) copy-start(s32[64,1]{0,1:T(1,128)} %param.11) | copy-start | bytes 772
  47.8 7.1 %collective-permute-start.2 = (bf16[8,2,256,128]{3,2,1,0:T(8,128)(2,1)S(1)}, bf16[8,2,256,128]{3,2,1,0:T(8,128)(2,1)S(1)}, u32[]{:S(2)}, u32[]{:S(2)}) collective-permute-start(bf16[8,2,256,128]{3,2,1,0:T(8,128)(2,1)S(1)} %get-tuple-element.28), channel_id=1, source_target_pairs={{0,1},{1,0},{2,3},{3,2},{4,5},{5,4},{6,7},{7,6},{8,9},{9,8},{10,11... | collective-permute-start | bytes 3145736 | tf_op jit(solution)/shard_map/ppermute | solution.py:403

commit v7 on v6

--- a/solution.py
+++ b/solution.py
@@ -21,6 +21,8 @@
 MODEL = 8192
 N_YL = 2
 N_Z = 16
+N_X = 4
+N_YH = 2
 PLANE = N_YL * CHIPS
 OWNED = N_YL * CAP * 4
 GROUP = 2
@@ -29,6 +31,11 @@
 EXP2_SCALE = SCALE * math.log2(math.e)
 F32 = jnp.float32
 BF16 = jnp.bfloat16
+
+
+def first_position():
+    chip = N_YH * lax.axis_index("x") + lax.axis_index("yh")
+    return (2 * chip + lax.axis_index("core")) * ROWS
 
 
 def prepare_kernel(
@@ -41,7 +48,7 @@
     ]
     for copy in copies:
         copy.start()
-    first = (2 * lax.axis_index("chip") + lax.axis_index("core")) * ROWS
+    first = first_position()
     row_pos = first + lax.broadcasted_iota(jnp.int32, low_ref.shape, 1)
     row_low = jnp.zeros(low_ref.shape, jnp.int32)
     end = jnp.int32(0)
@@ -61,19 +68,22 @@
     return ref[:, :, part * HD : (part + 1) * HD].reshape(HALF, HD)
 
 
-def products(w, ds, q_rows, go_rows):
+def products(w, ds, q_rows, go_rows, ref):
     dk = jnp.dot(ds[...], q_rows[...], preferred_element_type=F32) * SCALE
     dv = jnp.dot(w[...], go_rows[...], preferred_element_type=F32)
-    return dk.reshape(CHIPS, ROWS, HD), dv.reshape(CHIPS, ROWS, HD)
+    dq_t = lax.dot_general(
+        side_of(ref, 0), ds[...], (((0,), (0,)), ((), ())), preferred_element_type=F32
+    )
+    return dk.reshape(CHIPS, ROWS, HD), dv.reshape(CHIPS, ROWS, HD), dq_t
 
 
 def attention_kernel(
     q_rows, go_rows, low_ref, mine_ref, other_ref,
-    send_ref, w_mine, ds_mine, ds_other,
-    w_other, probs, top, total, delta,
+    send_ref, dq_t, w_mine, ds_mine,
+    w_other, ds_other, probs, top, total, delta,
 ):
     core = lax.axis_index("core")
-    first = (2 * lax.axis_index("chip") + core) * ROWS
+    first = first_position()
     row_pos = first + lax.broadcasted_iota(jnp.int32, (1, ROWS), 1)
     row_low = low_ref[0:1, :]
     groups = [pl.ds(g * GROUP * HD, GROUP * HD) for g in range(HEADS // GROUP)]
@@ -92,7 +102,8 @@
 
     def scores_of(ref, side):
         shape = (CHIPS, ROWS, ROWS)
-        chip = lax.broadcasted_iota(jnp.int32, shape, 0)
+        place = lax.broadcasted_iota(jnp.int32, shape, 0)
+        chip = N_YH * (place & (N_X - 1)) + place // N_X
         pos = (2 * chip + side) * ROWS + lax.broadcasted_iota(jnp.int32, shape, 1)
         pos = pos.reshape(HALF, ROWS)
         seen = (pos >= row_low) & (pos <= row_pos)
@@ -126,15 +137,17 @@
             w_ref[:, cols] = w.astype(BF16)
             pg = against(values, go_rows, cols)
             ds_ref[:, cols] = (w * (pg - delta[0:1, cols])).astype(BF16)
-    dk, dv = products(w_other, ds_other, q_rows, go_rows)
+    dk, dv, dq = products(w_other, ds_other, q_rows, go_rows, other_ref)
     send_ref[:, :, :HD] = dk.astype(BF16)
     send_ref[:, :, HD:] = dv.astype(BF16)
-
-
-def own_kernel(q_rows, go_rows, w_mine, ds_mine, keep_ref):
-    dk, dv = products(w_mine, ds_mine, q_rows, go_rows)
+    dq_t[...] = dq
+
+
+def own_kernel(q_rows, go_rows, mine_ref, dq_in, w_mine, ds_mine, keep_ref, dq_t):
+    dk, dv, dq = products(w_mine, ds_mine, q_rows, go_rows, mine_ref)
     keep_ref[:, :, :HD] = dk
     keep_ref[:, :, HD:] = dv
+    dq_t[...] = dq_in[...] + dq
 
 
 VMEM = pl.BlockSpec(memory_space=pltpu.VMEM)
@@ -179,10 +192,16 @@
     half = jax.ShapeDtypeStruct((HALF, wide), BF16)
     return pl.pallas_call(
         attention_kernel,
-        out_shape=(jax.ShapeDtypeStruct((CHIPS, ROWS, 2 * HD), BF16), half, half, half),
+        out_shape=(
+            jax.ShapeDtypeStruct((CHIPS, ROWS, 2 * HD), BF16),
+            jax.ShapeDtypeStruct((HD, wide), F32),
+            half,
+            half,
+        ),
         in_specs=[VMEM] * 5,
         out_specs=(VMEM,) * 4,
         scratch_shapes=[
+            pltpu.VMEM((HALF, wide), BF16),
             pltpu.VMEM((HALF, wide), BF16),
             pltpu.VMEM((SEQ, wide), F32),
             pltpu.VMEM((8, wide), F32),
@@ -194,15 +213,18 @@
     )(q_rows, go_rows, row_low, mine, other)
 
 
-def own_keys(q_rows, go_rows, w, ds):
+def own_keys(q_rows, go_rows, mine, dq_t, w, ds):
     return pl.pallas_call(
         own_kernel,
-        out_shape=jax.ShapeDtypeStruct((CHIPS, ROWS, 2 * HD), F32),
-        in_specs=[VMEM] * 4,
-        out_specs=VMEM,
+        out_shape=(
+            jax.ShapeDtypeStruct((CHIPS, ROWS, 2 * HD), F32),
+            jax.ShapeDtypeStruct((HD, HEADS * HD), F32),
+        ),
+        in_specs=[VMEM] * 6,
+        out_specs=(VMEM, VMEM),
         compiler_params=limit(12),
         name="own_keys",
-    )(q_rows, go_rows, w, ds)
+    )(q_rows, go_rows, mine, dq_t, w, ds)
 
 
 def low_half(shape, axis):
@@ -256,20 +278,11 @@
         place_ref[0, t] = ((o & (N_Z - 1)) * N_YL + o // N_Z) * CAP + slot
 
 
-def weight_keep_kernel(
-    owner_ref, k_ref, hidden_ref, mine_ref, other_ref, ds_mine, ds_other,
-    out_ref, dq_ref, place_ref,
-):
+def weight_keep_kernel(owner_ref, k_ref, hidden_ref, dq_t, out_ref, dq_ref, place_ref):
     slot_table(owner_ref, place_ref)
     half_tiles(k_ref[...], hidden_ref, out_ref)
-    dq_t = sum(
-        lax.dot_general(
-            side_of(ref, 0), ds[...], (((0,), (0,)), ((), ())), preferred_element_type=F32
-        )
-        for ref, ds in ((mine_ref, ds_mine), (other_ref, ds_other))
-    )
     for h in range(HEADS):
-        cols = slice(h * HD, (h + 1) * HD)
+        cols = pl.ds(h * HD, HD)
         dq_ref[:, cols] = (dq_t[:, cols].T * SCALE).astype(BF16)
 
 
@@ -288,7 +301,7 @@
     )(parts, hidden)
 
 
-def weight_keep(owner, k_t, hidden, mine, other, ds_mine, ds_other):
+def weight_keep(owner, k_t, hidden, dq_t):
     return pl.pallas_call(
         weight_keep_kernel,
         out_shape=(
@@ -296,11 +309,11 @@
             jax.ShapeDtypeStruct((ROWS, HEADS * HD), BF16),
             jax.ShapeDtypeStruct((1, TILES), jnp.int32),
         ),
-        in_specs=[SMEM] + [VMEM] * 6,
+        in_specs=[SMEM] + [VMEM] * 3,
         out_specs=(VMEM, VMEM, SMEM),
         compiler_params=limit(12),
         name="weight_tiles_to_keep",
-    )(owner, k_t, hidden, mine, other, ds_mine, ds_other)
+    )(owner, k_t, hidden, dq_t)
 
 
 def owner_kernel(place_ref, parts_ref, out_ref, sums, placed):
@@ -338,9 +351,13 @@
     gradient = jnp.sum(parts_ref[...].astype(F32), axis=0) * (1.0 / math.sqrt(N_DP * SEQ))
     gradient = gradient.astype(BF16)
     rows = OWNED // N_YL
+    some = 2 * N_YH
     for yl in range(N_YL):
         piece = gradient[yl * rows : (yl + 1) * rows]
-        out_ref[yl * PLANE : (yl + 1) * PLANE] = jnp.broadcast_to(piece[None], (PLANE, rows, TILE))
+        piece = jnp.broadcast_to(piece[None], (some, rows, TILE))
+        for x in range(N_X):
+            at = (x * N_YL + yl) * some
+            out_ref[at : at + some] = piece
 
 
 def owned_sum(parts):
@@ -385,36 +402,38 @@
 
 
 SWAP = ((0, 1), (1, 0))
+CHIP_AXES = ("yh", "x")
+PLANE_AXES = ("x", "yl", "yh")
 
 
 def body(hidden_in, query, key_value, grad_out, lengths, owner):
     mine = lax.all_to_all(
-        jnp.broadcast_to(key_value, (CHIPS, ROWS, 2 * HD)), "chip", 0, 0, tiled=True
+        jnp.broadcast_to(key_value, (CHIPS, ROWS, 2 * HD)), CHIP_AXES, 0, 0, tiled=True
     )
     other = lax.ppermute(mine, "core", SWAP)
     q_rows, go_rows, row_low = prepare(lengths, query[0], grad_out[0])
-    send, w, ds_mine, ds_other = attention(q_rows, go_rows, row_low, mine, other)
+    send, dq_t, w, ds = attention(q_rows, go_rows, row_low, mine, other)
     arrived = lax.ppermute(send, "core", SWAP)
-    keep = own_keys(q_rows, go_rows, w, ds_mine)
+    keep, dq_t = own_keys(q_rows, go_rows, mine, dq_t, w, ds)
     dkv = (keep + arrived.astype(F32)).astype(BF16)
-    dkv = lax.all_to_all(dkv, "chip", 0, 0, tiled=True)
+    dkv = lax.all_to_all(dkv, CHIP_AXES, 0, 0, tiled=True)
     hidden = hidden_in[0]
     grad_kv, k_t, send = weight_send(dkv, hidden)
     arrived = lax.ppermute(send, "core", SWAP)
-    keep, grad_query, place = weight_keep(
-        owner.reshape(1, TILES), k_t, hidden, mine, other, ds_mine, ds_other
-    )
+    keep, grad_query, place = weight_keep(owner.reshape(1, TILES), k_t, hidden, dq_t)
     wg = (keep + arrived.astype(F32)).astype(BF16).reshape(PLANE, TILES * 4, TILE)
-    wg = lax.all_to_all(wg, ("yl", "chip"), 0, 0, tiled=True)
+    wg = lax.all_to_all(wg, PLANE_AXES, 0, 0, tiled=True)
     outgoing = to_owners(place, wg)
     incoming = lax.all_to_all(outgoing, "z", 0, 0, tiled=True)
-    pieces = lax.all_to_all(owned_sum(incoming), ("yl", "chip", "core"), 0, 0, tiled=True)
+    pieces = lax.all_to_all(owned_sum(incoming), PLANE_AXES + ("core",), 0, 0, tiled=True)
     return grad_query[None], grad_kv[None], factors_of(pieces)[None]
 
 
 def solution(mesh):
-    fine = Mesh(mesh.devices.reshape(N_YL, N_Z, CHIPS, 2), ("yl", "z", "chip", "core"))
-    dp, ctx = ("yl", "z"), ("chip", "core")
+    fine = Mesh(
+        mesh.devices.reshape(N_YL, N_Z, N_X, N_YH, 2), ("yl", "z", "x", "yh", "core")
+    )
+    dp, ctx = ("yl", "z"), ("x", "yh", "core")
     split = P(dp, ctx, None)
     return jax.shard_map(
         body,

time: 119 us -> 119 us (level)
  blocking collectives: 90.1 us -> 92.3 us
  starting transfers between devices: 11.6 us -> 9.89 us
    all_to_all x4, blocking collectives: 63.4 us -> 65.6 us  [the longest x1 19.4 us: body(): wg = lax.all_to_all(wg, PLANE_AXES, 0, 0, tiled=True)]
    ppermute x2, starting transfers between devices: 6.31 us -> 4.99 us  [body(): arrived = lax.ppermute(send, 'core', SWAP)]
  transfers between devices with their start and end apart: 3 -> 3, of which waited for: 2 -> 1; matrix products, arithmetic and copies ran while one was open for 0% -> 0% of each run, Pallas kernels for 5% -> 4%
where the time goes in v7:
time: 119 us
  blocking collectives  92.3 us (78%)
  Pallas kernels  14.1 us (12%)
  starting transfers between devices  9.89 us (8%)
    all_to_all x1, blocking collectives, body(): incoming = lax.all_to_all(outgoing, 'z', 0, 0, tiled=True)  26.7 us
    all_to_all x1, blocking collectives, body(): wg = lax.all_to_all(wg, PLANE_AXES, 0, 0, tiled=True)  19.4 us
    all_to_all x1, blocking collectives, body(): lax.all_to_all(jnp.broadcast_to(key_value, (CHIPS, ROWS, 2 * HD)), CHIP_A...  16.8 us
    all_to_all x1, blocking collectives, body(): lax.all_to_all(owned_sum(incoming), PLANE_AXES + ('core',), 0, 0, tiled=T...  15.1 us
    all_to_all x1, blocking collectives, body(): dkv = lax.all_to_all(dkv, CHIP_AXES, 0, 0, tiled=True)  14.3 us
    pallas_call x1, Pallas kernels, attention(): pl.pallas_call(attention_kernel, out_shape=(jax.ShapeDtypeStruct((CHIPS,...  6.13 us
    ppermute x2, starting transfers between devices, body(): arrived = lax.ppermute(send, 'core', SWAP)  4.99 us
    ppermute x1, starting transfers between devices, body(): other = lax.ppermute(mine, 'core', SWAP)  4.9 us
  transfers between devices with their start and end apart: 3, of which 1 were waited for; matrix products, arithmetic and copies ran while one was open for 0% of the time, Pallas kernels for 4%

profile of v7, /device:TPU:1, one launch (start us, length us, event | category | flops | bytes accessed | tf_op | source)
XLA Modules:
  0.0 118.7 jit_solution(4263379257162696479)
XLA Ops:
  0.6 0.9 broadcast_in_dim.17
  1.5 16.8 %all_to_all.25.mine_ref = bf16[8,128,256]{2,1,0:T(8,128)(2,1)S(1)} all-to-all(bf16[8,128,256]{2,1,0:T(8,128)(2,1)S(1)} %broadcast_in_dim.17), channel_id=1, replica_groups=mesh['yl'=2,'z'=16,'x'=4,'yh'=2,'core'=2] {'yh','x'}, dimensions={0} | all-to-all | bytes 1048576 | tf_op jit(solution)/shard_map/all_to_all | solution.py:410
  18.3 4.9 %collective-permute-start = (bf16[8,128,256]{2,1,0:T(8,128)(2,1)S(1)}, bf16[8,128,256]{2,1,0:T(8,128)(2,1)S(1)}, u32[]{:S(2)}, u32[]{:S(2)}) collective-permute-start(bf16[8,128,256]{2,1,0:T(8,128)(2,1)S(1)} %all_to_all.25.mine_ref), channel_id=1, source_target_pairs={{0,1},{1,0},{2,3},{3,2},{4,5},{5,4},{6,7},{7,6},{8,9},{9,8},{10,11... | collective-permute-start | bytes 1572872 | tf_op jit(solution)/shard_map/ppermute | solution.py:413
  23.2 1.1 prepare_rows.1
  24.3 0.4 collective-permute-done.other_ref
  24.7 6.1 %attention_backward.1 = (bf16[8,128,256]{2,1,0:T(8,128)(2,1)S(1)}, f32[128,1024]{1,0:T(8,128)S(1)}, bf16[1024,1024]{1,0:T(8,128)(2,1)S(1)}, bf16[1024,1024]{1,0:T(8,128)(2,1)S(1)}) custom-call(bf16[1024,128]{1,0:T(8,128)(2,1)S(1)} %get-tuple-element.18.q_rows, bf16[1024,128]{1,0:T(8,128)(2,1)S(1)} %get-tuple-element.19.go_rows, ...), custom_call_target="tpu_custom_call" | custom-call | tf_op jit(solution)/shard_map/attention_backward/pallas_call | solution.py:193
  30.9 2.3 %collective-permute-start.1 = (bf16[8,128,256]{2,1,0:T(8,128)(2,1)S(1)}, bf16[8,128,256]{2,1,0:T(8,128)(2,1)S(1)}, u32[]{:S(2)}, u32[]{:S(2)}) collective-permute-start(bf16[8,128,256]{2,1,0:T(8,128)(2,1)S(1)} %get-tuple-element.25), channel_id=1, source_target_pairs={{0,1},{1,0},{2,3},{3,2},{4,5},{5,4},{6,7},{7,6},{8,9},{9,8},{10,11... | collective-permute-start | bytes 1572872 | tf_op jit(solution)/shard_map/ppermute | solution.py:416
  33.2 1.5 %own_keys.1 = (f32[8,128,256]{2,1,0:T(8,128)S(1)}, f32[128,1024]{1,0:T(8,128)S(1)}) custom-call(bf16[1024,128]{1,0:T(8,128)(2,1)S(1)} %get-tuple-element.18.q_rows, bf16[1024,128]{1,0:T(8,128)(2,1)S(1)} %get-tuple-element.19.go_rows, bf16[8,128,256]{2,1,0:T(8,128)(2,1)S(1)} %all_to_all.25.mine_ref, f32[128,1024]{1,0:T(8,128)S(1)} %get-tuple-element.21.dq_in, ...), custom_call_target="tpu_custom_call" | custom-call | tf_op jit(solution)/shard_map/own_keys/pallas_call | solution.py:217
  34.7 0.0 copy-start
  34.7 0.0 collective-permute-done.1
  34.7 0.2 add_convert_fusion.1
  34.9 0.0 copy-start.1
  34.9 14.3 %all_to_all.26.parts_ref = bf16[8,128,256]{2,1,0:T(8,128)(2,1)S(1)} all-to-all(bf16[8,128,256]{2,1,0:T(8,128)(2,1)S(1)} %add_convert_fusion.1), channel_id=1, replica_groups=mesh['yl'=2,'z'=16,'x'=4,'yh'=2,'core'=2] {'yh','x'}, dimensions={0} | all-to-all | bytes 1048576 | tf_op jit(solution)/shard_map/all_to_all | solution.py:419
  49.2 0.0 copy-done
  49.2 0.8 weight_tiles_to_send.1
  50.0 2.7 %collective-permute-start.2 = (bf16[8,2,256,128]{3,2,1,0:T(8,128)(2,1)S(1)}, bf16[8,2,256,128]{3,2,1,0:T(8,128)(2,1)S(1)}, u32[]{:S(2)}, u32[]{:S(2)}) collective-permute-start(bf16[8,2,256,128]{3,2,1,0:T(8,128)(2,1)S(1)} %get-tuple-element.32), channel_id=1, source_target_pairs={{0,1},{1,0},{2,3},{3,2},{4,5},{5,4},{6,7},{7,6},{8,9},{9,8},{10,11... | collective-permute-start | bytes 3145736 | tf_op jit(solution)/shard_map/ppermute | solution.py:422
  52.7 2.3 %weight_tiles_to_keep.1 = (f32[8,2,256,128]{3,2,1,0:T(8,128)S(1)}, bf16[128,1024]{1,0:T(8,128)(2,1)}, s32[1,64]{1,0:T(1,128)S(1)}) custom-call(s32[1,64]{1,0:T(1,128)S(1)} %bitcast.11, bf16[64,128]{1,0:T(8,128)(2,1)S(1)} %get-tuple-element.26.k_ref, bf16[128,8192]{1,0:T(8,128)(2,1)S(1)} %bitcast.10, f32[128,1024]{1,0:T(8,128)S(1)} %get-tuple-element.27.dq_t), custom_call_target="tpu_custom_call" | custom-call | tf_op jit(solution)/shard_map/weight_tiles_to_keep/pallas_call | solution.py:305
  55.1 0.0 collective-permute-done.2
  55.1 0.3 add_convert_fusion
  55.4 19.4 %all_to_all.27.parts_ref = bf16[16,256,128]{2,1,0:T(8,128)(2,1)S(1)} all-to-all(bf16[16,256,128]{2,1,0:T(8,128)(2,1)S(1)} %bitcast.12), channel_id=1, replica_groups=mesh['yl'=2,'z'=16,'x'=4,'yh'=2,'core'=2] {'x','yl','yh'}, dimensions={0} | all-to-all | bytes 2097152 | tf_op jit(solution)/shard_map/all_to_all | solution.py:425
  74.8 1.1 owner_slots.1
  75.9 26.7 %all_to_all.28.parts_ref = bf16[16,32,128]{2,1,0:T(8,128)(2,1)S(1)} all-to-all(bf16[16,32,128]{2,1,0:T(8,128)(2,1)S(1)} %owner_slots.1), channel_id=1, replica_groups=mesh['yl'=2,'z'=16,'x'=4,'yh'=2,'core'=2] {'z'}, dimensions={0} | all-to-all | bytes 262144 | tf_op jit(solution)/shard_map/all_to_all | solution.py:427
  102.6 15.1 %all_to_all.29.pieces_ref = bf16[32,16,128]{2,1,0:T(8,128)(2,1)S(1)} all-to-all(bf16[32,16,128]{2,1,0:T(8,128)(2,1)S(1)} %owned_sum.1), channel_id=1, replica_groups=mesh['yl'=2,'z'=16,'x'=4,'yh'=2,'core'=2] {'x','yl','yh','core'}, dimensions={0} | all-to-all | bytes 262144 | tf_op jit(solution)/shard_map/all_to_all | solution.py:428
  117.7 1.1 factors.1
  (2 shorter events, 0.0 us)
Async XLA Ops:
  18.3 6.4 %collective-permute-start = (bf16[8,128,256]{2,1,0:T(8,128)(2,1)S(1)}, bf16[8,128,256]{2,1,0:T(8,128)(2,1)S(1)}, u32[]{:S(2)}, u32[]{:S(2)}) collective-permute-start(bf16[8,128,256]{2,1,0:T(8,128)(2,1)S(1)} %all_to_all.25.mine_ref), channel_id=1, source_target_pairs={{0,1},{1,0},{2,3},{3,2},{4,5},{5,4},{6,7},{7,6},{8,9},{9,8},{10,11... | collective-permute-start | bytes 1572872 | tf_op jit(solution)/shard_map/ppermute | solution.py:413
  30.9 3.8 %collective-permute-start.1 = (bf16[8,128,256]{2,1,0:T(8,128)(2,1)S(1)}, bf16[8,128,256]{2,1,0:T(8,128)(2,1)S(1)}, u32[]{:S(2)}, u32[]{:S(2)}) collective-permute-start(bf16[8,128,256]{2,1,0:T(8,128)(2,1)S(1)} %get-tuple-element.25), channel_id=1, source_target_pairs={{0,1},{1,0},{2,3},{3,2},{4,5},{5,4},{6,7},{7,6},{8,9},{9,8},{10,11... | collective-permute-start | bytes 1572872 | tf_op jit(solution)/shard_map/ppermute | solution.py:416
  34.7 14.5 %copy-start = (bf16[1,128,8192]{2,1,0:T(8,128)(2,1)S(1)}, bf16[1,128,8192]{2,1,0:T(8,128)(2,1)}, u32[]{:S(2)}) copy-start(bf16[1,128,8192]{2,1,0:T(8,128)(2,1)} %param.6) | copy-start | bytes 6291460
  34.9 17.8 %copy-start.1 = (s32[64,1]{0,1:T(1,128)S(1)}, s32[64,1]{0,1:T(1,128)}, u32[]{:S(2)}) copy-start(s32[64,1]{0,1:T(1,128)} %param.11) | copy-start | bytes 772
  50.0 5.1 %collective-permute-start.2 = (bf16[8,2,256,128]{3,2,1,0:T(8,128)(2,1)S(1)}, bf16[8,2,256,128]{3,2,1,0:T(8,128)(2,1)S(1)}, u32[]{:S(2)}, u32[]{:S(2)}) collective-permute-start(bf16[8,2,256,128]{3,2,1,0:T(8,128)(2,1)S(1)} %get-tuple-element.32), channel_id=1, source_target_pairs={{0,1},{1,0},{2,3},{3,2},{4,5},{5,4},{6,7},{7,6},{8,9},{9,8},{10,11... | collective-permute-start | bytes 3145736 | tf_op jit(solution)/shard_map/ppermute | solution.py:422

commit v8 on v7

--- a/solution.py
+++ b/solution.py
@@ -38,13 +38,26 @@
     return (2 * chip + lax.axis_index("core")) * ROWS
 
 
+def slot_table(owner):
+    across = jnp.broadcast_to(owner.astype(F32), (TILES, TILES))
+    earlier = lax.broadcasted_iota(jnp.int32, (TILES, TILES), 0) < lax.broadcasted_iota(
+        jnp.int32, (TILES, TILES), 1
+    )
+    same = jnp.where((across.T == across) & earlier, 1.0, 0.0)
+    slot = jnp.sum(same, axis=0, keepdims=True).astype(jnp.int32)
+    return ((owner & (N_Z - 1)) * N_YL + (owner >> 4)) * CAP + slot
+
+
 def prepare_kernel(
-    lengths_hbm, q_hbm, go_hbm, q_rows, go_rows, low_ref, lengths_ref, q_ref, go_ref, sems
+    lengths_hbm, owner_hbm, q_hbm, go_hbm,
+    q_rows, go_rows, low_ref, place_ref,
+    lengths_ref, owner_ref, q_ref, go_ref, sems,
 ):
     copies = [
         pltpu.make_async_copy(lengths_hbm, lengths_ref, sems.at[0]),
-        pltpu.make_async_copy(q_hbm, q_ref, sems.at[1]),
-        pltpu.make_async_copy(go_hbm, go_ref, sems.at[2]),
+        pltpu.make_async_copy(owner_hbm, owner_ref, sems.at[1]),
+        pltpu.make_async_copy(q_hbm, q_ref, sems.at[2]),
+        pltpu.make_async_copy(go_hbm, go_ref, sems.at[3]),
     ]
     for copy in copies:
         copy.start()
@@ -57,7 +70,9 @@
         end = end + lengths_ref[0, d]
         row_low = jnp.maximum(row_low, jnp.where(row_pos >= end, end, 0))
     low_ref[...] = row_low
-    for copy, rows, ref in ((copies[1], q_rows, q_ref), (copies[2], go_rows, go_ref)):
+    copies[1].wait()
+    place_ref[...] = slot_table(owner_ref[...])
+    for copy, rows, ref in ((copies[2], q_rows, q_ref), (copies[3], go_rows, go_ref)):
         copy.wait()
         for h in range(HEADS):
             cols = pl.ds(h * HD, HD)
@@ -102,8 +117,7 @@
 
     def scores_of(ref, side):
         shape = (CHIPS, ROWS, ROWS)
-        place = lax.broadcasted_iota(jnp.int32, shape, 0)
-        chip = N_YH * (place & (N_X - 1)) + place // N_X
+        chip = lax.broadcasted_iota(jnp.int32, shape, 0)
         pos = (2 * chip + side) * ROWS + lax.broadcasted_iota(jnp.int32, shape, 1)
         pos = pos.reshape(HALF, ROWS)
         seen = (pos >= row_low) & (pos <= row_pos)
@@ -151,6 +165,7 @@
 
 
 VMEM = pl.BlockSpec(memory_space=pltpu.VMEM)
+SMEM = pl.BlockSpec(memory_space=pltpu.SMEM)
 
 
 def in_hbm(x):
@@ -161,7 +176,7 @@
     return pltpu.CompilerParams(vmem_limit_bytes=mib * 1024 * 1024)
 
 
-def prepare(lengths, query, grad_out):
+def prepare(lengths, owner, query, grad_out):
     hbm = pl.BlockSpec(memory_space=pltpu.HBM)
     wide = HEADS * HD
     return pl.pallas_call(
@@ -170,21 +185,20 @@
             jax.ShapeDtypeStruct((wide, HD), BF16),
             jax.ShapeDtypeStruct((wide, HD), BF16),
             jax.ShapeDtypeStruct((8, ROWS), jnp.int32),
+            jax.ShapeDtypeStruct((1, TILES), jnp.int32),
         ),
-        in_specs=[hbm, hbm, hbm],
-        out_specs=(VMEM, VMEM, VMEM),
+        in_specs=[hbm] * 4,
+        out_specs=(VMEM,) * 4,
         scratch_shapes=[
             pltpu.SMEM((1, 8), jnp.int32),
+            pltpu.VMEM((1, TILES), jnp.int32),
             pltpu.VMEM((ROWS, wide), BF16),
             pltpu.VMEM((ROWS, wide), BF16),
-            pltpu.SemaphoreType.DMA((3,)),
+            pltpu.SemaphoreType.DMA((4,)),
         ],
         compiler_params=limit(8),
         name="prepare_rows",
-    )(in_hbm(lengths), in_hbm(query), in_hbm(grad_out))
-
-
-SMEM = pl.BlockSpec(memory_space=pltpu.SMEM)
+    )(in_hbm(lengths), in_hbm(owner), in_hbm(query), in_hbm(grad_out))
 
 
 def attention(q_rows, go_rows, row_low, mine, other):
@@ -265,21 +279,7 @@
     half_tiles(jnp.where(core == 0, second, first).astype(BF16), hidden_ref, out_ref)
 
 
-def slot_table(owner_ref, place_ref):
-    held = [jnp.int32(0)] * 4
-    for t in range(TILES):
-        o = owner_ref[0, t]
-        word, shift = o >> 3, (o & 7) * 4
-        count = jnp.int32(0)
-        for i in range(4):
-            count = jnp.where(word == i, held[i], count)
-            held[i] = held[i] + jnp.where(word == i, 1 << shift, 0)
-        slot = (count >> shift) & 15
-        place_ref[0, t] = ((o & (N_Z - 1)) * N_YL + o // N_Z) * CAP + slot
-
-
-def weight_keep_kernel(owner_ref, k_ref, hidden_ref, dq_t, out_ref, dq_ref, place_ref):
-    slot_table(owner_ref, place_ref)
+def weight_keep_kernel(k_ref, hidden_ref, dq_t, out_ref, dq_ref):
     half_tiles(k_ref[...], hidden_ref, out_ref)
     for h in range(HEADS):
         cols = pl.ds(h * HD, HD)
@@ -301,19 +301,18 @@
     )(parts, hidden)
 
 
-def weight_keep(owner, k_t, hidden, dq_t):
+def weight_keep(k_t, hidden, dq_t):
     return pl.pallas_call(
         weight_keep_kernel,
         out_shape=(
             jax.ShapeDtypeStruct((PLANE // 2, 2, TILES * 4, TILE), F32),
             jax.ShapeDtypeStruct((ROWS, HEADS * HD), BF16),
-            jax.ShapeDtypeStruct((1, TILES), jnp.int32),
         ),
-        in_specs=[SMEM] + [VMEM] * 3,
-        out_specs=(VMEM, VMEM, SMEM),
+        in_specs=[VMEM] * 3,
+        out_specs=(VMEM, VMEM),
         compiler_params=limit(12),
         name="weight_tiles_to_keep",
-    )(owner, k_t, hidden, dq_t)
+    )(k_t, hidden, dq_t)
 
 
 def owner_kernel(place_ref, parts_ref, out_ref, sums, placed):
@@ -371,9 +370,10 @@
     )(parts)
 
 
-def factor_kernel(pieces_ref, out_ref):
+def factor_kernel(pieces_ref, out_hbm, out_ref, sems):
     pieces = pieces_ref[...].astype(F32)
     low = low_half((PLANE, 8, TILE), 1)
+    copies = []
     for two in range(CAP // 2):
         pair = pieces[:, two * 8 : (two + 1) * 8, :].reshape(PLANE, 2, 8, TILE)
         even, odd = pair[:, 0], pair[:, 1]
@@ -384,10 +384,15 @@
         for i in range(2):
             grad_t = both[i].reshape(TILE, TILE)
             flat = grad_t.astype(BF16)
-            flat_t = grad_t.T.astype(BF16)
+            flat_t = flat.T
             s = 2 * two + i
             out_ref[s, 0] = jnp.dot(flat_t, flat, preferred_element_type=F32) * (1.0 / TILE)
             out_ref[s, 1] = jnp.dot(flat, flat_t, preferred_element_type=F32) * (1.0 / TILE)
+            copy = pltpu.make_async_copy(out_ref.at[s], out_hbm.at[s], sems.at[s])
+            copy.start()
+            copies.append(copy)
+    for copy in copies:
+        copy.wait()
 
 
 def factors_of(pieces):
@@ -395,14 +400,18 @@
         factor_kernel,
         out_shape=jax.ShapeDtypeStruct((CAP, 2, TILE, TILE), F32),
         in_specs=[VMEM],
-        out_specs=VMEM,
+        out_specs=pl.BlockSpec(memory_space=pltpu.HBM),
+        scratch_shapes=[
+            pltpu.VMEM((CAP, 2, TILE, TILE), F32),
+            pltpu.SemaphoreType.DMA((CAP,)),
+        ],
         compiler_params=limit(8),
         name="factors",
     )(pieces)
 
 
 SWAP = ((0, 1), (1, 0))
-CHIP_AXES = ("yh", "x")
+CHIP_AXES = ("x", "yh")
 PLANE_AXES = ("x", "yl", "yh")
 
 
@@ -411,7 +420,9 @@
         jnp.broadcast_to(key_value, (CHIPS, ROWS, 2 * HD)), CHIP_AXES, 0, 0, tiled=True
     )
     other = lax.ppermute(mine, "core", SWAP)
-    q_rows, go_rows, row_low = prepare(lengths, query[0], grad_out[0])
+    q_rows, go_rows, row_low, place = prepare(
+        lengths, owner.reshape(1, TILES), query[0], grad_out[0]
+    )
     send, dq_t, w, ds = attention(q_rows, go_rows, row_low, mine, other)
     arrived = lax.ppermute(send, "core", SWAP)
     keep, dq_t = own_keys(q_rows, go_rows, mine, dq_t, w, ds)
@@ -420,7 +431,7 @@
     hidden = hidden_in[0]
     grad_kv, k_t, send = weight_send(dkv, hidden)
     arrived = lax.ppermute(send, "core", SWAP)
-    keep, grad_query, place = weight_keep(owner.reshape(1, TILES), k_t, hidden, dq_t)
+    keep, grad_query = weight_keep(k_t, hidden, dq_t)
     wg = (keep + arrived.astype(F32)).astype(BF16).reshape(PLANE, TILES * 4, TILE)
     wg = lax.all_to_all(wg, PLANE_AXES, 0, 0, tiled=True)
     outgoing = to_owners(place, wg)

time: 119 us -> 118 us (level)
  blocking collectives: 92.3 us -> 89.8 us
  starting transfers between devices: 9.89 us -> 11.6 us
  Pallas kernels: 14.1 us -> 12.8 us
    all_to_all x1, blocking collectives: 14.3 us -> 12.7 us  [body(): dkv = lax.all_to_all(dkv, CHIP_AXES, 0, 0, tiled=True)]
    ppermute x2, starting transfers between devices: 4.99 us -> 6.34 us  [body(): arrived = lax.ppermute(send, 'core', SWAP)]
    pallas_call x1, Pallas kernels: 2.35 us -> 1.13 us  [weight_keep(): pl.pallas_call(weight_keep_kernel, out_shape=(jax.ShapeDtypeStruct((PLANE...]
  transfers between devices with their start and end apart: 3 -> 3, of which waited for: 1 -> 2; matrix products, arithmetic and copies ran while one was open for 0% -> 0% of each run, Pallas kernels for 4% -> 3%
where the time goes in v8:
time: 118 us
  blocking collectives  89.8 us (76%)
  Pallas kernels  12.8 us (11%)
  starting transfers between devices  11.6 us (10%)
  waiting for transfers between devices  1.51 us (1%)
    all_to_all x1, blocking collectives, body(): incoming = lax.all_to_all(outgoing, 'z', 0, 0, tiled=True)  26.8 us
    all_to_all x1, blocking collectives, body(): wg = lax.all_to_all(wg, PLANE_AXES, 0, 0, tiled=True)  19.1 us
    all_to_all x1, blocking collectives, body(): lax.all_to_all(jnp.broadcast_to(key_value, (CHIPS, ROWS, 2 * HD)), CHIP_A...  16.1 us
    all_to_all x1, blocking collectives, body(): lax.all_to_all(owned_sum(incoming), PLANE_AXES + ('core',), 0, 0, tiled=T...  15 us
    all_to_all x1, blocking collectives, body(): dkv = lax.all_to_all(dkv, CHIP_AXES, 0, 0, tiled=True)  12.7 us
    ppermute x2, starting transfers between devices, body(): arrived = lax.ppermute(send, 'core', SWAP)  6.34 us
    pallas_call x1, Pallas kernels, attention(): pl.pallas_call(attention_kernel, out_shape=(jax.ShapeDtypeStruct((CHIPS,...  6.14 us
    ppermute x1, starting transfers between devices, body(): other = lax.ppermute(mine, 'core', SWAP)  5.25 us
  transfers between devices with their start and end apart: 3, of which 2 were waited for; matrix products, arithmetic and copies ran while one was open for 0% of the time, Pallas kernels for 3%

profile of v8, /device:TPU:1, one launch (start us, length us, event | category | flops | bytes accessed | tf_op | source)
XLA Modules:
  0.0 117.7 jit_solution(6194381868317500239)
XLA Ops:
  0.6 0.9 broadcast_in_dim.17
  1.5 16.1 %all_to_all.25.mine_ref = bf16[8,128,256]{2,1,0:T(8,128)(2,1)S(1)} all-to-all(bf16[8,128,256]{2,1,0:T(8,128)(2,1)S(1)} %broadcast_in_dim.17), channel_id=1, replica_groups=mesh['yl'=2,'z'=16,'x'=4,'yh'=2,'core'=2] {'x','yh'}, dimensions={0} | all-to-all | bytes 1048576 | tf_op jit(solution)/shard_map/all_to_all | solution.py:419
  17.6 5.3 %collective-permute-start = (bf16[8,128,256]{2,1,0:T(8,128)(2,1)S(1)}, bf16[8,128,256]{2,1,0:T(8,128)(2,1)S(1)}, u32[]{:S(2)}, u32[]{:S(2)}) collective-permute-start(bf16[8,128,256]{2,1,0:T(8,128)(2,1)S(1)} %all_to_all.25.mine_ref), channel_id=1, source_target_pairs={{0,1},{1,0},{2,3},{3,2},{4,5},{5,4},{6,7},{7,6},{8,9},{9,8},{10,11... | collective-permute-start | bytes 1572872 | tf_op jit(solution)/shard_map/ppermute | solution.py:422
  22.9 1.1 prepare_rows.1
  24.0 0.4 collective-permute-done.other_ref
  24.4 6.1 %attention_backward.1 = (bf16[8,128,256]{2,1,0:T(8,128)(2,1)S(1)}, f32[128,1024]{1,0:T(8,128)S(1)}, bf16[1024,1024]{1,0:T(8,128)(2,1)S(1)}, bf16[1024,1024]{1,0:T(8,128)(2,1)S(1)}) custom-call(bf16[1024,128]{1,0:T(8,128)(2,1)S(1)} %get-tuple-element.18.q_rows, bf16[1024,128]{1,0:T(8,128)(2,1)S(1)} %get-tuple-element.19.go_rows, ...), custom_call_target="tpu_custom_call" | custom-call | tf_op jit(solution)/shard_map/attention_backward/pallas_call | solution.py:207
  30.6 2.3 %collective-permute-start.1 = (bf16[8,128,256]{2,1,0:T(8,128)(2,1)S(1)}, bf16[8,128,256]{2,1,0:T(8,128)(2,1)S(1)}, u32[]{:S(2)}, u32[]{:S(2)}) collective-permute-start(bf16[8,128,256]{2,1,0:T(8,128)(2,1)S(1)} %get-tuple-element.25), channel_id=1, source_target_pairs={{0,1},{1,0},{2,3},{3,2},{4,5},{5,4},{6,7},{7,6},{8,9},{9,8},{10,11... | collective-permute-start | bytes 1572872 | tf_op jit(solution)/shard_map/ppermute | solution.py:427
  32.8 1.5 %own_keys.1 = (f32[8,128,256]{2,1,0:T(8,128)S(1)}, f32[128,1024]{1,0:T(8,128)S(1)}) custom-call(bf16[1024,128]{1,0:T(8,128)(2,1)S(1)} %get-tuple-element.18.q_rows, bf16[1024,128]{1,0:T(8,128)(2,1)S(1)} %get-tuple-element.19.go_rows, bf16[8,128,256]{2,1,0:T(8,128)(2,1)S(1)} %all_to_all.25.mine_ref, f32[128,1024]{1,0:T(8,128)S(1)} %get-tuple-element.21.dq_in, ...), custom_call_target="tpu_custom_call" | custom-call | tf_op jit(solution)/shard_map/own_keys/pallas_call | solution.py:231
  34.4 0.0 copy-start
  34.4 0.0 collective-permute-done.1
  34.4 0.1 add_convert_fusion.1
  34.5 12.7 %all_to_all.26.parts_ref = bf16[8,128,256]{2,1,0:T(8,128)(2,1)S(1)} all-to-all(bf16[8,128,256]{2,1,0:T(8,128)(2,1)S(1)} %add_convert_fusion.1), channel_id=1, replica_groups=mesh['yl'=2,'z'=16,'x'=4,'yh'=2,'core'=2] {'x','yh'}, dimensions={0} | all-to-all | bytes 1048576 | tf_op jit(solution)/shard_map/all_to_all | solution.py:430
  47.3 0.0 copy-done
  47.3 0.8 weight_tiles_to_send.1
  48.1 4.1 %collective-permute-start.2 = (bf16[8,2,256,128]{3,2,1,0:T(8,128)(2,1)S(1)}, bf16[8,2,256,128]{3,2,1,0:T(8,128)(2,1)S(1)}, u32[]{:S(2)}, u32[]{:S(2)}) collective-permute-start(bf16[8,2,256,128]{3,2,1,0:T(8,128)(2,1)S(1)} %get-tuple-element.32), channel_id=1, source_target_pairs={{0,1},{1,0},{2,3},{3,2},{4,5},{5,4},{6,7},{7,6},{8,9},{9,8},{10,11... | collective-permute-start | bytes 3145736 | tf_op jit(solution)/shard_map/ppermute | solution.py:433
  52.1 1.1 weight_tiles_to_keep.1
  53.3 1.1 collective-permute-done.2
  54.4 0.3 add_convert_fusion
  54.7 19.1 %all_to_all.27.parts_ref = bf16[16,256,128]{2,1,0:T(8,128)(2,1)S(1)} all-to-all(bf16[16,256,128]{2,1,0:T(8,128)(2,1)S(1)} %bitcast.11), channel_id=1, replica_groups=mesh['yl'=2,'z'=16,'x'=4,'yh'=2,'core'=2] {'x','yl','yh'}, dimensions={0} | all-to-all | bytes 2097152 | tf_op jit(solution)/shard_map/all_to_all | solution.py:436
  73.8 1.1 owner_slots.1
  74.8 26.8 %all_to_all.28.parts_ref = bf16[16,32,128]{2,1,0:T(8,128)(2,1)S(1)} all-to-all(bf16[16,32,128]{2,1,0:T(8,128)(2,1)S(1)} %owner_slots.1), channel_id=1, replica_groups=mesh['yl'=2,'z'=16,'x'=4,'yh'=2,'core'=2] {'z'}, dimensions={0} | all-to-all | bytes 262144 | tf_op jit(solution)/shard_map/all_to_all | solution.py:438
  101.6 15.0 %all_to_all.29.pieces_ref = bf16[32,16,128]{2,1,0:T(8,128)(2,1)S(1)} all-to-all(bf16[32,16,128]{2,1,0:T(8,128)(2,1)S(1)} %owned_sum.1), channel_id=1, replica_groups=mesh['yl'=2,'z'=16,'x'=4,'yh'=2,'core'=2] {'x','yl','yh','core'}, dimensions={0} | all-to-all | bytes 262144 | tf_op jit(solution)/shard_map/all_to_all | solution.py:439
  116.6 1.0 factors.1
  (1 shorter events, 0.0 us)
Async XLA Ops:
  17.6 6.8 %collective-permute-start = (bf16[8,128,256]{2,1,0:T(8,128)(2,1)S(1)}, bf16[8,128,256]{2,1,0:T(8,128)(2,1)S(1)}, u32[]{:S(2)}, u32[]{:S(2)}) collective-permute-start(bf16[8,128,256]{2,1,0:T(8,128)(2,1)S(1)} %all_to_all.25.mine_ref), channel_id=1, source_target_pairs={{0,1},{1,0},{2,3},{3,2},{4,5},{5,4},{6,7},{7,6},{8,9},{9,8},{10,11... | collective-permute-start | bytes 1572872 | tf_op jit(solution)/shard_map/ppermute | solution.py:422
  30.6 3.8 %collective-permute-start.1 = (bf16[8,128,256]{2,1,0:T(8,128)(2,1)S(1)}, bf16[8,128,256]{2,1,0:T(8,128)(2,1)S(1)}, u32[]{:S(2)}, u32[]{:S(2)}) collective-permute-start(bf16[8,128,256]{2,1,0:T(8,128)(2,1)S(1)} %get-tuple-element.25), channel_id=1, source_target_pairs={{0,1},{1,0},{2,3},{3,2},{4,5},{5,4},{6,7},{7,6},{8,9},{9,8},{10,11... | collective-permute-start | bytes 1572872 | tf_op jit(solution)/shard_map/ppermute | solution.py:427
  34.4 12.9 %copy-start = (bf16[1,128,8192]{2,1,0:T(8,128)(2,1)S(1)}, bf16[1,128,8192]{2,1,0:T(8,128)(2,1)}, u32[]{:S(2)}) copy-start(bf16[1,128,8192]{2,1,0:T(8,128)(2,1)} %param.6) | copy-start | bytes 6291460
  48.1 6.3 %collective-permute-start.2 = (bf16[8,2,256,128]{3,2,1,0:T(8,128)(2,1)S(1)}, bf16[8,2,256,128]{3,2,1,0:T(8,128)(2,1)S(1)}, u32[]{:S(2)}, u32[]{:S(2)}) collective-permute-start(bf16[8,2,256,128]{3,2,1,0:T(8,128)(2,1)S(1)} %get-tuple-element.32), channel_id=1, source_target_pairs={{0,1},{1,0},{2,3},{3,2},{4,5},{5,4},{6,7},{7,6},{8,9},{9,8},{10,11... | collective-permute-start | bytes 3145736 | tf_op jit(solution)/shard_map/ppermute | solution.py:433

commit v9 on v8

--- a/solution.py
+++ b/solution.py
@@ -83,19 +83,22 @@
     return ref[:, :, part * HD : (part + 1) * HD].reshape(HALF, HD)
 
 
-def products(w, ds, q_rows, go_rows, ref):
+def products(w, ds, q_rows, go_rows):
     dk = jnp.dot(ds[...], q_rows[...], preferred_element_type=F32) * SCALE
     dv = jnp.dot(w[...], go_rows[...], preferred_element_type=F32)
-    dq_t = lax.dot_general(
+    return dk.reshape(CHIPS, ROWS, HD), dv.reshape(CHIPS, ROWS, HD)
+
+
+def query_part(ds, ref):
+    return lax.dot_general(
         side_of(ref, 0), ds[...], (((0,), (0,)), ((), ())), preferred_element_type=F32
     )
-    return dk.reshape(CHIPS, ROWS, HD), dv.reshape(CHIPS, ROWS, HD), dq_t
 
 
 def attention_kernel(
     q_rows, go_rows, low_ref, mine_ref, other_ref,
-    send_ref, dq_t, w_mine, ds_mine,
-    w_other, ds_other, probs, top, total, delta,
+    send_ref, w_mine, ds_mine, ds_other,
+    w_other, probs, top, total, delta,
 ):
     core = lax.axis_index("core")
     first = first_position()
@@ -151,17 +154,16 @@
             w_ref[:, cols] = w.astype(BF16)
             pg = against(values, go_rows, cols)
             ds_ref[:, cols] = (w * (pg - delta[0:1, cols])).astype(BF16)
-    dk, dv, dq = products(w_other, ds_other, q_rows, go_rows, other_ref)
+    dk, dv = products(w_other, ds_other, q_rows, go_rows)
     send_ref[:, :, :HD] = dk.astype(BF16)
     send_ref[:, :, HD:] = dv.astype(BF16)
-    dq_t[...] = dq
-
-
-def own_kernel(q_rows, go_rows, mine_ref, dq_in, w_mine, ds_mine, keep_ref, dq_t):
-    dk, dv, dq = products(w_mine, ds_mine, q_rows, go_rows, mine_ref)
+
+
+def own_kernel(q_rows, go_rows, mine_ref, w_mine, ds_mine, keep_ref, dq_t):
+    dk, dv = products(w_mine, ds_mine, q_rows, go_rows)
     keep_ref[:, :, :HD] = dk
     keep_ref[:, :, HD:] = dv
-    dq_t[...] = dq_in[...] + dq
+    dq_t[...] = query_part(ds_mine, mine_ref)
 
 
 VMEM = pl.BlockSpec(memory_space=pltpu.VMEM)
@@ -208,14 +210,13 @@
         attention_kernel,
         out_shape=(
             jax.ShapeDtypeStruct((CHIPS, ROWS, 2 * HD), BF16),
-            jax.ShapeDtypeStruct((HD, wide), F32),
+            half,
             half,
             half,
         ),
         in_specs=[VMEM] * 5,
         out_specs=(VMEM,) * 4,
         scratch_shapes=[
-            pltpu.VMEM((HALF, wide), BF16),
             pltpu.VMEM((HALF, wide), BF16),
             pltpu.VMEM((SEQ, wide), F32),
             pltpu.VMEM((8, wide), F32),
@@ -227,18 +228,18 @@
     )(q_rows, go_rows, row_low, mine, other)
 
 
-def own_keys(q_rows, go_rows, mine, dq_t, w, ds):
+def own_keys(q_rows, go_rows, mine, w, ds):
     return pl.pallas_call(
         own_kernel,
         out_shape=(
             jax.ShapeDtypeStruct((CHIPS, ROWS, 2 * HD), F32),
             jax.ShapeDtypeStruct((HD, HEADS * HD), F32),
         ),
-        in_specs=[VMEM] * 6,
+        in_specs=[VMEM] * 5,
         out_specs=(VMEM, VMEM),
         compiler_params=limit(12),
         name="own_keys",
-    )(q_rows, go_rows, mine, dq_t, w, ds)
+    )(q_rows, go_rows, mine, w, ds)
 
 
 def low_half(shape, axis):
@@ -270,27 +271,36 @@
         out_ref[:, 1, rows, :] = jnp.concatenate(odds, axis=1).astype(out_ref.dtype)
 
 
-def weight_send_kernel(parts_ref, hidden_ref, kv_ref, k_ref, out_ref):
+def position_sums(parts_ref, part):
+    return jnp.sum(parts_ref[:, :, part * HD : (part + 1) * HD].astype(F32), axis=0).astype(BF16)
+
+
+def weight_send_kernel(parts_ref, hidden_ref, low_ref, k_ref, out_ref):
     core = lax.axis_index("core")
-    low = jnp.sum(parts_ref[...].astype(F32), axis=0).astype(BF16)
-    kv_ref[...] = low
-    first, second = halves(low[:, :HD].astype(F32))
+    low = position_sums(parts_ref, 0)
+    low_ref[...] = low
+    first, second = halves(low.astype(F32))
     k_ref[...] = jnp.where(core == 0, first, second).astype(BF16)
     half_tiles(jnp.where(core == 0, second, first).astype(BF16), hidden_ref, out_ref)
 
 
-def weight_keep_kernel(k_ref, hidden_ref, dq_t, out_ref, dq_ref):
+def weight_keep_kernel(
+    k_ref, hidden_ref, dq_t, ds_other, other_ref, low_ref, parts_ref, out_ref, dq_ref, kv_ref, dq_all
+):
+    kv_ref[:, :HD] = low_ref[...]
+    kv_ref[:, HD:] = position_sums(parts_ref, 1)
     half_tiles(k_ref[...], hidden_ref, out_ref)
+    dq_all[...] = dq_t[...] + query_part(ds_other, other_ref)
     for h in range(HEADS):
         cols = pl.ds(h * HD, HD)
-        dq_ref[:, cols] = (dq_t[:, cols].T * SCALE).astype(BF16)
+        dq_ref[:, cols] = (dq_all[:, cols].T * SCALE).astype(BF16)
 
 
 def weight_send(parts, hidden):
     return pl.pallas_call(
         weight_send_kernel,
         out_shape=(
-            jax.ShapeDtypeStruct((ROWS, 2 * HD), BF16),
+            jax.ShapeDtypeStruct((ROWS, HD), BF16),
             jax.ShapeDtypeStruct((HD // 2, ROWS), BF16),
             jax.ShapeDtypeStruct((PLANE // 2, 2, TILES * 4, TILE), BF16),
         ),
@@ -301,18 +311,20 @@
     )(parts, hidden)
 
 
-def weight_keep(k_t, hidden, dq_t):
+def weight_keep(k_t, hidden, dq_t, ds_other, other, low, parts):
     return pl.pallas_call(
         weight_keep_kernel,
         out_shape=(
             jax.ShapeDtypeStruct((PLANE // 2, 2, TILES * 4, TILE), F32),
             jax.ShapeDtypeStruct((ROWS, HEADS * HD), BF16),
+            jax.ShapeDtypeStruct((ROWS, 2 * HD), BF16),
         ),
-        in_specs=[VMEM] * 3,
-        out_specs=(VMEM, VMEM),
+        in_specs=[VMEM] * 7,
+        out_specs=(VMEM,) * 3,
+        scratch_shapes=[pltpu.VMEM((HD, HEADS * HD), F32)],
         compiler_params=limit(12),
         name="weight_tiles_to_keep",
-    )(k_t, hidden, dq_t)
+    )(k_t, hidden, dq_t, ds_other, other, low, parts)
 
 
 def owner_kernel(place_ref, parts_ref, out_ref, sums, placed):
@@ -423,15 +435,15 @@
     q_rows, go_rows, row_low, place = prepare(
         lengths, owner.reshape(1, TILES), query[0], grad_out[0]
     )
-    send, dq_t, w, ds = attention(q_rows, go_rows, row_low, mine, other)
+    send, w, ds, ds_other = attention(q_rows, go_rows, row_low, mine, other)
     arrived = lax.ppermute(send, "core", SWAP)
-    keep, dq_t = own_keys(q_rows, go_rows, mine, dq_t, w, ds)
+    keep, dq_t = own_keys(q_rows, go_rows, mine, w, ds)
     dkv = (keep + arrived.astype(F32)).astype(BF16)
     dkv = lax.all_to_all(dkv, CHIP_AXES, 0, 0, tiled=True)
     hidden = hidden_in[0]
-    grad_kv, k_t, send = weight_send(dkv, hidden)
+    low, k_t, send = weight_send(dkv, hidden)
     arrived = lax.ppermute(send, "core", SWAP)
-    keep, grad_query = weight_keep(k_t, hidden, dq_t)
+    keep, grad_query, grad_kv = weight_keep(k_t, hidden, dq_t, ds_other, other, low, dkv)
     wg = (keep + arrived.astype(F32)).astype(BF16).reshape(PLANE, TILES * 4, TILE)
     wg = lax.all_to_all(wg, PLANE_AXES, 0, 0, tiled=True)
     outgoing = to_owners(place, wg)

time: 118 us -> 118 us (level)
  transfers between devices with their start and end apart: 3 -> 3, of which waited for: 2 -> 2; matrix products, arithmetic and copies ran while one was open for 0% -> 0% of each run, Pallas kernels for 3% -> 4%
where the time goes in v9:
time: 118 us; the launch traced here: 117 us
  blocking collectives  89.7 us (76%)
  Pallas kernels  12.7 us (11%)
  starting transfers between devices  11.6 us (10%)
    all_to_all x1, blocking collectives, body(): incoming = lax.all_to_all(outgoing, 'z', 0, 0, tiled=True)  26.8 us
    all_to_all x1, blocking collectives, body(): wg = lax.all_to_all(wg, PLANE_AXES, 0, 0, tiled=True)  19.1 us
    all_to_all x1, blocking collectives, body(): lax.all_to_all(jnp.broadcast_to(key_value, (CHIPS, ROWS, 2 * HD)), CHIP_A...  16.1 us
    all_to_all x1, blocking collectives, body(): lax.all_to_all(owned_sum(incoming), PLANE_AXES + ('core',), 0, 0, tiled=T...  15 us
    all_to_all x1, blocking collectives, body(): dkv = lax.all_to_all(dkv, CHIP_AXES, 0, 0, tiled=True)  12.7 us
    ppermute x2, starting transfers between devices, body(): arrived = lax.ppermute(send, 'core', SWAP)  6.38 us
    pallas_call x1, Pallas kernels, attention(): pl.pallas_call(attention_kernel, out_shape=(jax.ShapeDtypeStruct((CHIPS,...  5.86 us
    ppermute x1, starting transfers between devices, body(): other = lax.ppermute(mine, 'core', SWAP)  5.25 us
  transfers between devices with their start and end apart: 3, of which 2 were waited for; matrix products, arithmetic and copies ran while one was open for 0% of the time, Pallas kernels for 4%

profile of v9, /device:TPU:1, one launch (start us, length us, event | category | flops | bytes accessed | tf_op | source)
XLA Modules:
  0.0 117.2 jit_solution(7204706723870381459)
XLA Ops:
  0.6 0.9 broadcast_in_dim.17
  1.5 16.1 %all_to_all.25.mine_ref = bf16[8,128,256]{2,1,0:T(8,128)(2,1)S(1)} all-to-all(bf16[8,128,256]{2,1,0:T(8,128)(2,1)S(1)} %broadcast_in_dim.17), channel_id=1, replica_groups=mesh['yl'=2,'z'=16,'x'=4,'yh'=2,'core'=2] {'x','yh'}, dimensions={0} | all-to-all | bytes 1048576 | tf_op jit(solution)/shard_map/all_to_all | solution.py:431
  17.6 5.3 %collective-permute-start = (bf16[8,128,256]{2,1,0:T(8,128)(2,1)S(1)}, bf16[8,128,256]{2,1,0:T(8,128)(2,1)S(1)}, u32[]{:S(2)}, u32[]{:S(2)}) collective-permute-start(bf16[8,128,256]{2,1,0:T(8,128)(2,1)S(1)} %all_to_all.25.mine_ref), channel_id=1, source_target_pairs={{0,1},{1,0},{2,3},{3,2},{4,5},{5,4},{6,7},{7,6},{8,9},{9,8},{10,11... | collective-permute-start | bytes 1572872 | tf_op jit(solution)/shard_map/ppermute | solution.py:434
  22.9 1.1 prepare_rows.1
  24.0 0.4 collective-permute-done.other_ref
  24.4 5.9 %attention_backward.1 = (bf16[8,128,256]{2,1,0:T(8,128)(2,1)S(1)}, bf16[1024,1024]{1,0:T(8,128)(2,1)S(1)}, bf16[1024,1024]{1,0:T(8,128)(2,1)S(1)}, bf16[1024,1024]{1,0:T(8,128)(2,1)S(1)}) custom-call(bf16[1024,128]{1,0:T(8,128)(2,1)S(1)} %get-tuple-element.19.q_rows, bf16[1024,128]{1,0:T(8,128)(2,1)S(1)} %get-tuple-element.20.go_rows, ...), custom_call_target="tpu_custom_call" | custom-call | tf_op jit(solution)/shard_map/attention_backward/pallas_call | solution.py:209
  30.3 2.3 %collective-permute-start.1 = (bf16[8,128,256]{2,1,0:T(8,128)(2,1)S(1)}, bf16[8,128,256]{2,1,0:T(8,128)(2,1)S(1)}, u32[]{:S(2)}, u32[]{:S(2)}) collective-permute-start(bf16[8,128,256]{2,1,0:T(8,128)(2,1)S(1)} %get-tuple-element.25), channel_id=1, source_target_pairs={{0,1},{1,0},{2,3},{3,2},{4,5},{5,4},{6,7},{7,6},{8,9},{9,8},{10,11... | collective-permute-start | bytes 1572872 | tf_op jit(solution)/shard_map/ppermute | solution.py:439
  32.6 1.5 %own_keys.1 = (f32[8,128,256]{2,1,0:T(8,128)S(1)}, f32[128,1024]{1,0:T(8,128)S(1)}) custom-call(bf16[1024,128]{1,0:T(8,128)(2,1)S(1)} %get-tuple-element.19.q_rows, bf16[1024,128]{1,0:T(8,128)(2,1)S(1)} %get-tuple-element.20.go_rows, bf16[8,128,256]{2,1,0:T(8,128)(2,1)S(1)} %all_to_all.25.mine_ref, bf16[1024,1024]{1,0:T(8,128)(2,1)S(1)} %get-tuple-element.22.w_mine, ...), custom_call_target="tpu_custom_call" | custom-call | tf_op jit(solution)/shard_map/own_keys/pallas_call | solution.py:232
  34.1 0.0 copy-start
  34.1 0.0 collective-permute-done.1
  34.1 0.2 add_convert_fusion.1
  34.3 12.7 %all_to_all.26.parts_ref = bf16[8,128,256]{2,1,0:T(8,128)(2,1)S(1)} all-to-all(bf16[8,128,256]{2,1,0:T(8,128)(2,1)S(1)} %add_convert_fusion.1), channel_id=1, replica_groups=mesh['yl'=2,'z'=16,'x'=4,'yh'=2,'core'=2] {'x','yh'}, dimensions={0} | all-to-all | bytes 1048576 | tf_op jit(solution)/shard_map/all_to_all | solution.py:442
  47.0 0.0 copy-done
  47.0 0.5 weight_tiles_to_send.1
  47.5 4.1 %collective-permute-start.2 = (bf16[8,2,256,128]{3,2,1,0:T(8,128)(2,1)S(1)}, bf16[8,2,256,128]{3,2,1,0:T(8,128)(2,1)S(1)}, u32[]{:S(2)}, u32[]{:S(2)}) collective-permute-start(bf16[8,2,256,128]{3,2,1,0:T(8,128)(2,1)S(1)} %get-tuple-element.34), channel_id=1, source_target_pairs={{0,1},{1,0},{2,3},{3,2},{4,5},{5,4},{6,7},{7,6},{8,9},{9,8},{10,11... | collective-permute-start | bytes 3145736 | tf_op jit(solution)/shard_map/ppermute | solution.py:445
  51.6 1.6 %weight_tiles_to_keep.1 = (f32[8,2,256,128]{3,2,1,0:T(8,128)S(1)}, bf16[128,1024]{1,0:T(8,128)(2,1)}, bf16[128,256]{1,0:T(8,128)(2,1)}) custom-call(bf16[64,128]{1,0:T(8,128)(2,1)S(1)} %get-tuple-element.26.k_ref, bf16[128,8192]{1,0:T(8,128)(2,1)S(1)} %bitcast.10, f32[128,1024]{1,0:T(8,128)S(1)} %get-tuple-element.27.dq_t, ...), custom_call_target="tpu_custom_call" | custom-call | tf_op jit(solution)/shard_map/weight_tiles_to_keep/pallas_call | solution.py:315
  53.2 0.7 collective-permute-done.2
  53.9 0.3 add_convert_fusion
  54.2 19.1 %all_to_all.27.parts_ref = bf16[16,256,128]{2,1,0:T(8,128)(2,1)S(1)} all-to-all(bf16[16,256,128]{2,1,0:T(8,128)(2,1)S(1)} %bitcast.11), channel_id=1, replica_groups=mesh['yl'=2,'z'=16,'x'=4,'yh'=2,'core'=2] {'x','yl','yh'}, dimensions={0} | all-to-all | bytes 2097152 | tf_op jit(solution)/shard_map/all_to_all | solution.py:448
  73.3 1.1 owner_slots.1
  74.4 26.8 %all_to_all.28.parts_ref = bf16[16,32,128]{2,1,0:T(8,128)(2,1)S(1)} all-to-all(bf16[16,32,128]{2,1,0:T(8,128)(2,1)S(1)} %owner_slots.1), channel_id=1, replica_groups=mesh['yl'=2,'z'=16,'x'=4,'yh'=2,'core'=2] {'z'}, dimensions={0} | all-to-all | bytes 262144 | tf_op jit(solution)/shard_map/all_to_all | solution.py:450
  101.2 15.0 %all_to_all.29.pieces_ref = bf16[32,16,128]{2,1,0:T(8,128)(2,1)S(1)} all-to-all(bf16[32,16,128]{2,1,0:T(8,128)(2,1)S(1)} %owned_sum.1), channel_id=1, replica_groups=mesh['yl'=2,'z'=16,'x'=4,'yh'=2,'core'=2] {'x','yl','yh','core'}, dimensions={0} | all-to-all | bytes 262144 | tf_op jit(solution)/shard_map/all_to_all | solution.py:451
  116.2 1.0 factors.1
  (1 shorter events, 0.0 us)
Async XLA Ops:
  17.6 6.8 %collective-permute-start = (bf16[8,128,256]{2,1,0:T(8,128)(2,1)S(1)}, bf16[8,128,256]{2,1,0:T(8,128)(2,1)S(1)}, u32[]{:S(2)}, u32[]{:S(2)}) collective-permute-start(bf16[8,128,256]{2,1,0:T(8,128)(2,1)S(1)} %all_to_all.25.mine_ref), channel_id=1, source_target_pairs={{0,1},{1,0},{2,3},{3,2},{4,5},{5,4},{6,7},{7,6},{8,9},{9,8},{10,11... | collective-permute-start | bytes 1572872 | tf_op jit(solution)/shard_map/ppermute | solution.py:434
  30.3 3.8 %collective-permute-start.1 = (bf16[8,128,256]{2,1,0:T(8,128)(2,1)S(1)}, bf16[8,128,256]{2,1,0:T(8,128)(2,1)S(1)}, u32[]{:S(2)}, u32[]{:S(2)}) collective-permute-start(bf16[8,128,256]{2,1,0:T(8,128)(2,1)S(1)} %get-tuple-element.25), channel_id=1, source_target_pairs={{0,1},{1,0},{2,3},{3,2},{4,5},{5,4},{6,7},{7,6},{8,9},{9,8},{10,11... | collective-permute-start | bytes 1572872 | tf_op jit(solution)/shard_map/ppermute | solution.py:439
  34.1 12.9 %copy-start = (bf16[1,128,8192]{2,1,0:T(8,128)(2,1)S(1)}, bf16[1,128,8192]{2,1,0:T(8,128)(2,1)}, u32[]{:S(2)}) copy-start(bf16[1,128,8192]{2,1,0:T(8,128)(2,1)} %param.6) | copy-start | bytes 6291460
  47.5 6.4 %collective-permute-start.2 = (bf16[8,2,256,128]{3,2,1,0:T(8,128)(2,1)S(1)}, bf16[8,2,256,128]{3,2,1,0:T(8,128)(2,1)S(1)}, u32[]{:S(2)}, u32[]{:S(2)}) collective-permute-start(bf16[8,2,256,128]{3,2,1,0:T(8,128)(2,1)S(1)} %get-tuple-element.34), channel_id=1, source_target_pairs={{0,1},{1,0},{2,3},{3,2},{4,5},{5,4},{6,7},{7,6},{8,9},{9,8},{10,11... | collective-permute-start | bytes 3145736 | tf_op jit(solution)/shard_map/ppermute | solution.py:445

commit v10 on v9

--- a/solution.py
+++ b/solution.py
@@ -333,14 +333,15 @@
     sums[:rows, :] = own
     sums[rows:, :] = pltpu.roll(own.reshape(rows // 8, 8, TILE), 4, axis=1).reshape(rows, TILE)
     placed[...] = jnp.zeros(placed.shape, F32)
-    low = low_half((8, TILE), 0)
     for t in range(TILES):
         place = place_ref[0, t]
-        half = place & 1
-        at = pl.ds(pl.multiple_of((place >> 1) * 8, 8), 8)
-        source = pl.multiple_of((half ^ (t & 1)) * rows + (t // 2) * 8, 8)
-        placed[at, :] = jnp.where(low == (half == 0), sums[pl.ds(source, 8), :], placed[at, :])
-    out_ref[...] = placed[...].astype(BF16).reshape(out_ref.shape)
+        at = pl.ds(pl.multiple_of(place * 8, 8), 8)
+        source = pl.multiple_of(((place & 1) ^ (t & 1)) * rows + (t // 2) * 8, 8)
+        placed[at, :] = sums[pl.ds(source, 8), :]
+    pairs = placed[...].reshape(N_DP * CAP // 2, 2, 8, TILE)
+    low = low_half((N_DP * CAP // 2, 8, TILE), 1)
+    merged = jnp.where(low, pairs[:, 0], pairs[:, 1])
+    out_ref[...] = merged.reshape(out_ref.shape).astype(BF16)
 
 
 def to_owners(place, parts):
@@ -351,7 +352,7 @@
         out_specs=VMEM,
         scratch_shapes=[
             pltpu.VMEM((2 * TILES * 4, TILE), F32),
-            pltpu.VMEM((N_Z * OWNED, TILE), F32),
+            pltpu.VMEM((N_DP * CAP * 8, TILE), F32),
         ],
         compiler_params=limit(12),
         name="owner_slots",

time: 118 us -> 117 us (level)
  no operation moved by 1% of the time
where the time goes in v10:
time: 117 us
  blocking collectives  89.7 us (77%)
  Pallas kernels  12.6 us (11%)
  starting transfers between devices  11.6 us (10%)
    all_to_all x1, blocking collectives, body(): incoming = lax.all_to_all(outgoing, 'z', 0, 0, tiled=True)  26.8 us
    all_to_all x1, blocking collectives, body(): wg = lax.all_to_all(wg, PLANE_AXES, 0, 0, tiled=True)  19.1 us
    all_to_all x1, blocking collectives, body(): lax.all_to_all(jnp.broadcast_to(key_value, (CHIPS, ROWS, 2 * HD)), CHIP_A...  16.1 us
    all_to_all x1, blocking collectives, body(): lax.all_to_all(owned_sum(incoming), PLANE_AXES + ('core',), 0, 0, tiled=T...  15 us
    all_to_all x1, blocking collectives, body(): dkv = lax.all_to_all(dkv, CHIP_AXES, 0, 0, tiled=True)  12.7 us
    ppermute x2, starting transfers between devices, body(): arrived = lax.ppermute(send, 'core', SWAP)  6.38 us
    pallas_call x1, Pallas kernels, attention(): pl.pallas_call(attention_kernel, out_shape=(jax.ShapeDtypeStruct((CHIPS,...  5.86 us
    ppermute x1, starting transfers between devices, body(): other = lax.ppermute(mine, 'core', SWAP)  5.25 us
  transfers between devices with their start and end apart: 3, of which 2 were waited for; matrix products, arithmetic and copies ran while one was open for 0% of the time, Pallas kernels for 4%

profile of v10, /device:TPU:1, one launch (start us, length us, event | category | flops | bytes accessed | tf_op | source)
XLA Modules:
  0.0 117.1 jit_solution(4653357418014200589)
XLA Ops:
  0.6 0.9 broadcast_in_dim.17
  1.5 16.1 %all_to_all.25.mine_ref = bf16[8,128,256]{2,1,0:T(8,128)(2,1)S(1)} all-to-all(bf16[8,128,256]{2,1,0:T(8,128)(2,1)S(1)} %broadcast_in_dim.17), channel_id=1, replica_groups=mesh['yl'=2,'z'=16,'x'=4,'yh'=2,'core'=2] {'x','yh'}, dimensions={0} | all-to-all | bytes 1048576 | tf_op jit(solution)/shard_map/all_to_all | solution.py:432
  17.6 5.3 %collective-permute-start = (bf16[8,128,256]{2,1,0:T(8,128)(2,1)S(1)}, bf16[8,128,256]{2,1,0:T(8,128)(2,1)S(1)}, u32[]{:S(2)}, u32[]{:S(2)}) collective-permute-start(bf16[8,128,256]{2,1,0:T(8,128)(2,1)S(1)} %all_to_all.25.mine_ref), channel_id=1, source_target_pairs={{0,1},{1,0},{2,3},{3,2},{4,5},{5,4},{6,7},{7,6},{8,9},{9,8},{10,11... | collective-permute-start | bytes 1572872 | tf_op jit(solution)/shard_map/ppermute | solution.py:435
  22.9 1.1 prepare_rows.1
  24.0 0.4 collective-permute-done.other_ref
  24.4 5.9 %attention_backward.1 = (bf16[8,128,256]{2,1,0:T(8,128)(2,1)S(1)}, bf16[1024,1024]{1,0:T(8,128)(2,1)S(1)}, bf16[1024,1024]{1,0:T(8,128)(2,1)S(1)}, bf16[1024,1024]{1,0:T(8,128)(2,1)S(1)}) custom-call(bf16[1024,128]{1,0:T(8,128)(2,1)S(1)} %get-tuple-element.19.q_rows, bf16[1024,128]{1,0:T(8,128)(2,1)S(1)} %get-tuple-element.20.go_rows, ...), custom_call_target="tpu_custom_call" | custom-call | tf_op jit(solution)/shard_map/attention_backward/pallas_call | solution.py:209
  30.3 2.3 %collective-permute-start.1 = (bf16[8,128,256]{2,1,0:T(8,128)(2,1)S(1)}, bf16[8,128,256]{2,1,0:T(8,128)(2,1)S(1)}, u32[]{:S(2)}, u32[]{:S(2)}) collective-permute-start(bf16[8,128,256]{2,1,0:T(8,128)(2,1)S(1)} %get-tuple-element.25), channel_id=1, source_target_pairs={{0,1},{1,0},{2,3},{3,2},{4,5},{5,4},{6,7},{7,6},{8,9},{9,8},{10,11... | collective-permute-start | bytes 1572872 | tf_op jit(solution)/shard_map/ppermute | solution.py:440
  32.6 1.5 %own_keys.1 = (f32[8,128,256]{2,1,0:T(8,128)S(1)}, f32[128,1024]{1,0:T(8,128)S(1)}) custom-call(bf16[1024,128]{1,0:T(8,128)(2,1)S(1)} %get-tuple-element.19.q_rows, bf16[1024,128]{1,0:T(8,128)(2,1)S(1)} %get-tuple-element.20.go_rows, bf16[8,128,256]{2,1,0:T(8,128)(2,1)S(1)} %all_to_all.25.mine_ref, bf16[1024,1024]{1,0:T(8,128)(2,1)S(1)} %get-tuple-element.22.w_mine, ...), custom_call_target="tpu_custom_call" | custom-call | tf_op jit(solution)/shard_map/own_keys/pallas_call | solution.py:232
  34.1 0.0 copy-start
  34.1 0.0 collective-permute-done.1
  34.1 0.2 add_convert_fusion.1
  34.3 12.7 %all_to_all.26.parts_ref = bf16[8,128,256]{2,1,0:T(8,128)(2,1)S(1)} all-to-all(bf16[8,128,256]{2,1,0:T(8,128)(2,1)S(1)} %add_convert_fusion.1), channel_id=1, replica_groups=mesh['yl'=2,'z'=16,'x'=4,'yh'=2,'core'=2] {'x','yh'}, dimensions={0} | all-to-all | bytes 1048576 | tf_op jit(solution)/shard_map/all_to_all | solution.py:443
  47.0 0.0 copy-done
  47.0 0.5 weight_tiles_to_send.1
  47.5 4.1 %collective-permute-start.2 = (bf16[8,2,256,128]{3,2,1,0:T(8,128)(2,1)S(1)}, bf16[8,2,256,128]{3,2,1,0:T(8,128)(2,1)S(1)}, u32[]{:S(2)}, u32[]{:S(2)}) collective-permute-start(bf16[8,2,256,128]{3,2,1,0:T(8,128)(2,1)S(1)} %get-tuple-element.34), channel_id=1, source_target_pairs={{0,1},{1,0},{2,3},{3,2},{4,5},{5,4},{6,7},{7,6},{8,9},{9,8},{10,11... | collective-permute-start | bytes 3145736 | tf_op jit(solution)/shard_map/ppermute | solution.py:446
  51.6 1.6 %weight_tiles_to_keep.1 = (f32[8,2,256,128]{3,2,1,0:T(8,128)S(1)}, bf16[128,1024]{1,0:T(8,128)(2,1)}, bf16[128,256]{1,0:T(8,128)(2,1)}) custom-call(bf16[64,128]{1,0:T(8,128)(2,1)S(1)} %get-tuple-element.26.k_ref, bf16[128,8192]{1,0:T(8,128)(2,1)S(1)} %bitcast.10, f32[128,1024]{1,0:T(8,128)S(1)} %get-tuple-element.27.dq_t, ...), custom_call_target="tpu_custom_call" | custom-call | tf_op jit(solution)/shard_map/weight_tiles_to_keep/pallas_call | solution.py:315
  53.2 0.7 collective-permute-done.2
  53.9 0.3 add_convert_fusion
  54.2 19.1 %all_to_all.27.parts_ref = bf16[16,256,128]{2,1,0:T(8,128)(2,1)S(1)} all-to-all(bf16[16,256,128]{2,1,0:T(8,128)(2,1)S(1)} %bitcast.11), channel_id=1, replica_groups=mesh['yl'=2,'z'=16,'x'=4,'yh'=2,'core'=2] {'x','yl','yh'}, dimensions={0} | all-to-all | bytes 2097152 | tf_op jit(solution)/shard_map/all_to_all | solution.py:449
  73.3 0.9 owner_slots.1
  74.2 26.8 %all_to_all.28.parts_ref = bf16[16,32,128]{2,1,0:T(8,128)(2,1)S(1)} all-to-all(bf16[16,32,128]{2,1,0:T(8,128)(2,1)S(1)} %owner_slots.1), channel_id=1, replica_groups=mesh['yl'=2,'z'=16,'x'=4,'yh'=2,'core'=2] {'z'}, dimensions={0} | all-to-all | bytes 262144 | tf_op jit(solution)/shard_map/all_to_all | solution.py:451
  101.0 15.0 %all_to_all.29.pieces_ref = bf16[32,16,128]{2,1,0:T(8,128)(2,1)S(1)} all-to-all(bf16[32,16,128]{2,1,0:T(8,128)(2,1)S(1)} %owned_sum.1), channel_id=1, replica_groups=mesh['yl'=2,'z'=16,'x'=4,'yh'=2,'core'=2] {'x','yl','yh','core'}, dimensions={0} | all-to-all | bytes 262144 | tf_op jit(solution)/shard_map/all_to_all | solution.py:452
  116.0 1.0 factors.1
  (1 shorter events, 0.0 us)
Async XLA Ops:
  17.6 6.8 %collective-permute-start = (bf16[8,128,256]{2,1,0:T(8,128)(2,1)S(1)}, bf16[8,128,256]{2,1,0:T(8,128)(2,1)S(1)}, u32[]{:S(2)}, u32[]{:S(2)}) collective-permute-start(bf16[8,128,256]{2,1,0:T(8,128)(2,1)S(1)} %all_to_all.25.mine_ref), channel_id=1, source_target_pairs={{0,1},{1,0},{2,3},{3,2},{4,5},{5,4},{6,7},{7,6},{8,9},{9,8},{10,11... | collective-permute-start | bytes 1572872 | tf_op jit(solution)/shard_map/ppermute | solution.py:435
  30.3 3.8 %collective-permute-start.1 = (bf16[8,128,256]{2,1,0:T(8,128)(2,1)S(1)}, bf16[8,128,256]{2,1,0:T(8,128)(2,1)S(1)}, u32[]{:S(2)}, u32[]{:S(2)}) collective-permute-start(bf16[8,128,256]{2,1,0:T(8,128)(2,1)S(1)} %get-tuple-element.25), channel_id=1, source_target_pairs={{0,1},{1,0},{2,3},{3,2},{4,5},{5,4},{6,7},{7,6},{8,9},{9,8},{10,11... | collective-permute-start | bytes 1572872 | tf_op jit(solution)/shard_map/ppermute | solution.py:440
  34.1 12.9 %copy-start = (bf16[1,128,8192]{2,1,0:T(8,128)(2,1)S(1)}, bf16[1,128,8192]{2,1,0:T(8,128)(2,1)}, u32[]{:S(2)}) copy-start(bf16[1,128,8192]{2,1,0:T(8,128)(2,1)} %param.6) | copy-start | bytes 6291460
  47.5 6.4 %collective-permute-start.2 = (bf16[8,2,256,128]{3,2,1,0:T(8,128)(2,1)S(1)}, bf16[8,2,256,128]{3,2,1,0:T(8,128)(2,1)S(1)}, u32[]{:S(2)}, u32[]{:S(2)}) collective-permute-start(bf16[8,2,256,128]{3,2,1,0:T(8,128)(2,1)S(1)} %get-tuple-element.34), channel_id=1, source_target_pairs={{0,1},{1,0},{2,3},{3,2},{4,5},{5,4},{6,7},{7,6},{8,9},{9,8},{10,11... | collective-permute-start | bytes 3145736 | tf_op jit(solution)/shard_map/ppermute | solution.py:446

commit v11 on v10

--- a/solution.py
+++ b/solution.py
@@ -178,6 +178,28 @@
     return pltpu.CompilerParams(vmem_limit_bytes=mib * 1024 * 1024)
 
 
+def spread_kernel(kv_hbm, out_ref, sems):
+    copies = [
+        pltpu.make_async_copy(kv_hbm.at[0], out_ref.at[i], sems.at[i]) for i in range(CHIPS)
+    ]
+    for copy in copies:
+        copy.start()
+    for copy in copies:
+        copy.wait()
+
+
+def spread(key_value):
+    return pl.pallas_call(
+        spread_kernel,
+        out_shape=jax.ShapeDtypeStruct((CHIPS, ROWS, 2 * HD), BF16),
+        in_specs=[pl.BlockSpec(memory_space=pltpu.HBM)],
+        out_specs=VMEM,
+        scratch_shapes=[pltpu.SemaphoreType.DMA((CHIPS,))],
+        compiler_params=limit(8),
+        name="spread_kv",
+    )(in_hbm(key_value))
+
+
 def prepare(lengths, owner, query, grad_out):
     hbm = pl.BlockSpec(memory_space=pltpu.HBM)
     wide = HEADS * HD
@@ -430,7 +452,7 @@
 
 def body(hidden_in, query, key_value, grad_out, lengths, owner):
     mine = lax.all_to_all(
-        jnp.broadcast_to(key_value, (CHIPS, ROWS, 2 * HD)), CHIP_AXES, 0, 0, tiled=True
+        spread(key_value), CHIP_AXES, 0, 0, tiled=True
     )
     other = lax.ppermute(mine, "core", SWAP)
     q_rows, go_rows, row_low, place = prepare(

time: 117 us -> 118 us (level)
  Pallas kernels: 12.6 us -> 13.9 us
    pallas_call x0 -> x1, Pallas kernels: none -> 1.3 us  [spread(): pl.pallas_call(spread_kernel, out_shape=jax.ShapeDtypeStruct((CHIPS, ROWS...]
where the time goes in v11:
time: 118 us; the launch traced here: 117 us
  blocking collectives  89.7 us (76%)
  Pallas kernels  13.9 us (12%)
  starting transfers between devices  11.6 us (10%)
    all_to_all x1, blocking collectives, body(): incoming = lax.all_to_all(outgoing, 'z', 0, 0, tiled=True)  26.8 us
    all_to_all x1, blocking collectives, body(): wg = lax.all_to_all(wg, PLANE_AXES, 0, 0, tiled=True)  19.1 us
    all_to_all x1, blocking collectives, body(): mine = lax.all_to_all(spread(key_value), CHIP_AXES, 0, 0, tiled=True)  16.1 us
    all_to_all x1, blocking collectives, body(): lax.all_to_all(owned_sum(incoming), PLANE_AXES + ('core',), 0, 0, tiled=T...  15 us
    all_to_all x1, blocking collectives, body(): dkv = lax.all_to_all(dkv, CHIP_AXES, 0, 0, tiled=True)  12.7 us
    ppermute x2, starting transfers between devices, body(): arrived = lax.ppermute(send, 'core', SWAP)  6.38 us
    pallas_call x1, Pallas kernels, attention(): pl.pallas_call(attention_kernel, out_shape=(jax.ShapeDtypeStruct((CHIPS,...  5.86 us
    ppermute x1, starting transfers between devices, body(): other = lax.ppermute(mine, 'core', SWAP)  5.25 us
  transfers between devices with their start and end apart: 3, of which 2 were waited for; matrix products, arithmetic and copies ran while one was open for 0% of the time, Pallas kernels for 4%

profile of v11, /device:TPU:1, one launch (start us, length us, event | category | flops | bytes accessed | tf_op | source)
XLA Modules:
  0.0 117.5 jit_solution(12655390951789145078)
XLA Ops:
  0.6 1.3 %spread_kv.1 = bf16[8,128,256]{2,1,0:T(8,128)(2,1)S(1)} custom-call(bf16[1,128,256]{2,1,0:T(8,128)(2,1)} %kv_hbm.1), custom_call_target="tpu_custom_call" | custom-call | tf_op jit(solution)/shard_map/spread_kv/pallas_call | solution.py:192
  1.9 16.1 %all_to_all.25.mine_ref = bf16[8,128,256]{2,1,0:T(8,128)(2,1)S(1)} all-to-all(bf16[8,128,256]{2,1,0:T(8,128)(2,1)S(1)} %spread_kv.1), channel_id=1, replica_groups=mesh['yl'=2,'z'=16,'x'=4,'yh'=2,'core'=2] {'x','yh'}, dimensions={0} | all-to-all | bytes 1048576 | tf_op jit(solution)/shard_map/all_to_all | solution.py:454
  18.1 5.3 %collective-permute-start = (bf16[8,128,256]{2,1,0:T(8,128)(2,1)S(1)}, bf16[8,128,256]{2,1,0:T(8,128)(2,1)S(1)}, u32[]{:S(2)}, u32[]{:S(2)}) collective-permute-start(bf16[8,128,256]{2,1,0:T(8,128)(2,1)S(1)} %all_to_all.25.mine_ref), channel_id=1, source_target_pairs={{0,1},{1,0},{2,3},{3,2},{4,5},{5,4},{6,7},{7,6},{8,9},{9,8},{10,11... | collective-permute-start | bytes 1572872 | tf_op jit(solution)/shard_map/ppermute | solution.py:457
  23.3 1.1 prepare_rows.1
  24.5 0.4 collective-permute-done.other_ref
  24.8 5.9 %attention_backward.1 = (bf16[8,128,256]{2,1,0:T(8,128)(2,1)S(1)}, bf16[1024,1024]{1,0:T(8,128)(2,1)S(1)}, bf16[1024,1024]{1,0:T(8,128)(2,1)S(1)}, bf16[1024,1024]{1,0:T(8,128)(2,1)S(1)}) custom-call(bf16[1024,128]{1,0:T(8,128)(2,1)S(1)} %get-tuple-element.19.q_rows, bf16[1024,128]{1,0:T(8,128)(2,1)S(1)} %get-tuple-element.20.go_rows, ...), custom_call_target="tpu_custom_call" | custom-call | tf_op jit(solution)/shard_map/attention_backward/pallas_call | solution.py:231
  30.7 2.3 %collective-permute-start.1 = (bf16[8,128,256]{2,1,0:T(8,128)(2,1)S(1)}, bf16[8,128,256]{2,1,0:T(8,128)(2,1)S(1)}, u32[]{:S(2)}, u32[]{:S(2)}) collective-permute-start(bf16[8,128,256]{2,1,0:T(8,128)(2,1)S(1)} %get-tuple-element.25), channel_id=1, source_target_pairs={{0,1},{1,0},{2,3},{3,2},{4,5},{5,4},{6,7},{7,6},{8,9},{9,8},{10,11... | collective-permute-start | bytes 1572872 | tf_op jit(solution)/shard_map/ppermute | solution.py:462
  33.0 1.5 %own_keys.1 = (f32[8,128,256]{2,1,0:T(8,128)S(1)}, f32[128,1024]{1,0:T(8,128)S(1)}) custom-call(bf16[1024,128]{1,0:T(8,128)(2,1)S(1)} %get-tuple-element.19.q_rows, bf16[1024,128]{1,0:T(8,128)(2,1)S(1)} %get-tuple-element.20.go_rows, bf16[8,128,256]{2,1,0:T(8,128)(2,1)S(1)} %all_to_all.25.mine_ref, bf16[1024,1024]{1,0:T(8,128)(2,1)S(1)} %get-tuple-element.22.w_mine, ...), custom_call_target="tpu_custom_call" | custom-call | tf_op jit(solution)/shard_map/own_keys/pallas_call | solution.py:254
  34.5 0.0 copy-start
  34.5 0.0 collective-permute-done.1
  34.5 0.2 add_convert_fusion.1
  34.7 12.7 %all_to_all.26.parts_ref = bf16[8,128,256]{2,1,0:T(8,128)(2,1)S(1)} all-to-all(bf16[8,128,256]{2,1,0:T(8,128)(2,1)S(1)} %add_convert_fusion.1), channel_id=1, replica_groups=mesh['yl'=2,'z'=16,'x'=4,'yh'=2,'core'=2] {'x','yh'}, dimensions={0} | all-to-all | bytes 1048576 | tf_op jit(solution)/shard_map/all_to_all | solution.py:465
  47.4 0.0 copy-done
  47.4 0.5 weight_tiles_to_send.1
  48.0 4.1 %collective-permute-start.2 = (bf16[8,2,256,128]{3,2,1,0:T(8,128)(2,1)S(1)}, bf16[8,2,256,128]{3,2,1,0:T(8,128)(2,1)S(1)}, u32[]{:S(2)}, u32[]{:S(2)}) collective-permute-start(bf16[8,2,256,128]{3,2,1,0:T(8,128)(2,1)S(1)} %get-tuple-element.34), channel_id=1, source_target_pairs={{0,1},{1,0},{2,3},{3,2},{4,5},{5,4},{6,7},{7,6},{8,9},{9,8},{10,11... | collective-permute-start | bytes 3145736 | tf_op jit(solution)/shard_map/ppermute | solution.py:468
  52.1 1.6 %weight_tiles_to_keep.1 = (f32[8,2,256,128]{3,2,1,0:T(8,128)S(1)}, bf16[128,1024]{1,0:T(8,128)(2,1)}, bf16[128,256]{1,0:T(8,128)(2,1)}) custom-call(bf16[64,128]{1,0:T(8,128)(2,1)S(1)} %get-tuple-element.26.k_ref, bf16[128,8192]{1,0:T(8,128)(2,1)S(1)} %bitcast.9, f32[128,1024]{1,0:T(8,128)S(1)} %get-tuple-element.27.dq_t, ...), custom_call_target="tpu_custom_call" | custom-call | tf_op jit(solution)/shard_map/weight_tiles_to_keep/pallas_call | solution.py:337
  53.6 0.7 collective-permute-done.2
  54.3 0.3 add_convert_fusion
  54.6 19.1 %all_to_all.27.parts_ref = bf16[16,256,128]{2,1,0:T(8,128)(2,1)S(1)} all-to-all(bf16[16,256,128]{2,1,0:T(8,128)(2,1)S(1)} %bitcast.10), channel_id=1, replica_groups=mesh['yl'=2,'z'=16,'x'=4,'yh'=2,'core'=2] {'x','yl','yh'}, dimensions={0} | all-to-all | bytes 2097152 | tf_op jit(solution)/shard_map/all_to_all | solution.py:471
  73.7 0.9 owner_slots.1
  74.6 26.8 %all_to_all.28.parts_ref = bf16[16,32,128]{2,1,0:T(8,128)(2,1)S(1)} all-to-all(bf16[16,32,128]{2,1,0:T(8,128)(2,1)S(1)} %owner_slots.1), channel_id=1, replica_groups=mesh['yl'=2,'z'=16,'x'=4,'yh'=2,'core'=2] {'z'}, dimensions={0} | all-to-all | bytes 262144 | tf_op jit(solution)/shard_map/all_to_all | solution.py:473
  101.5 15.0 %all_to_all.29.pieces_ref = bf16[32,16,128]{2,1,0:T(8,128)(2,1)S(1)} all-to-all(bf16[32,16,128]{2,1,0:T(8,128)(2,1)S(1)} %owned_sum.1), channel_id=1, replica_groups=mesh['yl'=2,'z'=16,'x'=4,'yh'=2,'core'=2] {'x','yl','yh','core'}, dimensions={0} | all-to-all | bytes 262144 | tf_op jit(solution)/shard_map/all_to_all | solution.py:474
  116.5 1.0 factors.1
  (1 shorter events, 0.0 us)
Async XLA Ops:
  18.1 6.8 %collective-permute-start = (bf16[8,128,256]{2,1,0:T(8,128)(2,1)S(1)}, bf16[8,128,256]{2,1,0:T(8,128)(2,1)S(1)}, u32[]{:S(2)}, u32[]{:S(2)}) collective-permute-start(bf16[8,128,256]{2,1,0:T(8,128)(2,1)S(1)} %all_to_all.25.mine_ref), channel_id=1, source_target_pairs={{0,1},{1,0},{2,3},{3,2},{4,5},{5,4},{6,7},{7,6},{8,9},{9,8},{10,11... | collective-permute-start | bytes 1572872 | tf_op jit(solution)/shard_map/ppermute | solution.py:457
  30.7 3.8 %collective-permute-start.1 = (bf16[8,128,256]{2,1,0:T(8,128)(2,1)S(1)}, bf16[8,128,256]{2,1,0:T(8,128)(2,1)S(1)}, u32[]{:S(2)}, u32[]{:S(2)}) collective-permute-start(bf16[8,128,256]{2,1,0:T(8,128)(2,1)S(1)} %get-tuple-element.25), channel_id=1, source_target_pairs={{0,1},{1,0},{2,3},{3,2},{4,5},{5,4},{6,7},{7,6},{8,9},{9,8},{10,11... | collective-permute-start | bytes 1572872 | tf_op jit(solution)/shard_map/ppermute | solution.py:462
  34.5 12.9 %copy-start = (bf16[1,128,8192]{2,1,0:T(8,128)(2,1)S(1)}, bf16[1,128,8192]{2,1,0:T(8,128)(2,1)}, u32[]{:S(2)}) copy-start(bf16[1,128,8192]{2,1,0:T(8,128)(2,1)} %param.6) | copy-start | bytes 6291460
  48.0 6.4 %collective-permute-start.2 = (bf16[8,2,256,128]{3,2,1,0:T(8,128)(2,1)S(1)}, bf16[8,2,256,128]{3,2,1,0:T(8,128)(2,1)S(1)}, u32[]{:S(2)}, u32[]{:S(2)}) collective-permute-start(bf16[8,2,256,128]{3,2,1,0:T(8,128)(2,1)S(1)} %get-tuple-element.34), channel_id=1, source_target_pairs={{0,1},{1,0},{2,3},{3,2},{4,5},{5,4},{6,7},{7,6},{8,9},{9,8},{10,11... | collective-permute-start | bytes 3145736 | tf_op jit(solution)/shard_map/ppermute | solution.py:468
